TPU v7x, 256 devices: a whole 4x4x8 slice. The times are simulated.
256 devices in a mesh: seq: 32 (over y, x, core), chan: 8 (over z).
Axes of the slice: x: 4, y: 4, z: 8, core: 2. Of those that a mesh axis runs over, the one named last changes fastest.
Arguments:
- query_in: bfloat16 [16384, 4096], P('seq', 'chan'), may hold values from -6 to 6
- key_in: bfloat16 [16384, 4096], P('seq', 'chan'), may hold values from -6 to 6
- value_in: bfloat16 [16384, 4096], P('seq', 'chan'), may hold values from -6 to 6
- filter_taps: float32 [16384, 4096], P('seq', 'chan'), may hold values from -0.046875 to 0.046875
- skip_gain: float32 [4096], P('chan'), may hold values from 0.5 to 1.5
- out_weight: bfloat16 [4096, 4096], P('chan'), may hold values from -0.125 to 0.125
Outputs:
- mixed: bfloat16 [16384, 4096], P('seq', 'chan')
All inputs are finite; a program needn't handle non-finite values.
Results may differ from a plain program's by a relative error of at most 0.0049.
Values sent between devices are 32-bit elements; how exact they have to be, the bound alone decides.
No kernel may reach another device: no remote copies, remote signals or barrier semaphores. Data moves between devices by JAX's collectives and lax.ppermute only.
A program may use at most 128 MiB of HBM per device.

v0:
```python
import math

import jax
import jax.numpy as jnp
import numpy as np
from jax import lax
from jax.sharding import PartitionSpec as P

HIGHEST = lax.Precision.HIGHEST


def angle_table(left_idx, right_idx, modulus):
    product = left_idx[:, None] * right_idx[None, :] % modulus
    theta = product.astype(jnp.float32) * (2.0 * math.pi / modulus)
    return (jnp.cos(theta), jnp.sin(theta))


def rotate_dft(form, cos_t, sin_t, factor, real_part, imag_part):
    real_out = jnp.einsum(form, cos_t, real_part, precision=HIGHEST)
    imag_out = factor * jnp.einsum(form, sin_t, real_part, precision=HIGHEST)
    if imag_part is not None:
        real_out = real_out - factor * jnp.einsum(form, sin_t, imag_part, precision=HIGHEST)
        imag_out = imag_out + jnp.einsum(form, cos_t, imag_part, precision=HIGHEST)
    return (real_out, imag_out)


def twiddle(real_part, imag_part, cos_t, sin_t, factor):
    return (
        real_part * cos_t - factor * imag_part * sin_t,
        imag_part * cos_t + factor * real_part * sin_t,
    )


def four_step_conv(signal, filter_taps):
    n_parts = lax.axis_size("seq")
    my_index = lax.axis_index("seq")
    tok_rows, ch_width = signal.shape
    blk_len = tok_rows // n_parts
    span_r = 2 * n_parts
    total_len = span_r * tok_rows
    first_np = np.arange(n_parts, dtype=np.int32)
    second_np = (span_r - first_np) % span_r
    second_np[0] = n_parts
    r_all = jnp.asarray(np.stack([first_np, second_np], 1).reshape(-1))
    moved_sig, moved_taps = (
        lax.all_to_all(signal, "seq", split_axis=0, concat_axis=0, tiled=True),
        lax.all_to_all(filter_taps, "seq", split_axis=0, concat_axis=0, tiled=True),
    )
    moved_sig = moved_sig.reshape(n_parts, blk_len, ch_width)
    moved_taps = moved_taps.reshape(n_parts, blk_len, ch_width)
    cos_q, sin_q = angle_table(r_all, jnp.arange(n_parts, dtype=jnp.int32), span_r)
    j_global = my_index * blk_len + jnp.arange(blk_len, dtype=jnp.int32)
    tw_cos, tw_sin = angle_table(r_all, j_global, total_len)
    tw_cos = tw_cos[:, :, None]
    tw_sin = tw_sin[:, :, None]

    def coarse(real_part):
        head_re, head_im = rotate_dft("rq,qjc->rjc", cos_q, sin_q, -1.0, real_part, None)
        return twiddle(head_re, head_im, tw_cos, tw_sin, -1.0)

    m_index = jnp.arange(tok_rows, dtype=jnp.int32)
    cos_b, sin_b = angle_table(m_index, m_index, tok_rows)

    def finish(real_part, imag_part):
        return rotate_dft("mj,rjc->rmc", cos_b, sin_b, -1.0, real_part, imag_part)

    sig_cre, sig_cim = coarse(moved_sig)
    taps_cre, taps_cim = coarse(moved_taps)
    got_a, got_b, got_c, got_d = (
        lax.all_to_all(sig_cre, "seq", split_axis=0, concat_axis=1, tiled=True),
        lax.all_to_all(sig_cim, "seq", split_axis=0, concat_axis=1, tiled=True),
        lax.all_to_all(taps_cre, "seq", split_axis=0, concat_axis=1, tiled=True),
        lax.all_to_all(taps_cim, "seq", split_axis=0, concat_axis=1, tiled=True),
    )
    sig_re, sig_im = finish(got_a, got_b)
    taps_re, taps_im = finish(got_c, got_d)
    prod_re = sig_re * taps_re - sig_im * taps_im
    prod_im = sig_re * taps_im + sig_im * taps_re
    back_re, back_im = rotate_dft("jm,rmc->rjc", cos_b, sin_b, 1.0, prod_re, prod_im)
    r_mine = lax.dynamic_slice(r_all, (2 * my_index,), (2,))
    inv_cos, inv_sin = angle_table(r_mine, m_index, total_len)
    back_re, back_im = twiddle(back_re, back_im, inv_cos[:, :, None], inv_sin[:, :, None], 1.0)
    cols_re, cols_im = (
        lax.all_to_all(back_re, "seq", split_axis=1, concat_axis=0, tiled=True),
        lax.all_to_all(back_im, "seq", split_axis=1, concat_axis=0, tiled=True),
    )
    positions = jnp.einsum("rq,rjc->qjc", cos_q, cols_re, precision=HIGHEST)
    positions = positions - jnp.einsum("rq,rjc->qjc", sin_q, cols_im, precision=HIGHEST)
    positions = positions * (1.0 / total_len)
    positions = positions.reshape(n_parts * blk_len, ch_width)
    return lax.all_to_all(positions, "seq", split_axis=0, concat_axis=0, tiled=True)


def on_device(query_in, key_in, value_in, filter_taps, skip_gain, out_weight):
    signal = key_in.astype(jnp.float32) * value_in.astype(jnp.float32)
    conv = four_step_conv(signal, filter_taps)
    response = conv + skip_gain[None, :] * signal
    gated = (query_in.astype(jnp.float32) * response).astype(jnp.bfloat16)
    partial_value = jnp.dot(gated, out_weight, preferred_element_type=jnp.float32)
    return lax.psum_scatter(partial_value, "chan", scatter_dimension=1, tiled=True).astype(
        jnp.bfloat16
    )


def solution(mesh):
    in_specs = (
        P("seq", "chan"),
        P("seq", "chan"),
        P("seq", "chan"),
        P("seq", "chan"),
        P("chan"),
        P("chan", None),
    )
    out_specs = P("seq", "chan")
    return jax.shard_map(
        on_device, mesh=mesh, in_specs=in_specs, out_specs=out_specs, check_vma=False
    )
```

profile of v0, /device:TPU:1, one launch (start us, length us, event | category | flops | bytes accessed | tf_op | source)
XLA Modules:
  0.0 523.3 jit_solution(6180727357134380537)
XLA Ops:
  6.5 8.7 %all-to-all-start.3 = ((f32[32,16,512]{2,1,0:T(8,128)}), f32[32,16,512]{2,1,0:T(8,128)S(1)}, u32[]{:S(2)}, u32[]{:S(2)}) async-start(f32[32,16,512]{2,1,0:T(8,128)} %bitcast.123), calls=%async_computation.3 | async-start | bytes 2097152 | tf_op jit(solution)/shard_map/all_to_all | solution.py:47
  16.4 16.0 %all-to-all-done.3 = f32[32,16,512]{2,1,0:T(8,128)S(1)} async-done(((f32[32,16,512]{2,1,0:T(8,128)}), f32[32,16,512]{2,1,0:T(8,128)S(1)}, u32[]{:S(2)}, u32[]{:S(2)}) %all-to-all-start.3) | async-done | bytes 1048608 | tf_op jit(solution)/shard_map/all_to_all | solution.py:47
  32.4 4.0 all-to-all-start
  36.6 3.8 fusion.39
  40.3 3.8 fusion.41
  44.1 9.6 %all-to-all-done = f32[32,16,512]{2,1,0:T(8,128)S(1)} async-done(((f32[32,16,512]{2,1,0:T(8,128)}), f32[32,16,512]{2,1,0:T(8,128)S(1)}, u32[]{:S(2)}, u32[]{:S(2)}) %all-to-all-start) | async-done | bytes 1048608 | tf_op jit(solution)/shard_map/all_to_all | solution.py:46
  53.7 2.4 fusion.43
  56.1 5.7 %multiply_add_fusion.4 = (f32[64,16,512]{2,0,1:T(8,128)S(1)}, f32[64,16,512]{2,0,1:T(8,128)}, f32[64,16,512]{2,0,1:T(8,128)S(1)}, f32[64,16,512]{2,0,1:T(8,128)}) fusion(f32[64,16,512]{2,0,1:T(8,128)S(1)} %fusion.43, f32[64,16]{0,1:T(8,128)S(1)} %get-tuple-element.16, f32[64,16]{0,1:T(8,128)S(1)} %get-tuple-element.15, f32[64,16]{0,1:T(8,128)S(1)} %get-tuple-element.17, ...), kind=kOutput, calls=%fused_computation.18 | convolution fusion | flops 207646720 | bytes 15745280 | tf_op jit(solution)/shard_map/rq,qjc->rjc/dot_general | solution.py:19
  61.9 2.6 copy.66
  64.4 5.3 %all-to-all-start.4 = ((f32[64,16,512]{2,1,0:T(8,128)}), f32[64,16,512]{2,1,0:T(8,128)}, u32[]{:S(2)}, u32[]{:S(2)}) async-start(f32[64,16,512]{2,1,0:T(8,128)} %copy.66), calls=%async_computation.4 | async-start | bytes 4194304 | tf_op jit(solution)/shard_map/all_to_all | solution.py:72
  69.7 4.2 copy.69
  73.9 23.6 %all-to-all-done.4 = f32[64,16,512]{2,1,0:T(8,128)} async-done(((f32[64,16,512]{2,1,0:T(8,128)}), f32[64,16,512]{2,1,0:T(8,128)}, u32[]{:S(2)}, u32[]{:S(2)}) %all-to-all-start.4) | async-done | bytes 2097184 | tf_op jit(solution)/shard_map/all_to_all | solution.py:72
  97.5 6.7 %all-to-all-start.5 = ((f32[64,16,512]{2,1,0:T(8,128)}), f32[64,16,512]{2,1,0:T(8,128)}, u32[]{:S(2)}, u32[]{:S(2)}) async-start(f32[64,16,512]{2,1,0:T(8,128)} %copy.69), calls=%async_computation.5 | async-start | bytes 4194304 | tf_op jit(solution)/shard_map/all_to_all | solution.py:73
  104.3 4.2 copy.58
  108.4 23.8 %all-to-all-done.5 = f32[64,16,512]{2,1,0:T(8,128)} async-done(((f32[64,16,512]{2,1,0:T(8,128)}), f32[64,16,512]{2,1,0:T(8,128)}, u32[]{:S(2)}, u32[]{:S(2)}) %all-to-all-start.5) | async-done | bytes 2097184 | tf_op jit(solution)/shard_map/all_to_all | solution.py:73
  132.2 6.7 %all-to-all-start.1 = ((f32[64,16,512]{2,1,0:T(8,128)}), f32[64,16,512]{2,1,0:T(8,128)}, u32[]{:S(2)}, u32[]{:S(2)}) async-start(f32[64,16,512]{2,1,0:T(8,128)} %copy.58), calls=%async_computation.1 | async-start | bytes 4194304 | tf_op jit(solution)/shard_map/all_to_all | solution.py:70
  139.0 2.5 copy.61
  141.5 25.4 %all-to-all-done.1 = f32[64,16,512]{2,1,0:T(8,128)} async-done(((f32[64,16,512]{2,1,0:T(8,128)}), f32[64,16,512]{2,1,0:T(8,128)}, u32[]{:S(2)}, u32[]{:S(2)}) %all-to-all-start.1) | async-done | bytes 2097184 | tf_op jit(solution)/shard_map/all_to_all | solution.py:70
  167.0 6.1 %all-to-all-start.2 = ((f32[64,16,512]{2,1,0:T(8,128)}), f32[64,16,512]{2,1,0:T(8,128)S(1)}, u32[]{:S(2)}, u32[]{:S(2)}) async-start(f32[64,16,512]{2,1,0:T(8,128)} %copy.61), calls=%async_computation.2 | async-start | bytes 4194304 | tf_op jit(solution)/shard_map/all_to_all | solution.py:71
  173.3 1.8 copy.67
  175.1 3.2 copy.70
  180.2 11.5 %fusion.32 = f32[2,512,512]{2,1,0:T(8,128)} fusion(f32[2,512,512]{2,1,0:T(8,128)S(1)} %bitcast.119), kind=kOutput, calls=%fused_computation.45 | convolution fusion | flops 3224895488 | bytes 4194304 | tf_op jit(solution)/shard_map/mj,rjc->rmc/dot_general | solution.py:19
  191.8 11.6 %fusion.22 = f32[2,512,512]{2,1,0:T(8,128)} fusion(f32[2,512,512]{2,1,0:T(8,128)S(1)} %bitcast.120), kind=kOutput, calls=%fused_computation.35 | convolution fusion | flops 3224895488 | bytes 4194304 | tf_op jit(solution)/shard_map/mj,rjc->rmc/dot_general | solution.py:20
  203.4 11.7 %fusion.34 = f32[2,512,512]{2,1,0:T(8,128)} fusion(f32[2,512,512]{2,1,0:T(8,128)S(1)} %bitcast.121), kind=kOutput, calls=%fused_computation.47 | convolution fusion | flops 3224895488 | bytes 4194304 | tf_op jit(solution)/shard_map/mj,rjc->rmc/dot_general | solution.py:19
  215.1 11.5 %fusion.24 = f32[2,512,512]{2,1,0:T(8,128)} fusion(f32[2,512,512]{2,1,0:T(8,128)S(1)} %bitcast.122), kind=kOutput, calls=%fused_computation.37 | convolution fusion | flops 3224895488 | bytes 4194304 | tf_op jit(solution)/shard_map/mj,rjc->rmc/dot_general | solution.py:20
  228.9 11.4 %multiply_subtract_fusion.1 = f32[2,512,512]{2,1,0:T(8,128)S(1)} fusion(f32[2,512,512]{2,1,0:T(8,128)S(1)} %copy-done.13, f32[2,512,512]{2,1,0:T(8,128)S(1)} %bitcast.117), kind=kOutput, calls=%fused_computation.14 | convolution fusion | flops 3225944064 | bytes 6291456 | tf_op jit(solution)/shard_map/mj,rjc->rmc/dot_general | solution.py:22
  240.4 11.2 %multiply_add_fusion.1 = f32[2,512,512]{2,1,0:T(8,128)S(1)} fusion(f32[2,512,512]{2,1,0:T(8,128)S(1)} %copy-done.11, f32[2,512,512]{2,1,0:T(8,128)S(1)} %bitcast.118), kind=kOutput, calls=%fused_computation.12 | convolution fusion | flops 3225944064 | bytes 6291456 | tf_op jit(solution)/shard_map/mj,rjc->rmc/dot_general | solution.py:23
  251.6 11.6 %multiply_subtract_fusion.3 = f32[2,512,512]{2,1,0:T(8,128)S(1)} fusion(f32[2,512,512]{2,1,0:T(8,128)S(1)} %copy-done.12, f32[2,512,512]{2,1,0:T(8,128)S(1)} %bitcast.112), kind=kOutput, calls=%fused_computation.17 | convolution fusion | flops 3225944064 | bytes 6291456 | tf_op jit(solution)/shard_map/mj,rjc->rmc/dot_general | solution.py:22
  263.2 11.6 %multiply_subtract_fusion = (f32[2,512,512]{2,1,0:T(8,128)S(1)}, f32[2,512,512]{2,1,0:T(8,128)S(1)}) fusion(f32[2,512,512]{2,1,0:T(8,128)S(1)} %multiply_add_fusion.1, f32[2,512,512]{2,1,0:T(8,128)S(1)} %multiply_subtract_fusion.3, f32[2,512,512]{2,1,0:T(8,128)S(1)} %multiply_subtract_fusion.1, f32[2,512,512]{2,1,0:T(8,128)S(1)} %bitcast.113, ...), kind=kOutput, calls=%fused_computation.11 | convolution fusion | flops 3229089792 | bytes 14680064 | tf_op jit(solution)/shard_map/mj,rjc->rmc/dot_general | solution.py:23
  274.8 8.6 %fusion.2 = f32[2,512,512]{2,1,0:T(8,128)S(1)} fusion(f32[2,512,512]{2,1,0:T(8,128)S(1)} %get-tuple-element.6), kind=kOutput, calls=%fused_computation.2 | convolution fusion | flops 3224895488 | bytes 4194304 | tf_op jit(solution)/shard_map/jm,rmc->rjc/dot_general | solution.py:22
  283.4 8.4 %fusion = f32[2,512,512]{2,1,0:T(8,128)S(1)} fusion(f32[2,512,512]{2,1,0:T(8,128)S(1)} %get-tuple-element.6), kind=kOutput, calls=%fused_computation | convolution fusion | flops 3224895488 | bytes 4194304 | tf_op jit(solution)/shard_map/jm,rmc->rjc/dot_general | solution.py:23
  291.8 8.7 %fusion.8 = f32[2,512,512]{2,1,0:T(8,128)S(1)} fusion(f32[2,512,512]{2,1,0:T(8,128)S(1)} %fusion.2, f32[2,512,512]{2,1,0:T(8,128)S(1)} %get-tuple-element.5), kind=kOutput, calls=%fused_computation.20 | convolution fusion | flops 3225419776 | bytes 6291456 | tf_op jit(solution)/shard_map/jm,rmc->rjc/dot_general | solution.py:19
  300.4 8.8 %add_bitcast_fusion = (f32[2,512,512]{1,2,0:T(8,128)}, f32[2,512,512]{1,2,0:T(8,128)S(1)}) fusion(f32[2,512,512]{2,1,0:T(8,128)S(1)} %fusion.8, f32[2,512]{1,0:T(2,128)S(1)} %get-tuple-element.20, f32[2,512]{1,0:T(2,128)S(1)} %get-tuple-element.19, f32[2,512,512]{2,1,0:T(8,128)S(1)} %fusion, f32[2,512,512]{2,1,0:T(8,128)S(1)} %get-tuple-element.5), kind=kOutput, calls=%fused_computation.8 | convolution fusion | flops 3228565504 | bytes 10493952 | tf_op jit(solution)/shard_map/jm,rmc->rjc/dot_general | solution.py:20
  309.2 2.4 copy.76
  311.7 7.5 %all-to-all-start.6 = ((f32[2,512,512]{2,0,1:T(2,128)}), f32[2,512,512]{2,0,1:T(2,128)S(1)}, u32[]{:S(2)}, u32[]{:S(2)}) async-start(f32[2,512,512]{2,0,1:T(2,128)} %copy.76), calls=%async_computation.6 | async-start | bytes 4194304 | tf_op jit(solution)/shard_map/all_to_all | solution.py:84
  319.2 4.1 copy.79
  323.3 23.7 %all-to-all-done.6 = f32[2,512,512]{2,0,1:T(2,128)S(1)} async-done(((f32[2,512,512]{2,0,1:T(2,128)}), f32[2,512,512]{2,0,1:T(2,128)S(1)}, u32[]{:S(2)}, u32[]{:S(2)}) %all-to-all-start.6) | async-done | bytes 2097184 | tf_op jit(solution)/shard_map/all_to_all | solution.py:84
  347.0 6.7 %all-to-all-start.7 = ((f32[2,512,512]{2,0,1:T(2,128)}), f32[2,512,512]{2,0,1:T(2,128)}, u32[]{:S(2)}, u32[]{:S(2)}) async-start(f32[2,512,512]{2,0,1:T(2,128)} %copy.79), calls=%async_computation.7 | async-start | bytes 4194304 | tf_op jit(solution)/shard_map/all_to_all | solution.py:85
  355.9 2.7 all_to_all.119
  358.6 2.8 fusion.67
  361.3 20.4 %all-to-all-done.7 = f32[2,512,512]{2,0,1:T(2,128)} async-done(((f32[2,512,512]{2,0,1:T(2,128)}), f32[2,512,512]{2,0,1:T(2,128)}, u32[]{:S(2)}, u32[]{:S(2)}) %all-to-all-start.7) | async-done | bytes 2097184 | tf_op jit(solution)/shard_map/all_to_all | solution.py:85
  381.7 2.0 copy.80
  383.7 3.0 copy.81
  386.7 2.7 all_to_all.123
  391.3 22.6 %all_to_all.135 = f32[32,16,512]{2,1,0:T(8,128)S(1)} all-to-all(f32[32,16,512]{2,1,0:T(8,128)S(1)} %copy.82), channel_id=1, replica_groups=mesh['seq'=32,'chan'=8] {'seq'}, dimensions={0} | all-to-all | bytes 2097152 | tf_op jit(solution)/shard_map/all_to_all | solution.py:91
  414.2 5.6 %fusion.168 = f32[512,4096]{1,0:T(8,128)} fusion(bf16[512,512]{1,0:T(8,128)(2,1)S(1)} %fusion.19, bf16[512,4096]{1,0:T(8,128)(2,1)S(1)} %copy-done.1), kind=kOutput, calls=%fused_computation.174 | convolution fusion | flops 2147483648 | bytes 13107200 | tf_op jit(solution)/shard_map/dot_general | solution.py:99
  419.9 94.0 %reduce-scatter.2.cloned.1.call-done = f32[512,512]{1,0:T(8,128)} async-done(((f32[512,4096]{1,0:T(8,128)}), f32[512,512]{1,0:T(8,128)}) %reduce-scatter.2.cloned.1.call-update) | async-done | bytes 1048592 | tf_op jit(solution)/shard_map/reduce_scatter | solution.py:100
  513.9 2.1 convert_element_type.71
  (43 shorter events, 9.8 us)
Async XLA Ops:
  6.5 8.7 %copy-start.6 = (bf16[512,512]{1,0:T(8,128)(2,1)S(1)}, bf16[512,512]{1,0:T(8,128)(2,1)}, u32[]{:S(2)}) copy-start(bf16[512,512]{1,0:T(8,128)(2,1)} %param.8) | copy-start | bytes 1572868
  6.5 8.7 %copy-start.4 = (bf16[512,512]{1,0:T(8,128)(2,1)S(1)}, bf16[512,512]{1,0:T(8,128)(2,1)}, u32[]{:S(2)}) copy-start(bf16[512,512]{1,0:T(8,128)(2,1)} %param.9) | copy-start | bytes 1572868
  6.5 25.9 %all-to-all-start.3 = ((f32[32,16,512]{2,1,0:T(8,128)}), f32[32,16,512]{2,1,0:T(8,128)S(1)}, u32[]{:S(2)}, u32[]{:S(2)}) async-start(f32[32,16,512]{2,1,0:T(8,128)} %bitcast.123), calls=%async_computation.3 | async-start | bytes 2097152 | tf_op jit(solution)/shard_map/all_to_all | solution.py:47
  15.3 21.2 %copy-start.9 = (s32[64]{0:T(128)S(1)}, s32[64]{0:T(128)}, u32[]{:S(2)}) copy-start(s32[64]{0:T(128)} %constant.78.clone) | copy-start | bytes 772
  32.4 21.3 %all-to-all-start = ((f32[32,16,512]{2,1,0:T(8,128)}), f32[32,16,512]{2,1,0:T(8,128)S(1)}, u32[]{:S(2)}, u32[]{:S(2)}) async-start(f32[32,16,512]{2,1,0:T(8,128)} %bitcast.1), calls=%async_computation | async-start | bytes 2097152 | tf_op jit(solution)/shard_map/all_to_all | solution.py:46
  53.7 2.4 copy-start
  64.4 33.1 %all-to-all-start.4 = ((f32[64,16,512]{2,1,0:T(8,128)}), f32[64,16,512]{2,1,0:T(8,128)}, u32[]{:S(2)}, u32[]{:S(2)}) async-start(f32[64,16,512]{2,1,0:T(8,128)} %copy.66), calls=%async_computation.4 | async-start | bytes 4194304 | tf_op jit(solution)/shard_map/all_to_all | solution.py:72
  97.5 34.7 %all-to-all-start.5 = ((f32[64,16,512]{2,1,0:T(8,128)}), f32[64,16,512]{2,1,0:T(8,128)}, u32[]{:S(2)}, u32[]{:S(2)}) async-start(f32[64,16,512]{2,1,0:T(8,128)} %copy.69), calls=%async_computation.5 | async-start | bytes 4194304 | tf_op jit(solution)/shard_map/all_to_all | solution.py:73
  132.2 34.7 %all-to-all-start.1 = ((f32[64,16,512]{2,1,0:T(8,128)}), f32[64,16,512]{2,1,0:T(8,128)}, u32[]{:S(2)}, u32[]{:S(2)}) async-start(f32[64,16,512]{2,1,0:T(8,128)} %copy.58), calls=%async_computation.1 | async-start | bytes 4194304 | tf_op jit(solution)/shard_map/all_to_all | solution.py:70
  167.0 59.7 %all-to-all-start.2 = ((f32[64,16,512]{2,1,0:T(8,128)}), f32[64,16,512]{2,1,0:T(8,128)S(1)}, u32[]{:S(2)}, u32[]{:S(2)}) async-start(f32[64,16,512]{2,1,0:T(8,128)} %copy.61), calls=%async_computation.2 | async-start | bytes 4194304 | tf_op jit(solution)/shard_map/all_to_all | solution.py:71
  226.7 1.6 copy-start.3
  226.7 2.2 copy-start.13
  228.9 11.4 %copy-start.11 = (f32[2,512,512]{2,1,0:T(8,128)S(1)}, f32[2,512,512]{2,1,0:T(8,128)}, u32[]{:S(2)}) copy-start(f32[2,512,512]{2,1,0:T(8,128)} %fusion.22) | copy-start | bytes 6291460
  240.4 11.2 %copy-start.12 = (f32[2,512,512]{2,1,0:T(8,128)S(1)}, f32[2,512,512]{2,1,0:T(8,128)}, u32[]{:S(2)}) copy-start(f32[2,512,512]{2,1,0:T(8,128)} %fusion.34) | copy-start | bytes 6291460
  251.5 11.6 %copy-start.2 = (f32[2,512,512]{2,1,0:T(8,128)S(1)}, f32[2,512,512]{2,1,0:T(8,128)}, u32[]{:S(2)}) copy-start(f32[2,512,512]{2,1,0:T(8,128)} %fusion.24) | copy-start | bytes 6291460
  311.7 35.3 %all-to-all-start.6 = ((f32[2,512,512]{2,0,1:T(2,128)}), f32[2,512,512]{2,0,1:T(2,128)S(1)}, u32[]{:S(2)}, u32[]{:S(2)}) async-start(f32[2,512,512]{2,0,1:T(2,128)} %copy.76), calls=%async_computation.6 | async-start | bytes 4194304 | tf_op jit(solution)/shard_map/all_to_all | solution.py:84
  347.0 34.7 %all-to-all-start.7 = ((f32[2,512,512]{2,0,1:T(2,128)}), f32[2,512,512]{2,0,1:T(2,128)}, u32[]{:S(2)}, u32[]{:S(2)}) async-start(f32[2,512,512]{2,0,1:T(2,128)} %copy.79), calls=%async_computation.7 | async-start | bytes 4194304 | tf_op jit(solution)/shard_map/all_to_all | solution.py:85
  353.8 160.1 %reduce-scatter.2.cloned.1.call-start = ((), (), s32[]{:S(2)}) async-start(), calls=%async_computation.10 | async-start | bytes 9437184 | tf_op jit(solution)/shard_map/reduce_scatter | solution.py:100
  390.6 23.3 %copy-start.5 = (bf16[512,512]{1,0:T(8,128)(2,1)S(1)}, bf16[512,512]{1,0:T(8,128)(2,1)}, u32[]{:S(2)}) copy-start(bf16[512,512]{1,0:T(8,128)(2,1)} %param.9) | copy-start | bytes 1572868
  390.6 23.3 %copy-start.7 = (bf16[512,512]{1,0:T(8,128)(2,1)S(1)}, bf16[512,512]{1,0:T(8,128)(2,1)}, u32[]{:S(2)}) copy-start(bf16[512,512]{1,0:T(8,128)(2,1)} %param.8) | copy-start | bytes 1572868
  390.6 23.3 %copy-start.8 = (bf16[512,512]{1,0:T(8,128)(2,1)S(1)}, bf16[512,512]{1,0:T(8,128)(2,1)}, u32[]{:S(2)}) copy-start(bf16[512,512]{1,0:T(8,128)(2,1)} %param.7) | copy-start | bytes 1572868
  390.6 23.3 %copy-start.10 = (f32[512]{0:T(512)S(1)}, f32[512]{0:T(512)}, u32[]{:S(2)}) copy-start(f32[512]{0:T(512)} %param.11) | copy-start | bytes 6148
  391.3 23.0 %copy-start.1 = (bf16[512,4096]{1,0:T(8,128)(2,1)S(1)}, bf16[512,4096]{1,0:T(8,128)(2,1)}, u32[]{:S(2)}) copy-start(bf16[512,4096]{1,0:T(8,128)(2,1)} %param.12) | copy-start | bytes 12582916
Sparse Core Ops, SparseCore 0:
  420.0 93.8 reduce-scatter.1
where the time goes:
time: 533 us; the launch traced here: 523 us
  waiting for transfers between devices  237 us (44%)
  matrix products  152 us (29%)
  starting transfers between devices  51.7 us (10%)
  local copies, waits for them, and re-layouts  42.4 us (8%)
  blocking collectives  22.6 us (4%)
  between operations  14.2 us (3%)
    reduce_scatter x1, waiting for transfers between devices, on_device(): lax.psum_scatter(partial_value, 'chan', scatter_dimension=1, tiled=True)  94 us
    dot_general x5, matrix products, rotate_dft(): real_out = jnp.einsum(form, cos_t, real_part, precision=HIGHEST)  41.4 us
    dot_general x5, matrix products, rotate_dft(): imag_out = factor * jnp.einsum(form, sin_t, real_part, precision=HIGHEST)  38.1 us
    dot_general x3, matrix products, rotate_dft(): jnp.einsum(form, sin_t, imag_part, precision=HIGHEST)  31.6 us
    dot_general x3, matrix products, rotate_dft(): imag_out = imag_out + jnp.einsum(form, cos_t, imag_part, precision=HIGHEST)  31.1 us
    all_to_all x1, waiting for transfers between devices, four_step_conv(): lax.all_to_all(sig_cre, 'seq', split_axis=0, concat_axis=1, tiled=True)  25.4 us
    all_to_all x1, waiting for transfers between devices, four_step_conv(): lax.all_to_all(taps_cim, 'seq', split_axis=0, concat_axis=1, tiled=True)  23.8 us
    all_to_all x1, waiting for transfers between devices, four_step_conv(): lax.all_to_all(back_re, 'seq', split_axis=1, concat_axis=0, tiled=True)  23.7 us
  transfers between devices with their start and end apart: 9, of which 8 were waited for; matrix products, arithmetic and copies ran while one was open for 16% of the time, Pallas kernels for 0%

commit v1 on v0

v1 whole, which is shorter than its diff:
```python
import jax
import jax.numpy as jnp
import ml_dtypes
import numpy as np
from jax import lax
from jax.experimental import pallas as pl
from jax.experimental.pallas import tpu as pltpu
from jax.sharding import PartitionSpec as P

LANES = 128
F32 = jnp.float32
BF16 = jnp.bfloat16
VMEM_BYTES = 48 * 1024 * 1024


def halves(table):
    head = table.astype(ml_dtypes.bfloat16)
    tail = (table - head.astype(np.float64)).astype(ml_dtypes.bfloat16)
    return head, tail


def transform_tables(n_parts):
    size = LANES
    total = size * size
    place = np.arange(size)
    pieces = size // n_parts
    a_of = pieces * (place % n_parts) + place // n_parts
    k1 = np.arange(size)
    coarse = -2.0 * np.pi * ((a_of[None, :] * (4 * k1[:, None] + 1)) % (4 * size)) / (4 * size)
    first = np.concatenate([np.cos(coarse), np.sin(coarse)], 0)
    b_of = np.arange(size)
    turn = -2.0 * np.pi * ((b_of[None, :] * (4 * k1[:, None] + 1)) % (4 * total)) / (4 * total)
    fine = -2.0 * np.pi * ((b_of[:, None] * k1[None, :]) % size) / size
    cos_f, sin_f = np.cos(fine), np.sin(fine)
    second = np.block([[cos_f, sin_f], [-sin_f, cos_f]])
    second_back = np.block([[cos_f.T, -sin_f.T], [sin_f.T, cos_f.T]])
    first_back = np.concatenate([np.cos(coarse).T, np.sin(coarse).T], 1) / total
    return first, np.cos(turn), np.sin(turn), second, second_back, first_back


def split(value):
    head = value.astype(BF16)
    return head, (value - head.astype(F32)).astype(BF16)


def dot(left, right):
    return jnp.dot(left, right, preferred_element_type=F32)


def dot_table_left(table_ref, value):
    head, tail = split(value)
    return dot(table_ref[0], head) + (dot(table_ref[1], head) + dot(table_ref[0], tail))


def dot_table_right(value, table_ref):
    head, tail = split(value)
    return dot(head, table_ref[0]) + (dot(head, table_ref[1]) + dot(tail, table_ref[0]))


def pack_kernel(key_ref, value_ref, taps_ref, out_ref):
    parts, _, _, width, _ = out_ref.shape
    signal = key_ref[...].astype(F32) * value_ref[...].astype(F32)
    out_ref[:, 0, 0] = signal.T.reshape(parts, width, LANES)
    out_ref[:, 1, 0] = taps_ref[...].T.reshape(parts, width, LANES)


def pack(key_in, value_in, filter_taps, n_parts):
    tok_rows, channels = key_in.shape
    pieces = tok_rows // LANES
    width = channels // n_parts
    block = pl.BlockSpec((LANES, channels), lambda j: (j, 0))
    return pl.pallas_call(
        pack_kernel,
        grid=(pieces,),
        in_specs=[block, block, block],
        out_specs=pl.BlockSpec((n_parts, 2, 1, width, LANES), lambda j: (0, 0, j, 0, 0)),
        out_shape=jax.ShapeDtypeStruct((n_parts, 2, pieces, width, LANES), F32),
        compiler_params=pltpu.CompilerParams(vmem_limit_bytes=VMEM_BYTES),
        name="pack",
    )(key_in, value_in, filter_taps)


def conv_kernel(n_parts, width, x_ref, first_ref, cos_ref, sin_ref, second_ref, back2_ref, back1_ref, out_ref):
    pieces = LANES // n_parts
    rows = pieces * width
    cos_t, sin_t = cos_ref[...], sin_ref[...]

    def column(part, channel):
        return jnp.concatenate(
            [
                x_ref[pl.ds(part * rows + j * width + channel, n_parts, stride=2 * rows), :]
                for j in range(pieces)
            ],
            0,
        )

    def spectra(channel):
        both = jnp.concatenate([column(0, channel), column(1, channel)], 1)
        coarse = dot_table_left(first_ref, both)
        turned = []
        for lane in (0, LANES):
            real = coarse[:LANES, lane : lane + LANES]
            imag = coarse[LANES:, lane : lane + LANES]
            turned.append(
                jnp.concatenate([real * cos_t - imag * sin_t, real * sin_t + imag * cos_t], 1)
            )
        full = dot_table_right(jnp.concatenate(turned, 0), second_ref)
        s_re, s_im = full[:LANES, :LANES], full[:LANES, LANES:]
        h_re, h_im = full[LANES:, :LANES], full[LANES:, LANES:]
        return jnp.concatenate([s_re * h_re - s_im * h_im, s_re * h_im + s_im * h_re], 1)

    @pl.loop(0, width // 2)
    def _(pair):
        product = jnp.concatenate([spectra(2 * pair), spectra(2 * pair + 1)], 0)
        back = dot_table_right(product, back2_ref)
        turned = []
        for row in (0, LANES):
            real = back[row : row + LANES, :LANES]
            imag = back[row : row + LANES, LANES:]
            turned.append(
                jnp.concatenate([real * cos_t + imag * sin_t, imag * cos_t - real * sin_t], 0)
            )
        result = dot_table_left(back1_ref, jnp.concatenate(turned, 1))
        for at in range(2):
            for j in range(pieces):
                out_ref[pl.ds(j * width + 2 * pair + at, n_parts, stride=rows), :] = result[
                    j * n_parts : (j + 1) * n_parts, at * LANES : (at + 1) * LANES
                ]


def convolve(moved, n_parts, width):
    first, turn_cos, turn_sin, second, back2, back1 = transform_tables(n_parts)
    tables = [
        jnp.asarray(np.stack(halves(first))),
        jnp.asarray(turn_cos.astype(np.float32)),
        jnp.asarray(turn_sin.astype(np.float32)),
        jnp.asarray(np.stack(halves(second))),
        jnp.asarray(np.stack(halves(back2))),
        jnp.asarray(np.stack(halves(back1))),
    ]
    pieces = LANES // n_parts
    return pl.pallas_call(
        lambda *refs: conv_kernel(n_parts, width, *refs),
        out_shape=jax.ShapeDtypeStruct((n_parts * pieces * width, LANES), F32),
        compiler_params=pltpu.CompilerParams(vmem_limit_bytes=VMEM_BYTES),
        name="convolve",
    )(moved, *tables)


def project_kernel(conv_ref, query_ref, key_ref, value_ref, gain_ref, weight_ref, out_ref):
    parts, _, width, _ = conv_ref.shape
    conv = conv_ref[:, 0].reshape(parts * width, LANES).T
    signal = key_ref[...].astype(F32) * value_ref[...].astype(F32)
    response = conv + gain_ref[...] * signal
    gated = (query_ref[...].astype(F32) * response).astype(BF16)
    out_cols = out_ref.shape[2]
    for z in range(out_ref.shape[0]):
        out_ref[z] = dot(gated, weight_ref[:, z * out_cols : (z + 1) * out_cols])


def project(conv, query_in, key_in, value_in, skip_gain, out_weight, n_chan):
    n_parts, pieces, width, _ = conv.shape
    tok_rows, channels = query_in.shape
    out_cols = out_weight.shape[1] // n_chan
    block = pl.BlockSpec((LANES, channels), lambda j: (j, 0))
    return pl.pallas_call(
        project_kernel,
        grid=(pieces,),
        in_specs=[
            pl.BlockSpec((n_parts, 1, width, LANES), lambda j: (0, j, 0, 0)),
            block,
            block,
            block,
            pl.BlockSpec((1, channels), lambda j: (0, 0)),
            pl.BlockSpec(out_weight.shape, lambda j: (0, 0)),
        ],
        out_specs=pl.BlockSpec((n_chan, LANES, out_cols), lambda j: (0, j, 0)),
        out_shape=jax.ShapeDtypeStruct((n_chan, tok_rows, out_cols), F32),
        compiler_params=pltpu.CompilerParams(vmem_limit_bytes=VMEM_BYTES),
        name="project",
    )(conv, query_in, key_in, value_in, skip_gain.reshape(1, channels), out_weight)


def on_device(query_in, key_in, value_in, filter_taps, skip_gain, out_weight):
    n_parts = lax.axis_size("seq")
    n_chan = lax.axis_size("chan")
    tok_rows, channels = key_in.shape
    pieces = tok_rows // LANES
    width = channels // n_parts
    packed = pack(key_in, value_in, filter_taps, n_parts)
    moved = lax.all_to_all(packed, "seq", split_axis=0, concat_axis=0, tiled=True)
    conv = convolve(moved.reshape(n_parts * 2 * pieces * width, LANES), n_parts, width)
    conv = conv.reshape(n_parts, pieces, width, LANES)
    conv = lax.all_to_all(conv, "seq", split_axis=0, concat_axis=0, tiled=True)
    partial = project(conv, query_in, key_in, value_in, skip_gain, out_weight, n_chan)
    mixed = lax.psum_scatter(partial, "chan", scatter_dimension=0, tiled=True)
    return mixed.reshape(tok_rows, mixed.shape[2]).astype(BF16)


def solution(mesh):
    in_specs = (
        P("seq", "chan"),
        P("seq", "chan"),
        P("seq", "chan"),
        P("seq", "chan"),
        P("chan"),
        P("chan", None),
    )
    return jax.shard_map(
        on_device, mesh=mesh, in_specs=in_specs, out_specs=P("seq", "chan"), check_vma=False
    )
```

time: 533 us -> 191 us (0.36); the launches traced: 523 us -> 191 us
  matrix products: 152 us -> 0 us
  waiting for transfers between devices: 237 us -> 94.1 us
  starting transfers between devices: 51.7 us -> 0.01 us
  local copies, waits for them, and re-layouts: 42.4 us -> 3.36 us
  blocking collectives: 22.6 us -> 57.6 us
  Pallas kernels: 0 us -> 20.3 us
    dot_general x19 -> x0, matrix products: 152 us -> none  [the longest x5 41.4 us: rotate_dft(): real_out = jnp.einsum(form, cos_t, real_part, precision=HIGHEST)]
    all_to_all x8 -> x0, waiting for transfers between devices: 143 us -> none  [the longest x1 25.4 us: four_step_conv(): lax.all_to_all(sig_cre, 'seq', split_axis=0, concat_axis=1, tiled=True)]
    all_to_all x8 -> x0, starting transfers between devices: 51.7 us -> none  [the longest x1 8.72 us: four_step_conv(): lax.all_to_all(filter_taps, 'seq', split_axis=0, concat_axis=0, tiled=True)]
    all_to_all x1 -> x2, blocking collectives: 22.6 us -> 57.6 us  [the longest x1 36.9 us: on_device(): lax.all_to_all(packed, 'seq', split_axis=0, concat_axis=0, tiled=True)]
    pallas_call x0 -> x3, Pallas kernels: none -> 20.3 us  [the longest x1 12.1 us: convolve(): pl.pallas_call(lambda *refs: conv_kernel(n_parts, width, *refs), out_shap...]
    all_to_all x10 -> x0, local copies, waits for them, and re-layouts: 19.6 us -> none  [the longest x3 7.65 us: four_step_conv(): lax.all_to_all(back_im, 'seq', split_axis=1, concat_axis=0, tiled=True)]
    add x3 -> x0, local copies, waits for them, and re-layouts: 10.9 us -> none  [twiddle(): imag_part * cos_t + factor * real_part * sin_t]
    sub x3 -> x0, local copies, waits for them, and re-layouts: 9.21 us -> none  [twiddle(): real_part * cos_t - factor * imag_part * sin_t]
  transfers between devices with their start and end apart: 9 -> 1, of which waited for: 8 -> 1; matrix products, arithmetic and copies ran while one was open for 16% -> 0% of each run, Pallas kernels for 0% -> 0%
where the time goes in v1:
time: 191 us
  waiting for transfers between devices  94.1 us (49%)
  blocking collectives  57.6 us (30%)
  Pallas kernels  20.3 us (11%)
  between operations  13.5 us (7%)
  local copies, waits for them, and re-layouts  3.36 us (2%)
  other arithmetic  2.08 us (1%)
    reduce_scatter x1, waiting for transfers between devices, on_device(): mixed = lax.psum_scatter(partial, 'chan', scatter_dimension=0, tiled=True)  94.1 us
    all_to_all x1, blocking collectives, on_device(): lax.all_to_all(packed, 'seq', split_axis=0, concat_axis=0, tiled=True)  36.9 us
    all_to_all x1, blocking collectives, on_device(): conv = lax.all_to_all(conv, 'seq', split_axis=0, concat_axis=0, tiled=True)  20.7 us
    pallas_call x1, Pallas kernels, convolve(): pl.pallas_call(lambda *refs: conv_kernel(n_parts, width, *refs), out_shap...  12.1 us
    pallas_call x1, Pallas kernels, project(): pl.pallas_call(project_kernel, grid=(pieces,), in_specs=[pl.BlockSpec((n_...  7.18 us
  transfers between devices with their start and end apart: 1, of which 1 were waited for; matrix products, arithmetic and copies ran while one was open for 0% of the time, Pallas kernels for 0%

profile of v1, /device:TPU:1, one launch (start us, length us, event | category | flops | bytes accessed | tf_op | source)
XLA Modules:
  0.0 190.9 jit_solution(6242558595013550250)
XLA Ops:
  6.5 0.0 reduce-scatter.2.cloned.1.call-start
  6.5 0.0 copy-start
  6.5 1.0 copy-done
  7.6 0.0 copy-start.2
  7.6 1.0 copy-done.2
  8.6 0.0 copy-start.4
  8.6 1.2 copy-done.4
  9.8 0.0 copy-start.6
  9.8 0.0 copy-start.7
  9.9 0.0 copy-start.8
  9.9 0.0 copy-start.9
  9.9 0.0 copy-start.10
  9.9 0.0 copy-start.11
  9.9 1.0 pack.1
  10.9 0.0 copy-start.1
  10.9 0.0 copy-start.3
  10.9 0.0 copy-start.5
  11.0 0.0 copy-start.12
  11.0 36.9 %all_to_all.10 = f32[32,2,4,16,128]{4,3,2,1,0:T(8,128)S(1)} all-to-all(f32[32,2,4,16,128]{4,3,2,1,0:T(8,128)S(1)} %pack.1), channel_id=1, replica_groups=mesh['seq'=32,'chan'=8] {'seq'}, dimensions={0} | all-to-all | bytes 4194304 | tf_op jit(solution)/shard_map/all_to_all | solution.py:191
  47.9 0.0 copy-done.6
  47.9 0.0 copy-done.7
  47.9 0.0 copy-done.8
  47.9 0.0 copy-done.9
  47.9 0.0 copy-done.10
  47.9 0.0 copy-done.11
  47.9 12.1 %convolve.1 = f32[2048,128]{1,0:T(8,128)S(1)} custom-call(f32[4096,128]{1,0:T(8,128)S(1)} %bitcast.5, bf16[2,256,128]{2,1,0:T(8,128)(2,1)S(1)} %copy-done.9, f32[128,128]{1,0:T(8,128)S(1)} %copy-done.11, f32[128,128]{1,0:T(8,128)S(1)} %copy-done.10, bf16[2,256,256]{2,1,0:T(8,128)(2,1)S(1)} %copy-done.7, bf16[2,256,256]{2,1,0:T(8,128)(2,1)S(1)} %copy-done.6, ...), custom_call_target="tpu_custom_call" | custom-call | tf_op jit(solution)/shard_map/convolve/pallas_call | solution.py:142
  60.0 20.7 %all_to_all.11.conv_ref = f32[32,4,16,128]{3,2,1,0:T(8,128)S(1)} all-to-all(f32[32,4,16,128]{3,2,1,0:T(8,128)S(1)} %bitcast.6), channel_id=1, replica_groups=mesh['seq'=32,'chan'=8] {'seq'}, dimensions={0} | all-to-all | bytes 2097152 | tf_op jit(solution)/shard_map/all_to_all | solution.py:194
  80.7 0.0 copy-done.1
  80.7 0.0 copy-done.3
  80.7 0.0 copy-done.5
  80.7 0.0 copy-done.12
  80.7 7.2 %project.1 = f32[8,512,512]{2,1,0:T(8,128)} custom-call(f32[32,4,16,128]{3,2,1,0:T(8,128)S(1)} %all_to_all.11.conv_ref, bf16[512,512]{1,0:T(8,128)(2,1)S(1)} %copy-done.5, bf16[512,512]{1,0:T(8,128)(2,1)S(1)} %copy-done.1, bf16[512,512]{1,0:T(8,128)(2,1)S(1)} %copy-done.3, f32[1,512]{1,0:T(1,128)S(1)} %bitcast.7, bf16[512,4096]{1,0:T(8,128)(2,1)} %weight_ref.1), custom_call_target="tpu_custom_call" | custom-call | tf_op jit(solution)/shard_map/project/pallas_call | solution.py:166
  87.9 0.0 reduce-scatter.2.cloned.1.call-update
  87.9 94.1 %reduce-scatter.2.cloned.1.call-done = f32[1,512,512]{2,1,0:T(8,128)} async-done(((f32[8,512,512]{2,1,0:T(8,128)}), f32[1,512,512]{2,1,0:T(8,128)}) %reduce-scatter.2.cloned.1.call-update) | async-done | bytes 1048592 | tf_op jit(solution)/shard_map/reduce_scatter | solution.py:196
  182.0 2.1 %convert_bitcast_fusion = bf16[512,512]{1,0:T(8,128)(2,1)} fusion(f32[1,512,512]{2,1,0:T(8,128)} %reduce-scatter.2.cloned.1.call-done), kind=kLoop, calls=%fused_computation | loop fusion | flops 262144 | bytes 1572864 | tf_op jit(solution)/shard_map/convert_element_type | solution.py:197
Async XLA Ops:
  6.5 175.5 %reduce-scatter.2.cloned.1.call-start = ((), (), s32[]{:S(2)}) async-start(), calls=%async_computation.3 | async-start | bytes 9437184 | tf_op jit(solution)/shard_map/reduce_scatter | solution.py:196
  6.5 1.0 copy-start
  7.6 1.0 copy-start.2
  8.6 1.2 copy-start.4
  9.8 38.1 %copy-start.6 = (bf16[2,256,256]{2,1,0:T(8,128)(2,1)S(1)}, bf16[2,256,256]{2,1,0:T(8,128)(2,1)}, u32[]{:S(2)}) copy-start(bf16[2,256,256]{2,1,0:T(8,128)(2,1)} %constant.16.clone.refs_5_) | copy-start | bytes 786436
  9.8 38.1 %copy-start.7 = (bf16[2,256,256]{2,1,0:T(8,128)(2,1)S(1)}, bf16[2,256,256]{2,1,0:T(8,128)(2,1)}, u32[]{:S(2)}) copy-start(bf16[2,256,256]{2,1,0:T(8,128)(2,1)} %constant.15.clone.refs_4_) | copy-start | bytes 786436
  9.9 38.1 %copy-start.8 = (bf16[2,128,256]{2,1,0:T(8,128)(2,1)S(1)}, bf16[2,128,256]{2,1,0:T(8,128)(2,1)}, u32[]{:S(2)}) copy-start(bf16[2,128,256]{2,1,0:T(8,128)(2,1)} %constant.17.clone.refs_6_) | copy-start | bytes 393220
  9.9 38.1 %copy-start.9 = (bf16[2,256,128]{2,1,0:T(8,128)(2,1)S(1)}, bf16[2,256,128]{2,1,0:T(8,128)(2,1)}, u32[]{:S(2)}) copy-start(bf16[2,256,128]{2,1,0:T(8,128)(2,1)} %constant.12.clone.refs_1_) | copy-start | bytes 393220
  9.9 38.1 %copy-start.10 = (f32[128,128]{1,0:T(8,128)S(1)}, f32[128,128]{1,0:T(8,128)}, u32[]{:S(2)}) copy-start(f32[128,128]{1,0:T(8,128)} %constant.14.clone.refs_3_) | copy-start | bytes 196612
  9.9 38.1 %copy-start.11 = (f32[128,128]{1,0:T(8,128)S(1)}, f32[128,128]{1,0:T(8,128)}, u32[]{:S(2)}) copy-start(f32[128,128]{1,0:T(8,128)} %constant.13.clone.refs_2_) | copy-start | bytes 196612
  10.9 69.8 %copy-start.1 = (bf16[512,512]{1,0:T(8,128)(2,1)S(1)}, bf16[512,512]{1,0:T(8,128)(2,1)}, u32[]{:S(2)}) copy-start(bf16[512,512]{1,0:T(8,128)(2,1)} %key_ref.3) | copy-start | bytes 1572868
  10.9 69.8 %copy-start.3 = (bf16[512,512]{1,0:T(8,128)(2,1)S(1)}, bf16[512,512]{1,0:T(8,128)(2,1)}, u32[]{:S(2)}) copy-start(bf16[512,512]{1,0:T(8,128)(2,1)} %value_ref.3) | copy-start | bytes 1572868
  10.9 69.8 %copy-start.5 = (bf16[512,512]{1,0:T(8,128)(2,1)S(1)}, bf16[512,512]{1,0:T(8,128)(2,1)}, u32[]{:S(2)}) copy-start(bf16[512,512]{1,0:T(8,128)(2,1)} %query_ref.1) | copy-start | bytes 1572868
  11.0 69.8 %copy-start.12 = (f32[512]{0:T(512)S(1)}, f32[512]{0:T(512)}, u32[]{:S(2)}) copy-start(f32[512]{0:T(512)} %param.16) | copy-start | bytes 6148
Sparse Core Ops, SparseCore 0:
  88.0 93.9 reduce-scatter.1

commit v2 on v1

--- a/solution.py
+++ b/solution.py
@@ -147,24 +147,20 @@
     )(moved, *tables)
 
 
-def project_kernel(conv_ref, query_ref, key_ref, value_ref, gain_ref, weight_ref, out_ref):
+def gate_kernel(conv_ref, query_ref, key_ref, value_ref, gain_ref, out_ref):
     parts, _, width, _ = conv_ref.shape
     conv = conv_ref[:, 0].reshape(parts * width, LANES).T
     signal = key_ref[...].astype(F32) * value_ref[...].astype(F32)
     response = conv + gain_ref[...] * signal
-    gated = (query_ref[...].astype(F32) * response).astype(BF16)
-    out_cols = out_ref.shape[2]
-    for z in range(out_ref.shape[0]):
-        out_ref[z] = dot(gated, weight_ref[:, z * out_cols : (z + 1) * out_cols])
-
-
-def project(conv, query_in, key_in, value_in, skip_gain, out_weight, n_chan):
+    out_ref[...] = (query_ref[...].astype(F32) * response).astype(BF16)
+
+
+def gate(conv, first, query_in, key_in, value_in, skip_gain):
     n_parts, pieces, width, _ = conv.shape
-    tok_rows, channels = query_in.shape
-    out_cols = out_weight.shape[1] // n_chan
-    block = pl.BlockSpec((LANES, channels), lambda j: (j, 0))
+    channels = query_in.shape[1]
+    block = pl.BlockSpec((LANES, channels), lambda j: (j + first, 0))
     return pl.pallas_call(
-        project_kernel,
+        gate_kernel,
         grid=(pieces,),
         in_specs=[
             pl.BlockSpec((n_parts, 1, width, LANES), lambda j: (0, j, 0, 0)),
@@ -172,13 +168,22 @@
             block,
             block,
             pl.BlockSpec((1, channels), lambda j: (0, 0)),
-            pl.BlockSpec(out_weight.shape, lambda j: (0, 0)),
         ],
-        out_specs=pl.BlockSpec((n_chan, LANES, out_cols), lambda j: (0, j, 0)),
-        out_shape=jax.ShapeDtypeStruct((n_chan, tok_rows, out_cols), F32),
+        out_specs=pl.BlockSpec((LANES, channels), lambda j: (j, 0)),
+        out_shape=jax.ShapeDtypeStruct((pieces * LANES, channels), BF16),
         compiler_params=pltpu.CompilerParams(vmem_limit_bytes=VMEM_BYTES),
-        name="project",
-    )(conv, query_in, key_in, value_in, skip_gain.reshape(1, channels), out_weight)
+        name="gate",
+    )(conv, query_in, key_in, value_in, skip_gain.reshape(1, channels))
+
+
+def ring_sum(gated, weights, way):
+    n_chan = len(weights)
+    hops = [(i, (i + way) % n_chan) for i in range(n_chan)]
+    total = dot(gated, weights[0])
+    for step in range(1, n_chan):
+        got = lax.ppermute(total, "chan", hops)
+        total = got + dot(gated, weights[step])
+    return total
 
 
 def on_device(query_in, key_in, value_in, filter_taps, skip_gain, out_weight):
@@ -191,10 +196,24 @@
     moved = lax.all_to_all(packed, "seq", split_axis=0, concat_axis=0, tiled=True)
     conv = convolve(moved.reshape(n_parts * 2 * pieces * width, LANES), n_parts, width)
     conv = conv.reshape(n_parts, pieces, width, LANES)
-    conv = lax.all_to_all(conv, "seq", split_axis=0, concat_axis=0, tiled=True)
-    partial = project(conv, query_in, key_in, value_in, skip_gain, out_weight, n_chan)
-    mixed = lax.psum_scatter(partial, "chan", scatter_dimension=0, tiled=True)
-    return mixed.reshape(tok_rows, mixed.shape[2]).astype(BF16)
+    me = lax.axis_index("chan")
+    out_cols = out_weight.shape[1] // n_chan
+
+    def columns(of):
+        start = lax.rem(of + 2 * n_chan, n_chan) * out_cols
+        return lax.dynamic_slice(out_weight, (0, start), (channels, out_cols))
+
+    down = [columns(me - 1 - step) for step in range(n_chan)]
+    up = [down[n_chan - 2 - step] for step in range(n_chan - 1)] + [down[n_chan - 1]]
+    rows = []
+    half = pieces // 2
+    for first in (0, half):
+        part = lax.all_to_all(conv[:, first : first + half], "seq", split_axis=0, concat_axis=0, tiled=True)
+        gated = gate(part, first, query_in, key_in, value_in, skip_gain)
+        middle = half * LANES // 2
+        rows.append(ring_sum(gated[:middle], down, 1))
+        rows.append(ring_sum(gated[middle:], up, -1))
+    return jnp.concatenate(rows, 0).astype(BF16)
 
 
 def solution(mesh):

time: 191 us -> 175 us (0.916)
  starting transfers between devices: 0.01 us -> 50.6 us
  waiting for transfers between devices: 94.1 us -> 49.1 us
  blocking collectives: 57.6 us -> 36.8 us
  matrix products: 0 us -> 17.8 us
  between operations: 13.5 us -> 0.78 us
  Pallas kernels: 20.3 us -> 13.7 us
    reduce_scatter x1 -> x0, waiting for transfers between devices: 94.1 us -> none  [on_device(): mixed = lax.psum_scatter(partial, 'chan', scatter_dimension=0, tiled=True)]
    ppermute x0 -> x28, starting transfers between devices: none -> 42.7 us  [ring_sum(): got = lax.ppermute(total, 'chan', hops)]
    ppermute x0 -> x28, waiting for transfers between devices: none -> 37.1 us  [ring_sum(): got = lax.ppermute(total, 'chan', hops)]
    all_to_all x1 -> x0, blocking collectives: 20.7 us -> none  [on_device(): conv = lax.all_to_all(conv, 'seq', split_axis=0, concat_axis=0, tiled=True)]
    dot_general x0 -> x32, matrix products: none -> 17.8 us  [dot(): return jnp.dot(left, right, preferred_element_type=F32)]
    all_to_all x0 -> x2, waiting for transfers between devices: none -> 12 us  [on_device(): lax.all_to_all(conv[:, first:first + half], 'seq', split_axis=0, concat_a...]
    all_to_all x0 -> x2, starting transfers between devices: none -> 7.93 us  [on_device(): lax.all_to_all(conv[:, first:first + half], 'seq', split_axis=0, concat_a...]
    pallas_call x1 -> x2, Pallas kernels: 7.18 us -> 0.71 us  [gate(): pl.pallas_call(gate_kernel, grid=(pieces,), in_specs=[pl.BlockSpec((n_par...]
  transfers between devices with their start and end apart: 1 -> 30, of which waited for: 1 -> 16; matrix products, arithmetic and copies ran while one was open for 0% -> 9% of each run, Pallas kernels for 0% -> 0%
where the time goes in v2:
time: 175 us
  starting transfers between devices  50.6 us (29%)
  waiting for transfers between devices  49.1 us (28%)
  blocking collectives  36.8 us (21%)
  matrix products  17.8 us (10%)
  Pallas kernels  13.7 us (8%)
  local copies, waits for them, and re-layouts  4.45 us (3%)
  other arithmetic  1.82 us (1%)
    ppermute x28, starting transfers between devices, ring_sum(): got = lax.ppermute(total, 'chan', hops)  42.7 us
    ppermute x28, waiting for transfers between devices, ring_sum(): got = lax.ppermute(total, 'chan', hops)  37.1 us
    all_to_all x1, blocking collectives, on_device(): lax.all_to_all(packed, 'seq', split_axis=0, concat_axis=0, tiled=True)  36.8 us
    dot_general x32, matrix products, dot(): return jnp.dot(left, right, preferred_element_type=F32)  17.8 us
    all_to_all x2, waiting for transfers between devices, on_device(): lax.all_to_all(conv[:, first:first + half], 'seq', split_axis=0, concat_a...  12 us
    pallas_call x1, Pallas kernels, convolve(): pl.pallas_call(lambda *refs: conv_kernel(n_parts, width, *refs), out_shap...  11.9 us
    all_to_all x2, starting transfers between devices, on_device(): lax.all_to_all(conv[:, first:first + half], 'seq', split_axis=0, concat_a...  7.93 us
  transfers between devices with their start and end apart: 30, of which 16 were waited for; matrix products, arithmetic and copies ran while one was open for 9% of the time, Pallas kernels for 0%

profile of v2, /device:TPU:1, one launch (start us, length us, event | category | flops | bytes accessed | tf_op | source)
XLA Modules:
  0.0 175.0 jit_solution(8114819803229496149)
XLA Ops:
  0.0 1.0 copy-done
  1.0 1.0 copy-done.2
  2.1 1.2 copy-done.5
  3.3 1.0 pack.1
  4.4 36.8 %all_to_all.15 = f32[32,2,4,16,128]{4,3,2,1,0:T(8,128)S(1)} all-to-all(f32[32,2,4,16,128]{4,3,2,1,0:T(8,128)S(1)} %pack.1), channel_id=1, replica_groups=mesh['seq'=32,'chan'=8] {'seq'}, dimensions={0} | all-to-all | bytes 4194304 | tf_op jit(solution)/shard_map/all_to_all | solution.py:196
  41.3 11.9 %convolve.1 = f32[2048,128]{1,0:T(8,128)S(1)} custom-call(f32[4096,128]{1,0:T(8,128)S(1)} %bitcast.3, bf16[2,256,128]{2,1,0:T(8,128)(2,1)S(1)} %copy-done.8, f32[128,128]{1,0:T(8,128)S(1)} %copy-done.10, f32[128,128]{1,0:T(8,128)S(1)} %copy-done.11, bf16[2,256,256]{2,1,0:T(8,128)(2,1)S(1)} %copy-done.6, bf16[2,256,256]{2,1,0:T(8,128)(2,1)S(1)} %copy-done.7, ...), custom_call_target="tpu_custom_call" | custom-call | tf_op jit(solution)/shard_map/convolve/pallas_call | solution.py:142
  53.2 1.0 fusion.124
  54.2 3.9 %all-to-all-start.1 = ((f32[32,2,16,128]{3,2,1,0:T(8,128)}), f32[32,2,16,128]{3,2,1,0:T(8,128)S(1)}, u32[]{:S(2)}, u32[]{:S(2)}) async-start(f32[32,2,16,128]{3,2,1,0:T(8,128)} %get-tuple-element.5), calls=%async_computation.1 | async-start | bytes 1048576 | tf_op jit(solution)/shard_map/all_to_all | solution.py:211
  58.2 11.6 %all-to-all-done.1.conv_ref = f32[32,2,16,128]{3,2,1,0:T(8,128)S(1)} async-done(((f32[32,2,16,128]{3,2,1,0:T(8,128)}), f32[32,2,16,128]{3,2,1,0:T(8,128)S(1)}, u32[]{:S(2)}, u32[]{:S(2)}) %all-to-all-start.1) | async-done | bytes 524320 | tf_op jit(solution)/shard_map/all_to_all | solution.py:211
  69.9 4.0 %all-to-all-start.2 = ((f32[32,2,16,128]{3,2,1,0:T(8,128)}), f32[32,2,16,128]{3,2,1,0:T(8,128)S(1)}, u32[]{:S(2)}, u32[]{:S(2)}) async-start(f32[32,2,16,128]{3,2,1,0:T(8,128)} %get-tuple-element.6), calls=%async_computation.2 | async-start | bytes 1048576 | tf_op jit(solution)/shard_map/all_to_all | solution.py:211
  74.3 1.5 fusion.14
  75.8 2.0 %fusion.12 = f32[128,512]{1,0:T(8,128)} fusion(bf16[512,4096]{1,0:T(8,128)(2,1)} %param.17, s32[]{:T(128)S(6)} %select_n.30, bf16[256,512]{1,0:T(8,128)(2,1)S(1)} %gate.2), kind=kOutput, calls=%fused_computation.17 | convolution fusion | flops 67108864 | bytes 917508 | tf_op jit(solution)/shard_map/dot_general | solution.py:47
  78.0 0.9 fusion.26
  78.9 0.9 fusion.36
  80.8 0.9 fusion.44
  82.0 1.0 fusion.58
  83.2 1.0 fusion.6
  85.9 1.5 fusion.54
  87.3 1.3 fusion.40
  89.1 1.7 collective-permute-start
  91.1 4.0 %collective-permute-start.7 = (f32[128,512]{1,0:T(8,128)S(1)}, f32[128,512]{1,0:T(8,128)S(1)}, u32[]{:S(2)}, u32[]{:S(2)}) collective-permute-start(f32[128,512]{1,0:T(8,128)S(1)} %copy-done.21), channel_id=1, source_target_pairs={{0,7},{1,0},{2,1},{3,2},{4,3},{5,4},{6,5},{7,6},{8,15},{9,8},{10,9... | collective-permute-start | bytes 786440 | tf_op jit(solution)/shard_map/ppermute | solution.py:184
  95.5 2.7 %collective-permute-start.21 = (f32[128,512]{1,0:T(8,128)S(1)}, f32[128,512]{1,0:T(8,128)S(1)}, u32[]{:S(2)}, u32[]{:S(2)}) collective-permute-start(f32[128,512]{1,0:T(8,128)S(1)} %fusion.8), channel_id=1, source_target_pairs={{0,7},{1,0},{2,1},{3,2},{4,3},{5,4},{6,5},{7,6},{8,15},{9,8},{10,9... | collective-permute-start | bytes 786440 | tf_op jit(solution)/shard_map/ppermute | solution.py:184
  98.1 2.9 %collective-permute-done = f32[128,512]{1,0:T(8,128)S(1)} collective-permute-done((f32[128,512]{1,0:T(8,128)S(1)}, f32[128,512]{1,0:T(8,128)S(1)}, u32[]{:S(2)}, u32[]{:S(2)}) %collective-permute-start) | collective-permute-done | bytes 262176 | tf_op jit(solution)/shard_map/ppermute | solution.py:184
  101.7 2.7 %collective-permute-start.8 = (f32[128,512]{1,0:T(8,128)S(1)}, f32[128,512]{1,0:T(8,128)S(1)}, u32[]{:S(2)}, u32[]{:S(2)}) collective-permute-start(f32[128,512]{1,0:T(8,128)S(1)} %convolution_add_fusion.2), channel_id=1, source_target_pairs={{0,7},{1,0},{2,1},{3,2},{4,3},{5,4},{6,5},{7,6},{8,15},{9,8},{10,9... | collective-permute-start | bytes 786440 | tf_op jit(solution)/shard_map/ppermute | solution.py:184
  104.4 2.3 %collective-permute-done.14 = f32[128,512]{1,0:T(8,128)S(1)} collective-permute-done((f32[128,512]{1,0:T(8,128)S(1)}, f32[128,512]{1,0:T(8,128)S(1)}, u32[]{:S(2)}, u32[]{:S(2)}) %collective-permute-start.14) | collective-permute-done | bytes 262176 | tf_op jit(solution)/shard_map/ppermute | solution.py:184
  107.3 2.7 %collective-permute-start.22 = (f32[128,512]{1,0:T(8,128)S(1)}, f32[128,512]{1,0:T(8,128)S(1)}, u32[]{:S(2)}, u32[]{:S(2)}) collective-permute-start(f32[128,512]{1,0:T(8,128)S(1)} %convolution_add_fusion), channel_id=1, source_target_pairs={{0,7},{1,0},{2,1},{3,2},{4,3},{5,4},{6,5},{7,6},{8,15},{9,8},{10,9... | collective-permute-start | bytes 786440 | tf_op jit(solution)/shard_map/ppermute | solution.py:184
  110.0 2.3 %collective-permute-done.1 = f32[128,512]{1,0:T(8,128)S(1)} collective-permute-done((f32[128,512]{1,0:T(8,128)S(1)}, f32[128,512]{1,0:T(8,128)S(1)}, u32[]{:S(2)}, u32[]{:S(2)}) %collective-permute-start.1) | collective-permute-done | bytes 262176 | tf_op jit(solution)/shard_map/ppermute | solution.py:184
  112.9 2.7 %collective-permute-start.9 = (f32[128,512]{1,0:T(8,128)S(1)}, f32[128,512]{1,0:T(8,128)S(1)}, u32[]{:S(2)}, u32[]{:S(2)}) collective-permute-start(f32[128,512]{1,0:T(8,128)S(1)} %add.194), channel_id=1, source_target_pairs={{0,7},{1,0},{2,1},{3,2},{4,3},{5,4},{6,5},{7,6},{8,15},{9,8},{10,9... | collective-permute-start | bytes 786440 | tf_op jit(solution)/shard_map/ppermute | solution.py:184
  115.9 2.0 %collective-permute-done.15 = f32[128,512]{1,0:T(8,128)S(1)} collective-permute-done((f32[128,512]{1,0:T(8,128)S(1)}, f32[128,512]{1,0:T(8,128)S(1)}, u32[]{:S(2)}, u32[]{:S(2)}) %collective-permute-start.15) | collective-permute-done | bytes 262176 | tf_op jit(solution)/shard_map/ppermute | solution.py:184
  118.1 2.7 %collective-permute-start.23 = (f32[128,512]{1,0:T(8,128)S(1)}, f32[128,512]{1,0:T(8,128)S(1)}, u32[]{:S(2)}, u32[]{:S(2)}) collective-permute-start(f32[128,512]{1,0:T(8,128)S(1)} %add.208), channel_id=1, source_target_pairs={{0,7},{1,0},{2,1},{3,2},{4,3},{5,4},{6,5},{7,6},{8,15},{9,8},{10,9... | collective-permute-start | bytes 786440 | tf_op jit(solution)/shard_map/ppermute | solution.py:184
  120.9 2.7 %collective-permute-done.2 = f32[128,512]{1,0:T(8,128)S(1)} collective-permute-done((f32[128,512]{1,0:T(8,128)S(1)}, f32[128,512]{1,0:T(8,128)S(1)}, u32[]{:S(2)}, u32[]{:S(2)}) %collective-permute-start.2) | collective-permute-done | bytes 262176 | tf_op jit(solution)/shard_map/ppermute | solution.py:184
  124.0 2.7 %collective-permute-start.10 = (f32[128,512]{1,0:T(8,128)S(1)}, f32[128,512]{1,0:T(8,128)S(1)}, u32[]{:S(2)}, u32[]{:S(2)}) collective-permute-start(f32[128,512]{1,0:T(8,128)S(1)} %add.195), channel_id=1, source_target_pairs={{0,7},{1,0},{2,1},{3,2},{4,3},{5,4},{6,5},{7,6},{8,15},{9,8},{10,9... | collective-permute-start | bytes 786440 | tf_op jit(solution)/shard_map/ppermute | solution.py:184
  127.0 2.2 %collective-permute-done.16 = f32[128,512]{1,0:T(8,128)S(1)} collective-permute-done((f32[128,512]{1,0:T(8,128)S(1)}, f32[128,512]{1,0:T(8,128)S(1)}, u32[]{:S(2)}, u32[]{:S(2)}) %collective-permute-start.16) | collective-permute-done | bytes 262176 | tf_op jit(solution)/shard_map/ppermute | solution.py:184
  129.4 2.7 %collective-permute-start.24 = (f32[128,512]{1,0:T(8,128)S(1)}, f32[128,512]{1,0:T(8,128)S(1)}, u32[]{:S(2)}, u32[]{:S(2)}) collective-permute-start(f32[128,512]{1,0:T(8,128)S(1)} %add.209), channel_id=1, source_target_pairs={{0,7},{1,0},{2,1},{3,2},{4,3},{5,4},{6,5},{7,6},{8,15},{9,8},{10,9... | collective-permute-start | bytes 786440 | tf_op jit(solution)/shard_map/ppermute | solution.py:184
  132.1 2.7 %collective-permute-done.3 = f32[128,512]{1,0:T(8,128)S(1)} collective-permute-done((f32[128,512]{1,0:T(8,128)S(1)}, f32[128,512]{1,0:T(8,128)S(1)}, u32[]{:S(2)}, u32[]{:S(2)}) %collective-permute-start.3) | collective-permute-done | bytes 262176 | tf_op jit(solution)/shard_map/ppermute | solution.py:184
  135.2 2.7 %collective-permute-start.11 = (f32[128,512]{1,0:T(8,128)S(1)}, f32[128,512]{1,0:T(8,128)S(1)}, u32[]{:S(2)}, u32[]{:S(2)}) collective-permute-start(f32[128,512]{1,0:T(8,128)S(1)} %add.196), channel_id=1, source_target_pairs={{0,7},{1,0},{2,1},{3,2},{4,3},{5,4},{6,5},{7,6},{8,15},{9,8},{10,9... | collective-permute-start | bytes 786440 | tf_op jit(solution)/shard_map/ppermute | solution.py:184
  138.2 2.2 %collective-permute-done.17 = f32[128,512]{1,0:T(8,128)S(1)} collective-permute-done((f32[128,512]{1,0:T(8,128)S(1)}, f32[128,512]{1,0:T(8,128)S(1)}, u32[]{:S(2)}, u32[]{:S(2)}) %collective-permute-start.17) | collective-permute-done | bytes 262176 | tf_op jit(solution)/shard_map/ppermute | solution.py:184
  140.6 2.7 %collective-permute-start.25 = (f32[128,512]{1,0:T(8,128)S(1)}, f32[128,512]{1,0:T(8,128)S(1)}, u32[]{:S(2)}, u32[]{:S(2)}) collective-permute-start(f32[128,512]{1,0:T(8,128)S(1)} %add.210), channel_id=1, source_target_pairs={{0,7},{1,0},{2,1},{3,2},{4,3},{5,4},{6,5},{7,6},{8,15},{9,8},{10,9... | collective-permute-start | bytes 786440 | tf_op jit(solution)/shard_map/ppermute | solution.py:184
  143.3 2.7 %collective-permute-done.4 = f32[128,512]{1,0:T(8,128)S(1)} collective-permute-done((f32[128,512]{1,0:T(8,128)S(1)}, f32[128,512]{1,0:T(8,128)S(1)}, u32[]{:S(2)}, u32[]{:S(2)}) %collective-permute-start.4) | collective-permute-done | bytes 262176 | tf_op jit(solution)/shard_map/ppermute | solution.py:184
  146.5 2.7 %collective-permute-start.12 = (f32[128,512]{1,0:T(8,128)S(1)}, f32[128,512]{1,0:T(8,128)S(1)}, u32[]{:S(2)}, u32[]{:S(2)}) collective-permute-start(f32[128,512]{1,0:T(8,128)S(1)} %add.197), channel_id=1, source_target_pairs={{0,7},{1,0},{2,1},{3,2},{4,3},{5,4},{6,5},{7,6},{8,15},{9,8},{10,9... | collective-permute-start | bytes 786440 | tf_op jit(solution)/shard_map/ppermute | solution.py:184
  149.4 2.2 %collective-permute-done.18 = f32[128,512]{1,0:T(8,128)S(1)} collective-permute-done((f32[128,512]{1,0:T(8,128)S(1)}, f32[128,512]{1,0:T(8,128)S(1)}, u32[]{:S(2)}, u32[]{:S(2)}) %collective-permute-start.18) | collective-permute-done | bytes 262176 | tf_op jit(solution)/shard_map/ppermute | solution.py:184
  152.1 2.7 %collective-permute-start.26 = (f32[128,512]{1,0:T(8,128)S(1)}, f32[128,512]{1,0:T(8,128)S(1)}, u32[]{:S(2)}, u32[]{:S(2)}) collective-permute-start(f32[128,512]{1,0:T(8,128)S(1)} %add.211), channel_id=1, source_target_pairs={{0,7},{1,0},{2,1},{3,2},{4,3},{5,4},{6,5},{7,6},{8,15},{9,8},{10,9... | collective-permute-start | bytes 786440 | tf_op jit(solution)/shard_map/ppermute | solution.py:184
  154.8 2.5 %collective-permute-done.5 = f32[128,512]{1,0:T(8,128)S(1)} collective-permute-done((f32[128,512]{1,0:T(8,128)S(1)}, f32[128,512]{1,0:T(8,128)S(1)}, u32[]{:S(2)}, u32[]{:S(2)}) %collective-permute-start.5) | collective-permute-done | bytes 262176 | tf_op jit(solution)/shard_map/ppermute | solution.py:184
  157.7 2.7 %collective-permute-start.13 = (f32[128,512]{1,0:T(8,128)S(1)}, f32[128,512]{1,0:T(8,128)S(1)}, u32[]{:S(2)}, u32[]{:S(2)}) collective-permute-start(f32[128,512]{1,0:T(8,128)S(1)} %add.198), channel_id=1, source_target_pairs={{0,7},{1,0},{2,1},{3,2},{4,3},{5,4},{6,5},{7,6},{8,15},{9,8},{10,9... | collective-permute-start | bytes 786440 | tf_op jit(solution)/shard_map/ppermute | solution.py:184
  160.7 2.2 %collective-permute-done.19 = f32[128,512]{1,0:T(8,128)S(1)} collective-permute-done((f32[128,512]{1,0:T(8,128)S(1)}, f32[128,512]{1,0:T(8,128)S(1)}, u32[]{:S(2)}, u32[]{:S(2)}) %collective-permute-start.19) | collective-permute-done | bytes 262176 | tf_op jit(solution)/shard_map/ppermute | solution.py:184
  163.1 2.7 %collective-permute-start.27 = (f32[128,512]{1,0:T(8,128)S(1)}, f32[128,512]{1,0:T(8,128)S(1)}, u32[]{:S(2)}, u32[]{:S(2)}) collective-permute-start(f32[128,512]{1,0:T(8,128)S(1)} %add.212), channel_id=1, source_target_pairs={{0,7},{1,0},{2,1},{3,2},{4,3},{5,4},{6,5},{7,6},{8,15},{9,8},{10,9... | collective-permute-start | bytes 786440 | tf_op jit(solution)/shard_map/ppermute | solution.py:184
  165.8 2.7 %collective-permute-done.6 = f32[128,512]{1,0:T(8,128)S(1)} collective-permute-done((f32[128,512]{1,0:T(8,128)S(1)}, f32[128,512]{1,0:T(8,128)S(1)}, u32[]{:S(2)}, u32[]{:S(2)}) %collective-permute-start.6) | collective-permute-done | bytes 262176 | tf_op jit(solution)/shard_map/ppermute | solution.py:184
  168.6 5.5 %collective-permute-done.20 = f32[128,512]{1,0:T(8,128)S(1)} collective-permute-done((f32[128,512]{1,0:T(8,128)S(1)}, f32[128,512]{1,0:T(8,128)S(1)}, u32[]{:S(2)}, u32[]{:S(2)}) %collective-permute-start.20) | collective-permute-done | bytes 262176 | tf_op jit(solution)/shard_map/ppermute | solution.py:184
  (121 shorter events, 11.4 us)
Async XLA Ops:
  3.3 37.9 %copy-start.6 = (bf16[2,256,256]{2,1,0:T(8,128)(2,1)S(1)}, bf16[2,256,256]{2,1,0:T(8,128)(2,1)}, u32[]{:S(2)}) copy-start(bf16[2,256,256]{2,1,0:T(8,128)(2,1)} %constant.82.clone.refs_4_) | copy-start | bytes 786436
  3.3 37.9 %copy-start.7 = (bf16[2,256,256]{2,1,0:T(8,128)(2,1)S(1)}, bf16[2,256,256]{2,1,0:T(8,128)(2,1)}, u32[]{:S(2)}) copy-start(bf16[2,256,256]{2,1,0:T(8,128)(2,1)} %constant.83.clone.refs_5_) | copy-start | bytes 786436
  3.3 37.9 %copy-start.8 = (bf16[2,256,128]{2,1,0:T(8,128)(2,1)S(1)}, bf16[2,256,128]{2,1,0:T(8,128)(2,1)}, u32[]{:S(2)}) copy-start(bf16[2,256,128]{2,1,0:T(8,128)(2,1)} %constant.79.clone.refs_1_) | copy-start | bytes 393220
  3.3 37.9 %copy-start.9 = (bf16[2,128,256]{2,1,0:T(8,128)(2,1)S(1)}, bf16[2,128,256]{2,1,0:T(8,128)(2,1)}, u32[]{:S(2)}) copy-start(bf16[2,128,256]{2,1,0:T(8,128)(2,1)} %constant.84.clone.refs_6_) | copy-start | bytes 393220
  3.3 37.9 %copy-start.10 = (f32[128,128]{1,0:T(8,128)S(1)}, f32[128,128]{1,0:T(8,128)}, u32[]{:S(2)}) copy-start(f32[128,128]{1,0:T(8,128)} %constant.80.clone.refs_2_) | copy-start | bytes 196612
  3.3 37.9 %copy-start.11 = (f32[128,128]{1,0:T(8,128)S(1)}, f32[128,128]{1,0:T(8,128)}, u32[]{:S(2)}) copy-start(f32[128,128]{1,0:T(8,128)} %constant.81.clone.refs_3_) | copy-start | bytes 196612
  41.2 32.7 %copy-start.1 = (bf16[512,512]{1,0:T(8,128)(2,1)S(1)}, bf16[512,512]{1,0:T(8,128)(2,1)}, u32[]{:S(2)}) copy-start(bf16[512,512]{1,0:T(8,128)(2,1)} %key_ref.5) | copy-start | bytes 1572868
  41.2 32.7 %copy-start.3 = (bf16[512,512]{1,0:T(8,128)(2,1)S(1)}, bf16[512,512]{1,0:T(8,128)(2,1)}, u32[]{:S(2)}) copy-start(bf16[512,512]{1,0:T(8,128)(2,1)} %value_ref.5) | copy-start | bytes 1572868
  41.2 32.7 %copy-start.4 = (bf16[512,512]{1,0:T(8,128)(2,1)S(1)}, bf16[512,512]{1,0:T(8,128)(2,1)}, u32[]{:S(2)}) copy-start(bf16[512,512]{1,0:T(8,128)(2,1)} %query_ref.3) | copy-start | bytes 1572868
  41.2 32.6 %copy-start.12 = (f32[512]{0:T(512)S(1)}, f32[512]{0:T(512)}, u32[]{:S(2)}) copy-start(f32[512]{0:T(512)} %param.16) | copy-start | bytes 6148
  54.2 15.6 %all-to-all-start.1 = ((f32[32,2,16,128]{3,2,1,0:T(8,128)}), f32[32,2,16,128]{3,2,1,0:T(8,128)S(1)}, u32[]{:S(2)}, u32[]{:S(2)}) async-start(f32[32,2,16,128]{3,2,1,0:T(8,128)} %get-tuple-element.5), calls=%async_computation.1 | async-start | bytes 1048576 | tf_op jit(solution)/shard_map/all_to_all | solution.py:211
  69.9 15.7 %all-to-all-start.2 = ((f32[32,2,16,128]{3,2,1,0:T(8,128)}), f32[32,2,16,128]{3,2,1,0:T(8,128)S(1)}, u32[]{:S(2)}, u32[]{:S(2)}) async-start(f32[32,2,16,128]{3,2,1,0:T(8,128)} %get-tuple-element.6), calls=%async_computation.2 | async-start | bytes 1048576 | tf_op jit(solution)/shard_map/all_to_all | solution.py:211
  73.9 3.9 %copy-start.13 = (bf16[512,4096]{1,0:T(8,128)(2,1)S(1)}, bf16[512,4096]{1,0:T(8,128)(2,1)}, u32[]{:S(2)}) copy-start(bf16[512,4096]{1,0:T(8,128)(2,1)} %param.17) | copy-start | bytes 12582916
  85.5 5.6 %copy-start.21 = (f32[128,512]{1,0:T(8,128)S(1)}, f32[128,512]{1,0:T(8,128)}, u32[]{:S(2)}) copy-start(f32[128,512]{1,0:T(8,128)} %fusion.12) | copy-start | bytes 786436
  88.6 23.7 %copy-start.18 = (f32[128,512]{1,0:T(8,128)S(1)}, f32[128,512]{1,0:T(8,128)}, u32[]{:S(2)}) copy-start(f32[128,512]{1,0:T(8,128)} %fusion.44) | copy-start | bytes 786436
  89.1 23.8 %copy-start.17 = (f32[128,512]{1,0:T(8,128)S(1)}, f32[128,512]{1,0:T(8,128)}, u32[]{:S(2)}) copy-start(f32[128,512]{1,0:T(8,128)} %fusion.26) | copy-start | bytes 786436
  89.1 11.9 %collective-permute-start = (f32[128,512]{1,0:T(8,128)S(1)}, f32[128,512]{1,0:T(8,128)S(1)}, u32[]{:S(2)}, u32[]{:S(2)}) collective-permute-start(f32[128,512]{1,0:T(8,128)S(1)} %copy-done.22), channel_id=1, source_target_pairs={{0,1},{1,2},{2,3},{3,4},{4,5},{5,6},{6,7},{7,0},{8,9},{9,10},{10,1... | collective-permute-start | bytes 786440 | tf_op jit(solution)/shard_map/ppermute | solution.py:184
  91.1 10.3 %collective-permute-start.7 = (f32[128,512]{1,0:T(8,128)S(1)}, f32[128,512]{1,0:T(8,128)S(1)}, u32[]{:S(2)}, u32[]{:S(2)}) collective-permute-start(f32[128,512]{1,0:T(8,128)S(1)} %copy-done.21), channel_id=1, source_target_pairs={{0,7},{1,0},{2,1},{3,2},{4,3},{5,4},{6,5},{7,6},{8,15},{9,8},{10,9... | collective-permute-start | bytes 786440 | tf_op jit(solution)/shard_map/ppermute | solution.py:184
  95.4 11.3 %collective-permute-start.14 = (f32[128,512]{1,0:T(8,128)S(1)}, f32[128,512]{1,0:T(8,128)S(1)}, u32[]{:S(2)}, u32[]{:S(2)}) collective-permute-start(f32[128,512]{1,0:T(8,128)S(1)} %fusion.54), channel_id=1, source_target_pairs={{0,1},{1,2},{2,3},{3,4},{4,5},{5,6},{6,7},{7,0},{8,9},{9,10},{10,1... | collective-permute-start | bytes 786440 | tf_op jit(solution)/shard_map/ppermute | solution.py:184
  95.5 11.6 %collective-permute-start.21 = (f32[128,512]{1,0:T(8,128)S(1)}, f32[128,512]{1,0:T(8,128)S(1)}, u32[]{:S(2)}, u32[]{:S(2)}) collective-permute-start(f32[128,512]{1,0:T(8,128)S(1)} %fusion.8), channel_id=1, source_target_pairs={{0,7},{1,0},{2,1},{3,2},{4,3},{5,4},{6,5},{7,6},{8,15},{9,8},{10,9... | collective-permute-start | bytes 786440 | tf_op jit(solution)/shard_map/ppermute | solution.py:184
  101.3 22.2 %copy-start.16 = (f32[128,512]{1,0:T(8,128)S(1)}, f32[128,512]{1,0:T(8,128)}, u32[]{:S(2)}) copy-start(f32[128,512]{1,0:T(8,128)} %fusion.36) | copy-start | bytes 786436
  101.4 11.0 %collective-permute-start.1 = (f32[128,512]{1,0:T(8,128)S(1)}, f32[128,512]{1,0:T(8,128)S(1)}, u32[]{:S(2)}, u32[]{:S(2)}) collective-permute-start(f32[128,512]{1,0:T(8,128)S(1)} %convolution_add_fusion.3), channel_id=1, source_target_pairs={{0,1},{1,2},{2,3},{3,4},{4,5},{5,6},{6,7},{7,0},{8,9},{9,10},{10,1... | collective-permute-start | bytes 786440 | tf_op jit(solution)/shard_map/ppermute | solution.py:184
  101.7 11.2 %collective-permute-start.8 = (f32[128,512]{1,0:T(8,128)S(1)}, f32[128,512]{1,0:T(8,128)S(1)}, u32[]{:S(2)}, u32[]{:S(2)}) collective-permute-start(f32[128,512]{1,0:T(8,128)S(1)} %convolution_add_fusion.2), channel_id=1, source_target_pairs={{0,7},{1,0},{2,1},{3,2},{4,3},{5,4},{6,5},{7,6},{8,15},{9,8},{10,9... | collective-permute-start | bytes 786440 | tf_op jit(solution)/shard_map/ppermute | solution.py:184
  107.0 17.0 %copy-start.15 = (f32[128,512]{1,0:T(8,128)S(1)}, f32[128,512]{1,0:T(8,128)}, u32[]{:S(2)}) copy-start(f32[128,512]{1,0:T(8,128)} %fusion.34) | copy-start | bytes 786436
  107.0 11.0 %collective-permute-start.15 = (f32[128,512]{1,0:T(8,128)S(1)}, f32[128,512]{1,0:T(8,128)S(1)}, u32[]{:S(2)}, u32[]{:S(2)}) collective-permute-start(f32[128,512]{1,0:T(8,128)S(1)} %convolution_add_fusion.1), channel_id=1, source_target_pairs={{0,1},{1,2},{2,3},{3,4},{4,5},{5,6},{6,7},{7,0},{8,9},{9,10},{10,1... | collective-permute-start | bytes 786440 | tf_op jit(solution)/shard_map/ppermute | solution.py:184
  107.3 10.8 %collective-permute-start.22 = (f32[128,512]{1,0:T(8,128)S(1)}, f32[128,512]{1,0:T(8,128)S(1)}, u32[]{:S(2)}, u32[]{:S(2)}) collective-permute-start(f32[128,512]{1,0:T(8,128)S(1)} %convolution_add_fusion), channel_id=1, source_target_pairs={{0,7},{1,0},{2,1},{3,2},{4,3},{5,4},{6,5},{7,6},{8,15},{9,8},{10,9... | collective-permute-start | bytes 786440 | tf_op jit(solution)/shard_map/ppermute | solution.py:184
  112.4 11.2 %collective-permute-start.2 = (f32[128,512]{1,0:T(8,128)S(1)}, f32[128,512]{1,0:T(8,128)S(1)}, u32[]{:S(2)}, u32[]{:S(2)}) collective-permute-start(f32[128,512]{1,0:T(8,128)S(1)} %add.177), channel_id=1, source_target_pairs={{0,1},{1,2},{2,3},{3,4},{4,5},{5,6},{6,7},{7,0},{8,9},{9,10},{10,1... | collective-permute-start | bytes 786440 | tf_op jit(solution)/shard_map/ppermute | solution.py:184
  112.9 11.0 %collective-permute-start.9 = (f32[128,512]{1,0:T(8,128)S(1)}, f32[128,512]{1,0:T(8,128)S(1)}, u32[]{:S(2)}, u32[]{:S(2)}) collective-permute-start(f32[128,512]{1,0:T(8,128)S(1)} %add.194), channel_id=1, source_target_pairs={{0,7},{1,0},{2,1},{3,2},{4,3},{5,4},{6,5},{7,6},{8,15},{9,8},{10,9... | collective-permute-start | bytes 786440 | tf_op jit(solution)/shard_map/ppermute | solution.py:184
  118.0 11.2 %collective-permute-start.16 = (f32[128,512]{1,0:T(8,128)S(1)}, f32[128,512]{1,0:T(8,128)S(1)}, u32[]{:S(2)}, u32[]{:S(2)}) collective-permute-start(f32[128,512]{1,0:T(8,128)S(1)} %add.201), channel_id=1, source_target_pairs={{0,1},{1,2},{2,3},{3,4},{4,5},{5,6},{6,7},{7,0},{8,9},{9,10},{10,1... | collective-permute-start | bytes 786440 | tf_op jit(solution)/shard_map/ppermute | solution.py:184
  118.1 11.2 %collective-permute-start.23 = (f32[128,512]{1,0:T(8,128)S(1)}, f32[128,512]{1,0:T(8,128)S(1)}, u32[]{:S(2)}, u32[]{:S(2)}) collective-permute-start(f32[128,512]{1,0:T(8,128)S(1)} %add.208), channel_id=1, source_target_pairs={{0,7},{1,0},{2,1},{3,2},{4,3},{5,4},{6,5},{7,6},{8,15},{9,8},{10,9... | collective-permute-start | bytes 786440 | tf_op jit(solution)/shard_map/ppermute | solution.py:184
  123.6 11.2 %collective-permute-start.3 = (f32[128,512]{1,0:T(8,128)S(1)}, f32[128,512]{1,0:T(8,128)S(1)}, u32[]{:S(2)}, u32[]{:S(2)}) collective-permute-start(f32[128,512]{1,0:T(8,128)S(1)} %add.180), channel_id=1, source_target_pairs={{0,1},{1,2},{2,3},{3,4},{4,5},{5,6},{6,7},{7,0},{8,9},{9,10},{10,1... | collective-permute-start | bytes 786440 | tf_op jit(solution)/shard_map/ppermute | solution.py:184
  124.0 11.2 %collective-permute-start.10 = (f32[128,512]{1,0:T(8,128)S(1)}, f32[128,512]{1,0:T(8,128)S(1)}, u32[]{:S(2)}, u32[]{:S(2)}) collective-permute-start(f32[128,512]{1,0:T(8,128)S(1)} %add.195), channel_id=1, source_target_pairs={{0,7},{1,0},{2,1},{3,2},{4,3},{5,4},{6,5},{7,6},{8,15},{9,8},{10,9... | collective-permute-start | bytes 786440 | tf_op jit(solution)/shard_map/ppermute | solution.py:184
  129.2 11.2 %collective-permute-start.17 = (f32[128,512]{1,0:T(8,128)S(1)}, f32[128,512]{1,0:T(8,128)S(1)}, u32[]{:S(2)}, u32[]{:S(2)}) collective-permute-start(f32[128,512]{1,0:T(8,128)S(1)} %add.202), channel_id=1, source_target_pairs={{0,1},{1,2},{2,3},{3,4},{4,5},{5,6},{6,7},{7,0},{8,9},{9,10},{10,1... | collective-permute-start | bytes 786440 | tf_op jit(solution)/shard_map/ppermute | solution.py:184
  129.4 11.2 %collective-permute-start.24 = (f32[128,512]{1,0:T(8,128)S(1)}, f32[128,512]{1,0:T(8,128)S(1)}, u32[]{:S(2)}, u32[]{:S(2)}) collective-permute-start(f32[128,512]{1,0:T(8,128)S(1)} %add.209), channel_id=1, source_target_pairs={{0,7},{1,0},{2,1},{3,2},{4,3},{5,4},{6,5},{7,6},{8,15},{9,8},{10,9... | collective-permute-start | bytes 786440 | tf_op jit(solution)/shard_map/ppermute | solution.py:184
  134.8 11.2 %collective-permute-start.4 = (f32[128,512]{1,0:T(8,128)S(1)}, f32[128,512]{1,0:T(8,128)S(1)}, u32[]{:S(2)}, u32[]{:S(2)}) collective-permute-start(f32[128,512]{1,0:T(8,128)S(1)} %add.183), channel_id=1, source_target_pairs={{0,1},{1,2},{2,3},{3,4},{4,5},{5,6},{6,7},{7,0},{8,9},{9,10},{10,1... | collective-permute-start | bytes 786440 | tf_op jit(solution)/shard_map/ppermute | solution.py:184
  135.2 11.2 %collective-permute-start.11 = (f32[128,512]{1,0:T(8,128)S(1)}, f32[128,512]{1,0:T(8,128)S(1)}, u32[]{:S(2)}, u32[]{:S(2)}) collective-permute-start(f32[128,512]{1,0:T(8,128)S(1)} %add.196), channel_id=1, source_target_pairs={{0,7},{1,0},{2,1},{3,2},{4,3},{5,4},{6,5},{7,6},{8,15},{9,8},{10,9... | collective-permute-start | bytes 786440 | tf_op jit(solution)/shard_map/ppermute | solution.py:184
  140.5 11.2 %collective-permute-start.18 = (f32[128,512]{1,0:T(8,128)S(1)}, f32[128,512]{1,0:T(8,128)S(1)}, u32[]{:S(2)}, u32[]{:S(2)}) collective-permute-start(f32[128,512]{1,0:T(8,128)S(1)} %add.203), channel_id=1, source_target_pairs={{0,1},{1,2},{2,3},{3,4},{4,5},{5,6},{6,7},{7,0},{8,9},{9,10},{10,1... | collective-permute-start | bytes 786440 | tf_op jit(solution)/shard_map/ppermute | solution.py:184
  140.6 11.4 %collective-permute-start.25 = (f32[128,512]{1,0:T(8,128)S(1)}, f32[128,512]{1,0:T(8,128)S(1)}, u32[]{:S(2)}, u32[]{:S(2)}) collective-permute-start(f32[128,512]{1,0:T(8,128)S(1)} %add.210), channel_id=1, source_target_pairs={{0,7},{1,0},{2,1},{3,2},{4,3},{5,4},{6,5},{7,6},{8,15},{9,8},{10,9... | collective-permute-start | bytes 786440 | tf_op jit(solution)/shard_map/ppermute | solution.py:184
  146.1 11.2 %collective-permute-start.5 = (f32[128,512]{1,0:T(8,128)S(1)}, f32[128,512]{1,0:T(8,128)S(1)}, u32[]{:S(2)}, u32[]{:S(2)}) collective-permute-start(f32[128,512]{1,0:T(8,128)S(1)} %add.186), channel_id=1, source_target_pairs={{0,1},{1,2},{2,3},{3,4},{4,5},{5,6},{6,7},{7,0},{8,9},{9,10},{10,1... | collective-permute-start | bytes 786440 | tf_op jit(solution)/shard_map/ppermute | solution.py:184
  146.4 22.1 %copy-start.20 = (f32[128,512]{1,0:T(8,128)S(1)}, f32[128,512]{1,0:T(8,128)}, u32[]{:S(2)}) copy-start(f32[128,512]{1,0:T(8,128)} %fusion.6) | copy-start | bytes 786436
  146.5 22.1 %copy-start.19 = (f32[128,512]{1,0:T(8,128)S(1)}, f32[128,512]{1,0:T(8,128)}, u32[]{:S(2)}) copy-start(f32[128,512]{1,0:T(8,128)} %fusion.4) | copy-start | bytes 786436
  146.5 11.2 %collective-permute-start.12 = (f32[128,512]{1,0:T(8,128)S(1)}, f32[128,512]{1,0:T(8,128)S(1)}, u32[]{:S(2)}, u32[]{:S(2)}) collective-permute-start(f32[128,512]{1,0:T(8,128)S(1)} %add.197), channel_id=1, source_target_pairs={{0,7},{1,0},{2,1},{3,2},{4,3},{5,4},{6,5},{7,6},{8,15},{9,8},{10,9... | collective-permute-start | bytes 786440 | tf_op jit(solution)/shard_map/ppermute | solution.py:184
  151.7 11.2 %collective-permute-start.19 = (f32[128,512]{1,0:T(8,128)S(1)}, f32[128,512]{1,0:T(8,128)S(1)}, u32[]{:S(2)}, u32[]{:S(2)}) collective-permute-start(f32[128,512]{1,0:T(8,128)S(1)} %add.204), channel_id=1, source_target_pairs={{0,1},{1,2},{2,3},{3,4},{4,5},{5,6},{6,7},{7,0},{8,9},{9,10},{10,1... | collective-permute-start | bytes 786440 | tf_op jit(solution)/shard_map/ppermute | solution.py:184
  152.1 11.0 %collective-permute-start.26 = (f32[128,512]{1,0:T(8,128)S(1)}, f32[128,512]{1,0:T(8,128)S(1)}, u32[]{:S(2)}, u32[]{:S(2)}) collective-permute-start(f32[128,512]{1,0:T(8,128)S(1)} %add.211), channel_id=1, source_target_pairs={{0,7},{1,0},{2,1},{3,2},{4,3},{5,4},{6,5},{7,6},{8,15},{9,8},{10,9... | collective-permute-start | bytes 786440 | tf_op jit(solution)/shard_map/ppermute | solution.py:184
  157.3 11.2 %collective-permute-start.6 = (f32[128,512]{1,0:T(8,128)S(1)}, f32[128,512]{1,0:T(8,128)S(1)}, u32[]{:S(2)}, u32[]{:S(2)}) collective-permute-start(f32[128,512]{1,0:T(8,128)S(1)} %add.189), channel_id=1, source_target_pairs={{0,1},{1,2},{2,3},{3,4},{4,5},{5,6},{6,7},{7,0},{8,9},{9,10},{10,1... | collective-permute-start | bytes 786440 | tf_op jit(solution)/shard_map/ppermute | solution.py:184
  157.7 10.8 %collective-permute-start.13 = (f32[128,512]{1,0:T(8,128)S(1)}, f32[128,512]{1,0:T(8,128)S(1)}, u32[]{:S(2)}, u32[]{:S(2)}) collective-permute-start(f32[128,512]{1,0:T(8,128)S(1)} %add.198), channel_id=1, source_target_pairs={{0,7},{1,0},{2,1},{3,2},{4,3},{5,4},{6,5},{7,6},{8,15},{9,8},{10,9... | collective-permute-start | bytes 786440 | tf_op jit(solution)/shard_map/ppermute | solution.py:184
  162.9 11.2 %collective-permute-start.20 = (f32[128,512]{1,0:T(8,128)S(1)}, f32[128,512]{1,0:T(8,128)S(1)}, u32[]{:S(2)}, u32[]{:S(2)}) collective-permute-start(f32[128,512]{1,0:T(8,128)S(1)} %add.205), channel_id=1, source_target_pairs={{0,1},{1,2},{2,3},{3,4},{4,5},{5,6},{6,7},{7,0},{8,9},{9,10},{10,1... | collective-permute-start | bytes 786440 | tf_op jit(solution)/shard_map/ppermute | solution.py:184
  163.1 11.1 %collective-permute-start.27 = (f32[128,512]{1,0:T(8,128)S(1)}, f32[128,512]{1,0:T(8,128)S(1)}, u32[]{:S(2)}, u32[]{:S(2)}) collective-permute-start(f32[128,512]{1,0:T(8,128)S(1)} %add.212), channel_id=1, source_target_pairs={{0,7},{1,0},{2,1},{3,2},{4,3},{5,4},{6,5},{7,6},{8,15},{9,8},{10,9... | collective-permute-start | bytes 786440 | tf_op jit(solution)/shard_map/ppermute | solution.py:184
  (5 other events, 10.0 us)

commit v3 on v2

--- a/solution.py
+++ b/solution.py
@@ -69,6 +69,9 @@
     pieces = tok_rows // LANES
     width = channels // n_parts
     block = pl.BlockSpec((LANES, channels), lambda j: (j, 0))
+    key_in, value_in, filter_taps = (
+        pltpu.with_memory_space_constraint(x, pltpu.HBM) for x in (key_in, value_in, filter_taps)
+    )
     return pl.pallas_call(
         pack_kernel,
         grid=(pieces,),
@@ -155,10 +158,10 @@
     out_ref[...] = (query_ref[...].astype(F32) * response).astype(BF16)
 
 
-def gate(conv, first, query_in, key_in, value_in, skip_gain):
+def gate(conv, query_in, key_in, value_in, skip_gain):
     n_parts, pieces, width, _ = conv.shape
     channels = query_in.shape[1]
-    block = pl.BlockSpec((LANES, channels), lambda j: (j + first, 0))
+    block = pl.BlockSpec((LANES, channels), lambda j: (j, 0))
     return pl.pallas_call(
         gate_kernel,
         grid=(pieces,),
@@ -205,14 +208,13 @@
 
     down = [columns(me - 1 - step) for step in range(n_chan)]
     up = [down[n_chan - 2 - step] for step in range(n_chan - 1)] + [down[n_chan - 1]]
-    rows = []
-    half = pieces // 2
-    for first in (0, half):
-        part = lax.all_to_all(conv[:, first : first + half], "seq", split_axis=0, concat_axis=0, tiled=True)
-        gated = gate(part, first, query_in, key_in, value_in, skip_gain)
-        middle = half * LANES // 2
-        rows.append(ring_sum(gated[:middle], down, 1))
-        rows.append(ring_sum(gated[middle:], up, -1))
+    conv = lax.all_to_all(conv, "seq", split_axis=0, concat_axis=0, tiled=True)
+    gated = gate(conv, query_in, key_in, value_in, skip_gain)
+    quarter = tok_rows // 4
+    rows = [
+        ring_sum(gated[i * quarter : (i + 1) * quarter], (down, up)[i % 2], (1, -1)[i % 2])
+        for i in range(4)
+    ]
     return jnp.concatenate(rows, 0).astype(BF16)
 
 

time: 175 us -> 167 us (0.954)
  matrix products: 17.8 us -> 10 us
  waiting for transfers between devices: 49.1 us -> 54.6 us
  local copies, waits for them, and re-layouts: 4.45 us -> 0.05 us
  starting transfers between devices: 50.6 us -> 46.6 us
  Pallas kernels: 13.7 us -> 16.6 us
    dot_general x32, matrix products: 17.8 us -> 10 us  [dot(): return jnp.dot(left, right, preferred_element_type=F32)]
    all_to_all x2 -> x1, waiting for transfers between devices: 12 us -> 17.2 us  [on_device(): conv = lax.all_to_all(conv, 'seq', split_axis=0, concat_axis=0, tiled=True)]
    all_to_all x2 -> x1, starting transfers between devices: 7.93 us -> 3.98 us  [on_device(): conv = lax.all_to_all(conv, 'seq', split_axis=0, concat_axis=0, tiled=True)]
    unnamed x46 -> x22, local copies, waits for them, and re-layouts: 3.4 us -> 0.05 us
    pallas_call x1, Pallas kernels: 1.02 us -> 3.02 us  [pack(): pl.pallas_call(pack_kernel, grid=(pieces,), in_specs=[block, block, block...]
  transfers between devices with their start and end apart: 30 -> 29, of which waited for: 16 -> 15; matrix products, arithmetic and copies ran while one was open for 9% -> 3% of each run, Pallas kernels for 0% -> 0%
where the time goes in v3:
time: 167 us
  waiting for transfers between devices  54.6 us (33%)
  starting transfers between devices  46.6 us (28%)
  blocking collectives  36.8 us (22%)
  Pallas kernels  16.6 us (10%)
  matrix products  10 us (6%)
  other arithmetic  1.71 us (1%)
    ppermute x28, starting transfers between devices, ring_sum(): got = lax.ppermute(total, 'chan', hops)  42.7 us
    ppermute x28, waiting for transfers between devices, ring_sum(): got = lax.ppermute(total, 'chan', hops)  37.4 us
    all_to_all x1, blocking collectives, on_device(): lax.all_to_all(packed, 'seq', split_axis=0, concat_axis=0, tiled=True)  36.8 us
    all_to_all x1, waiting for transfers between devices, on_device(): conv = lax.all_to_all(conv, 'seq', split_axis=0, concat_axis=0, tiled=True)  17.2 us
    pallas_call x1, Pallas kernels, convolve(): pl.pallas_call(lambda *refs: conv_kernel(n_parts, width, *refs), out_shap...  12.9 us
    dot_general x32, matrix products, dot(): return jnp.dot(left, right, preferred_element_type=F32)  10 us
    all_to_all x1, starting transfers between devices, on_device(): conv = lax.all_to_all(conv, 'seq', split_axis=0, concat_axis=0, tiled=True)  3.98 us
  transfers between devices with their start and end apart: 29, of which 15 were waited for; matrix products, arithmetic and copies ran while one was open for 3% of the time, Pallas kernels for 0%

profile of v3, /device:TPU:1, one launch (start us, length us, event | category | flops | bytes accessed | tf_op | source)
XLA Modules:
  0.0 167.1 jit_solution(16708237644994623151)
XLA Ops:
  0.0 3.0 %pack.1 = f32[32,2,4,16,128]{4,3,2,1,0:T(8,128)S(1)} custom-call(bf16[512,512]{1,0:T(8,128)(2,1)} %key_ref.3, bf16[512,512]{1,0:T(8,128)(2,1)} %value_ref.3, f32[512,512]{1,0:T(8,128)} %taps_ref.1), custom_call_target="tpu_custom_call" | custom-call | tf_op jit(solution)/shard_map/pack/pallas_call | solution.py:75
  3.1 36.8 %all_to_all.10 = f32[32,2,4,16,128]{4,3,2,1,0:T(8,128)S(1)} all-to-all(f32[32,2,4,16,128]{4,3,2,1,0:T(8,128)S(1)} %pack.1), channel_id=1, replica_groups=mesh['seq'=32,'chan'=8] {'seq'}, dimensions={0} | all-to-all | bytes 4194304 | tf_op jit(solution)/shard_map/all_to_all | solution.py:199
  39.9 12.9 %convolve.1 = f32[2048,128]{1,0:T(8,128)} custom-call(f32[4096,128]{1,0:T(8,128)S(1)} %bitcast.3, bf16[2,256,128]{2,1,0:T(8,128)(2,1)S(1)} %copy-done.5, f32[128,128]{1,0:T(8,128)S(1)} %copy-done.7, f32[128,128]{1,0:T(8,128)S(1)} %copy-done.8, bf16[2,256,256]{2,1,0:T(8,128)(2,1)S(1)} %copy-done.3, bf16[2,256,256]{2,1,0:T(8,128)(2,1)S(1)} %copy-done.4, ...), custom_call_target="tpu_custom_call" | custom-call | tf_op jit(solution)/shard_map/convolve/pallas_call | solution.py:145
  52.8 4.0 %all-to-all-start.1 = ((f32[32,4,16,128]{3,2,1,0:T(8,128)}), f32[32,4,16,128]{3,2,1,0:T(8,128)S(1)}, u32[]{:S(2)}, u32[]{:S(2)}) async-start(f32[32,4,16,128]{3,2,1,0:T(8,128)} %bitcast.1), calls=%async_computation.1 | async-start | bytes 2097152 | tf_op jit(solution)/shard_map/all_to_all | solution.py:211
  56.9 17.2 %all-to-all-done.1.conv_ref = f32[32,4,16,128]{3,2,1,0:T(8,128)S(1)} async-done(((f32[32,4,16,128]{3,2,1,0:T(8,128)}), f32[32,4,16,128]{3,2,1,0:T(8,128)S(1)}, u32[]{:S(2)}, u32[]{:S(2)}) %all-to-all-start.1) | async-done | bytes 1048608 | tf_op jit(solution)/shard_map/all_to_all | solution.py:211
  74.1 0.7 gate.1
  74.8 1.6 fusion.14
  76.5 1.3 fusion.12
  79.7 0.2 fusion.6
  80.0 0.2 fusion.4
  80.2 0.2 fusion.54
  80.4 0.2 fusion.40
  80.7 0.2 fusion.32
  80.9 0.2 fusion.8
  81.2 1.7 %collective-permute-start = (f32[128,512]{1,0:T(8,128)S(1)}, f32[128,512]{1,0:T(8,128)S(1)}, u32[]{:S(2)}, u32[]{:S(2)}) collective-permute-start(f32[128,512]{1,0:T(8,128)S(1)} %fusion.58), channel_id=1, source_target_pairs={{0,1},{1,2},{2,3},{3,4},{4,5},{5,6},{6,7},{7,0},{8,9},{9,10},{10,1... | collective-permute-start | bytes 786440 | tf_op jit(solution)/shard_map/ppermute | solution.py:187
  83.1 4.0 %collective-permute-start.7 = (f32[128,512]{1,0:T(8,128)S(1)}, f32[128,512]{1,0:T(8,128)S(1)}, u32[]{:S(2)}, u32[]{:S(2)}) collective-permute-start(f32[128,512]{1,0:T(8,128)S(1)} %fusion.12), channel_id=1, source_target_pairs={{0,7},{1,0},{2,1},{3,2},{4,3},{5,4},{6,5},{7,6},{8,15},{9,8},{10,9... | collective-permute-start | bytes 786440 | tf_op jit(solution)/shard_map/ppermute | solution.py:187
  87.5 2.7 %collective-permute-start.21 = (f32[128,512]{1,0:T(8,128)S(1)}, f32[128,512]{1,0:T(8,128)S(1)}, u32[]{:S(2)}, u32[]{:S(2)}) collective-permute-start(f32[128,512]{1,0:T(8,128)S(1)} %fusion.8), channel_id=1, source_target_pairs={{0,7},{1,0},{2,1},{3,2},{4,3},{5,4},{6,5},{7,6},{8,15},{9,8},{10,9... | collective-permute-start | bytes 786440 | tf_op jit(solution)/shard_map/ppermute | solution.py:187
  90.2 3.0 %collective-permute-done = f32[128,512]{1,0:T(8,128)S(1)} collective-permute-done((f32[128,512]{1,0:T(8,128)S(1)}, f32[128,512]{1,0:T(8,128)S(1)}, u32[]{:S(2)}, u32[]{:S(2)}) %collective-permute-start) | collective-permute-done | bytes 262176 | tf_op jit(solution)/shard_map/ppermute | solution.py:187
  93.5 0.2 convolution_add_fusion.2
  93.8 2.7 %collective-permute-start.8 = (f32[128,512]{1,0:T(8,128)S(1)}, f32[128,512]{1,0:T(8,128)S(1)}, u32[]{:S(2)}, u32[]{:S(2)}) collective-permute-start(f32[128,512]{1,0:T(8,128)S(1)} %convolution_add_fusion.2), channel_id=1, source_target_pairs={{0,7},{1,0},{2,1},{3,2},{4,3},{5,4},{6,5},{7,6},{8,15},{9,8},{10,9... | collective-permute-start | bytes 786440 | tf_op jit(solution)/shard_map/ppermute | solution.py:187
  96.5 2.3 %collective-permute-done.14 = f32[128,512]{1,0:T(8,128)S(1)} collective-permute-done((f32[128,512]{1,0:T(8,128)S(1)}, f32[128,512]{1,0:T(8,128)S(1)}, u32[]{:S(2)}, u32[]{:S(2)}) %collective-permute-start.14) | collective-permute-done | bytes 262176 | tf_op jit(solution)/shard_map/ppermute | solution.py:187
  99.1 0.2 convolution_add_fusion
  99.4 2.7 %collective-permute-start.22 = (f32[128,512]{1,0:T(8,128)S(1)}, f32[128,512]{1,0:T(8,128)S(1)}, u32[]{:S(2)}, u32[]{:S(2)}) collective-permute-start(f32[128,512]{1,0:T(8,128)S(1)} %convolution_add_fusion), channel_id=1, source_target_pairs={{0,7},{1,0},{2,1},{3,2},{4,3},{5,4},{6,5},{7,6},{8,15},{9,8},{10,9... | collective-permute-start | bytes 786440 | tf_op jit(solution)/shard_map/ppermute | solution.py:187
  102.1 2.3 %collective-permute-done.1 = f32[128,512]{1,0:T(8,128)S(1)} collective-permute-done((f32[128,512]{1,0:T(8,128)S(1)}, f32[128,512]{1,0:T(8,128)S(1)}, u32[]{:S(2)}, u32[]{:S(2)}) %collective-permute-start.1) | collective-permute-done | bytes 262176 | tf_op jit(solution)/shard_map/ppermute | solution.py:187
  104.5 0.3 collective-permute-start.2
  105.0 2.7 %collective-permute-start.9 = (f32[128,512]{1,0:T(8,128)S(1)}, f32[128,512]{1,0:T(8,128)S(1)}, u32[]{:S(2)}, u32[]{:S(2)}) collective-permute-start(f32[128,512]{1,0:T(8,128)S(1)} %add.194), channel_id=1, source_target_pairs={{0,7},{1,0},{2,1},{3,2},{4,3},{5,4},{6,5},{7,6},{8,15},{9,8},{10,9... | collective-permute-start | bytes 786440 | tf_op jit(solution)/shard_map/ppermute | solution.py:187
  108.0 2.0 %collective-permute-done.15 = f32[128,512]{1,0:T(8,128)S(1)} collective-permute-done((f32[128,512]{1,0:T(8,128)S(1)}, f32[128,512]{1,0:T(8,128)S(1)}, u32[]{:S(2)}, u32[]{:S(2)}) %collective-permute-start.15) | collective-permute-done | bytes 262176 | tf_op jit(solution)/shard_map/ppermute | solution.py:187
  110.2 2.7 %collective-permute-start.23 = (f32[128,512]{1,0:T(8,128)S(1)}, f32[128,512]{1,0:T(8,128)S(1)}, u32[]{:S(2)}, u32[]{:S(2)}) collective-permute-start(f32[128,512]{1,0:T(8,128)S(1)} %add.208), channel_id=1, source_target_pairs={{0,7},{1,0},{2,1},{3,2},{4,3},{5,4},{6,5},{7,6},{8,15},{9,8},{10,9... | collective-permute-start | bytes 786440 | tf_op jit(solution)/shard_map/ppermute | solution.py:187
  112.9 2.7 %collective-permute-done.2 = f32[128,512]{1,0:T(8,128)S(1)} collective-permute-done((f32[128,512]{1,0:T(8,128)S(1)}, f32[128,512]{1,0:T(8,128)S(1)}, u32[]{:S(2)}, u32[]{:S(2)}) %collective-permute-start.2) | collective-permute-done | bytes 262176 | tf_op jit(solution)/shard_map/ppermute | solution.py:187
  116.1 2.7 %collective-permute-start.10 = (f32[128,512]{1,0:T(8,128)S(1)}, f32[128,512]{1,0:T(8,128)S(1)}, u32[]{:S(2)}, u32[]{:S(2)}) collective-permute-start(f32[128,512]{1,0:T(8,128)S(1)} %add.195), channel_id=1, source_target_pairs={{0,7},{1,0},{2,1},{3,2},{4,3},{5,4},{6,5},{7,6},{8,15},{9,8},{10,9... | collective-permute-start | bytes 786440 | tf_op jit(solution)/shard_map/ppermute | solution.py:187
  119.1 2.2 %collective-permute-done.16 = f32[128,512]{1,0:T(8,128)S(1)} collective-permute-done((f32[128,512]{1,0:T(8,128)S(1)}, f32[128,512]{1,0:T(8,128)S(1)}, u32[]{:S(2)}, u32[]{:S(2)}) %collective-permute-start.16) | collective-permute-done | bytes 262176 | tf_op jit(solution)/shard_map/ppermute | solution.py:187
  121.5 2.7 %collective-permute-start.24 = (f32[128,512]{1,0:T(8,128)S(1)}, f32[128,512]{1,0:T(8,128)S(1)}, u32[]{:S(2)}, u32[]{:S(2)}) collective-permute-start(f32[128,512]{1,0:T(8,128)S(1)} %add.209), channel_id=1, source_target_pairs={{0,7},{1,0},{2,1},{3,2},{4,3},{5,4},{6,5},{7,6},{8,15},{9,8},{10,9... | collective-permute-start | bytes 786440 | tf_op jit(solution)/shard_map/ppermute | solution.py:187
  124.2 2.7 %collective-permute-done.3 = f32[128,512]{1,0:T(8,128)S(1)} collective-permute-done((f32[128,512]{1,0:T(8,128)S(1)}, f32[128,512]{1,0:T(8,128)S(1)}, u32[]{:S(2)}, u32[]{:S(2)}) %collective-permute-start.3) | collective-permute-done | bytes 262176 | tf_op jit(solution)/shard_map/ppermute | solution.py:187
  127.3 2.7 %collective-permute-start.11 = (f32[128,512]{1,0:T(8,128)S(1)}, f32[128,512]{1,0:T(8,128)S(1)}, u32[]{:S(2)}, u32[]{:S(2)}) collective-permute-start(f32[128,512]{1,0:T(8,128)S(1)} %add.196), channel_id=1, source_target_pairs={{0,7},{1,0},{2,1},{3,2},{4,3},{5,4},{6,5},{7,6},{8,15},{9,8},{10,9... | collective-permute-start | bytes 786440 | tf_op jit(solution)/shard_map/ppermute | solution.py:187
  130.3 2.2 %collective-permute-done.17 = f32[128,512]{1,0:T(8,128)S(1)} collective-permute-done((f32[128,512]{1,0:T(8,128)S(1)}, f32[128,512]{1,0:T(8,128)S(1)}, u32[]{:S(2)}, u32[]{:S(2)}) %collective-permute-start.17) | collective-permute-done | bytes 262176 | tf_op jit(solution)/shard_map/ppermute | solution.py:187
  132.7 2.7 %collective-permute-start.25 = (f32[128,512]{1,0:T(8,128)S(1)}, f32[128,512]{1,0:T(8,128)S(1)}, u32[]{:S(2)}, u32[]{:S(2)}) collective-permute-start(f32[128,512]{1,0:T(8,128)S(1)} %add.210), channel_id=1, source_target_pairs={{0,7},{1,0},{2,1},{3,2},{4,3},{5,4},{6,5},{7,6},{8,15},{9,8},{10,9... | collective-permute-start | bytes 786440 | tf_op jit(solution)/shard_map/ppermute | solution.py:187
  135.4 2.7 %collective-permute-done.4 = f32[128,512]{1,0:T(8,128)S(1)} collective-permute-done((f32[128,512]{1,0:T(8,128)S(1)}, f32[128,512]{1,0:T(8,128)S(1)}, u32[]{:S(2)}, u32[]{:S(2)}) %collective-permute-start.4) | collective-permute-done | bytes 262176 | tf_op jit(solution)/shard_map/ppermute | solution.py:187
  138.6 2.7 %collective-permute-start.12 = (f32[128,512]{1,0:T(8,128)S(1)}, f32[128,512]{1,0:T(8,128)S(1)}, u32[]{:S(2)}, u32[]{:S(2)}) collective-permute-start(f32[128,512]{1,0:T(8,128)S(1)} %add.197), channel_id=1, source_target_pairs={{0,7},{1,0},{2,1},{3,2},{4,3},{5,4},{6,5},{7,6},{8,15},{9,8},{10,9... | collective-permute-start | bytes 786440 | tf_op jit(solution)/shard_map/ppermute | solution.py:187
  141.5 2.2 %collective-permute-done.18 = f32[128,512]{1,0:T(8,128)S(1)} collective-permute-done((f32[128,512]{1,0:T(8,128)S(1)}, f32[128,512]{1,0:T(8,128)S(1)}, u32[]{:S(2)}, u32[]{:S(2)}) %collective-permute-start.18) | collective-permute-done | bytes 262176 | tf_op jit(solution)/shard_map/ppermute | solution.py:187
  143.9 2.9 %collective-permute-start.26 = (f32[128,512]{1,0:T(8,128)S(1)}, f32[128,512]{1,0:T(8,128)S(1)}, u32[]{:S(2)}, u32[]{:S(2)}) collective-permute-start(f32[128,512]{1,0:T(8,128)S(1)} %add.211), channel_id=1, source_target_pairs={{0,7},{1,0},{2,1},{3,2},{4,3},{5,4},{6,5},{7,6},{8,15},{9,8},{10,9... | collective-permute-start | bytes 786440 | tf_op jit(solution)/shard_map/ppermute | solution.py:187
  146.9 2.5 %collective-permute-done.5 = f32[128,512]{1,0:T(8,128)S(1)} collective-permute-done((f32[128,512]{1,0:T(8,128)S(1)}, f32[128,512]{1,0:T(8,128)S(1)}, u32[]{:S(2)}, u32[]{:S(2)}) %collective-permute-start.5) | collective-permute-done | bytes 262176 | tf_op jit(solution)/shard_map/ppermute | solution.py:187
  149.5 0.2 fusion.52
  149.8 2.7 %collective-permute-start.13 = (f32[128,512]{1,0:T(8,128)S(1)}, f32[128,512]{1,0:T(8,128)S(1)}, u32[]{:S(2)}, u32[]{:S(2)}) collective-permute-start(f32[128,512]{1,0:T(8,128)S(1)} %add.198), channel_id=1, source_target_pairs={{0,7},{1,0},{2,1},{3,2},{4,3},{5,4},{6,5},{7,6},{8,15},{9,8},{10,9... | collective-permute-start | bytes 786440 | tf_op jit(solution)/shard_map/ppermute | solution.py:187
  152.8 2.2 %collective-permute-done.19 = f32[128,512]{1,0:T(8,128)S(1)} collective-permute-done((f32[128,512]{1,0:T(8,128)S(1)}, f32[128,512]{1,0:T(8,128)S(1)}, u32[]{:S(2)}, u32[]{:S(2)}) %collective-permute-start.19) | collective-permute-done | bytes 262176 | tf_op jit(solution)/shard_map/ppermute | solution.py:187
  155.2 2.7 %collective-permute-start.27 = (f32[128,512]{1,0:T(8,128)S(1)}, f32[128,512]{1,0:T(8,128)S(1)}, u32[]{:S(2)}, u32[]{:S(2)}) collective-permute-start(f32[128,512]{1,0:T(8,128)S(1)} %add.212), channel_id=1, source_target_pairs={{0,7},{1,0},{2,1},{3,2},{4,3},{5,4},{6,5},{7,6},{8,15},{9,8},{10,9... | collective-permute-start | bytes 786440 | tf_op jit(solution)/shard_map/ppermute | solution.py:187
  157.9 2.7 %collective-permute-done.6 = f32[128,512]{1,0:T(8,128)S(1)} collective-permute-done((f32[128,512]{1,0:T(8,128)S(1)}, f32[128,512]{1,0:T(8,128)S(1)}, u32[]{:S(2)}, u32[]{:S(2)}) %collective-permute-start.6) | collective-permute-done | bytes 262176 | tf_op jit(solution)/shard_map/ppermute | solution.py:187
  160.7 5.5 %collective-permute-done.20 = f32[128,512]{1,0:T(8,128)S(1)} collective-permute-done((f32[128,512]{1,0:T(8,128)S(1)}, f32[128,512]{1,0:T(8,128)S(1)}, u32[]{:S(2)}, u32[]{:S(2)}) %collective-permute-start.20) | collective-permute-done | bytes 262176 | tf_op jit(solution)/shard_map/ppermute | solution.py:187
  166.3 0.8 pad_maximum_fusion
  (93 shorter events, 6.9 us)
Async XLA Ops:
  0.0 39.9 %copy-start.3 = (bf16[2,256,256]{2,1,0:T(8,128)(2,1)S(1)}, bf16[2,256,256]{2,1,0:T(8,128)(2,1)}, u32[]{:S(2)}) copy-start(bf16[2,256,256]{2,1,0:T(8,128)(2,1)} %constant.82.clone.refs_4_) | copy-start | bytes 786436
  0.0 39.9 %copy-start.4 = (bf16[2,256,256]{2,1,0:T(8,128)(2,1)S(1)}, bf16[2,256,256]{2,1,0:T(8,128)(2,1)}, u32[]{:S(2)}) copy-start(bf16[2,256,256]{2,1,0:T(8,128)(2,1)} %constant.83.clone.refs_5_) | copy-start | bytes 786436
  0.0 39.9 %copy-start.5 = (bf16[2,256,128]{2,1,0:T(8,128)(2,1)S(1)}, bf16[2,256,128]{2,1,0:T(8,128)(2,1)}, u32[]{:S(2)}) copy-start(bf16[2,256,128]{2,1,0:T(8,128)(2,1)} %constant.79.clone.refs_1_) | copy-start | bytes 393220
  0.0 39.9 %copy-start.6 = (bf16[2,128,256]{2,1,0:T(8,128)(2,1)S(1)}, bf16[2,128,256]{2,1,0:T(8,128)(2,1)}, u32[]{:S(2)}) copy-start(bf16[2,128,256]{2,1,0:T(8,128)(2,1)} %constant.84.clone.refs_6_) | copy-start | bytes 393220
  0.0 39.9 %copy-start.7 = (f32[128,128]{1,0:T(8,128)S(1)}, f32[128,128]{1,0:T(8,128)}, u32[]{:S(2)}) copy-start(f32[128,128]{1,0:T(8,128)} %constant.80.clone.refs_2_) | copy-start | bytes 196612
  0.0 39.9 %copy-start.8 = (f32[128,128]{1,0:T(8,128)S(1)}, f32[128,128]{1,0:T(8,128)}, u32[]{:S(2)}) copy-start(f32[128,128]{1,0:T(8,128)} %constant.81.clone.refs_3_) | copy-start | bytes 196612
  39.9 34.2 %copy-start = (bf16[512,512]{1,0:T(8,128)(2,1)S(1)}, bf16[512,512]{1,0:T(8,128)(2,1)}, u32[]{:S(2)}) copy-start(bf16[512,512]{1,0:T(8,128)(2,1)} %key_ref.3) | copy-start | bytes 1572868
  39.9 34.2 %copy-start.1 = (bf16[512,512]{1,0:T(8,128)(2,1)S(1)}, bf16[512,512]{1,0:T(8,128)(2,1)}, u32[]{:S(2)}) copy-start(bf16[512,512]{1,0:T(8,128)(2,1)} %value_ref.3) | copy-start | bytes 1572868
  39.9 34.2 %copy-start.2 = (bf16[512,512]{1,0:T(8,128)(2,1)S(1)}, bf16[512,512]{1,0:T(8,128)(2,1)}, u32[]{:S(2)}) copy-start(bf16[512,512]{1,0:T(8,128)(2,1)} %query_ref.1) | copy-start | bytes 1572868
  39.9 34.3 %copy-start.9 = (f32[512]{0:T(512)S(1)}, f32[512]{0:T(512)}, u32[]{:S(2)}) copy-start(f32[512]{0:T(512)} %param.16) | copy-start | bytes 6148
  52.8 21.3 %all-to-all-start.1 = ((f32[32,4,16,128]{3,2,1,0:T(8,128)}), f32[32,4,16,128]{3,2,1,0:T(8,128)S(1)}, u32[]{:S(2)}, u32[]{:S(2)}) async-start(f32[32,4,16,128]{3,2,1,0:T(8,128)} %bitcast.1), calls=%async_computation.1 | async-start | bytes 2097152 | tf_op jit(solution)/shard_map/all_to_all | solution.py:211
  74.1 3.6 %copy-start.10 = (bf16[512,4096]{1,0:T(8,128)(2,1)S(1)}, bf16[512,4096]{1,0:T(8,128)(2,1)}, u32[]{:S(2)}) copy-start(bf16[512,4096]{1,0:T(8,128)(2,1)} %param.17) | copy-start | bytes 12582916
  81.2 12.0 %collective-permute-start = (f32[128,512]{1,0:T(8,128)S(1)}, f32[128,512]{1,0:T(8,128)S(1)}, u32[]{:S(2)}, u32[]{:S(2)}) collective-permute-start(f32[128,512]{1,0:T(8,128)S(1)} %fusion.58), channel_id=1, source_target_pairs={{0,1},{1,2},{2,3},{3,4},{4,5},{5,6},{6,7},{7,0},{8,9},{9,10},{10,1... | collective-permute-start | bytes 786440 | tf_op jit(solution)/shard_map/ppermute | solution.py:187
  83.1 10.4 %collective-permute-start.7 = (f32[128,512]{1,0:T(8,128)S(1)}, f32[128,512]{1,0:T(8,128)S(1)}, u32[]{:S(2)}, u32[]{:S(2)}) collective-permute-start(f32[128,512]{1,0:T(8,128)S(1)} %fusion.12), channel_id=1, source_target_pairs={{0,7},{1,0},{2,1},{3,2},{4,3},{5,4},{6,5},{7,6},{8,15},{9,8},{10,9... | collective-permute-start | bytes 786440 | tf_op jit(solution)/shard_map/ppermute | solution.py:187
  87.4 11.4 %collective-permute-start.14 = (f32[128,512]{1,0:T(8,128)S(1)}, f32[128,512]{1,0:T(8,128)S(1)}, u32[]{:S(2)}, u32[]{:S(2)}) collective-permute-start(f32[128,512]{1,0:T(8,128)S(1)} %fusion.54), channel_id=1, source_target_pairs={{0,1},{1,2},{2,3},{3,4},{4,5},{5,6},{6,7},{7,0},{8,9},{9,10},{10,1... | collective-permute-start | bytes 786440 | tf_op jit(solution)/shard_map/ppermute | solution.py:187
  87.5 11.6 %collective-permute-start.21 = (f32[128,512]{1,0:T(8,128)S(1)}, f32[128,512]{1,0:T(8,128)S(1)}, u32[]{:S(2)}, u32[]{:S(2)}) collective-permute-start(f32[128,512]{1,0:T(8,128)S(1)} %fusion.8), channel_id=1, source_target_pairs={{0,7},{1,0},{2,1},{3,2},{4,3},{5,4},{6,5},{7,6},{8,15},{9,8},{10,9... | collective-permute-start | bytes 786440 | tf_op jit(solution)/shard_map/ppermute | solution.py:187
  93.4 11.0 %collective-permute-start.1 = (f32[128,512]{1,0:T(8,128)S(1)}, f32[128,512]{1,0:T(8,128)S(1)}, u32[]{:S(2)}, u32[]{:S(2)}) collective-permute-start(f32[128,512]{1,0:T(8,128)S(1)} %convolution_add_fusion.3), channel_id=1, source_target_pairs={{0,1},{1,2},{2,3},{3,4},{4,5},{5,6},{6,7},{7,0},{8,9},{9,10},{10,1... | collective-permute-start | bytes 786440 | tf_op jit(solution)/shard_map/ppermute | solution.py:187
  93.8 11.2 %collective-permute-start.8 = (f32[128,512]{1,0:T(8,128)S(1)}, f32[128,512]{1,0:T(8,128)S(1)}, u32[]{:S(2)}, u32[]{:S(2)}) collective-permute-start(f32[128,512]{1,0:T(8,128)S(1)} %convolution_add_fusion.2), channel_id=1, source_target_pairs={{0,7},{1,0},{2,1},{3,2},{4,3},{5,4},{6,5},{7,6},{8,15},{9,8},{10,9... | collective-permute-start | bytes 786440 | tf_op jit(solution)/shard_map/ppermute | solution.py:187
  99.0 11.0 %collective-permute-start.15 = (f32[128,512]{1,0:T(8,128)S(1)}, f32[128,512]{1,0:T(8,128)S(1)}, u32[]{:S(2)}, u32[]{:S(2)}) collective-permute-start(f32[128,512]{1,0:T(8,128)S(1)} %convolution_add_fusion.1), channel_id=1, source_target_pairs={{0,1},{1,2},{2,3},{3,4},{4,5},{5,6},{6,7},{7,0},{8,9},{9,10},{10,1... | collective-permute-start | bytes 786440 | tf_op jit(solution)/shard_map/ppermute | solution.py:187
  99.4 10.8 %collective-permute-start.22 = (f32[128,512]{1,0:T(8,128)S(1)}, f32[128,512]{1,0:T(8,128)S(1)}, u32[]{:S(2)}, u32[]{:S(2)}) collective-permute-start(f32[128,512]{1,0:T(8,128)S(1)} %convolution_add_fusion), channel_id=1, source_target_pairs={{0,7},{1,0},{2,1},{3,2},{4,3},{5,4},{6,5},{7,6},{8,15},{9,8},{10,9... | collective-permute-start | bytes 786440 | tf_op jit(solution)/shard_map/ppermute | solution.py:187
  104.5 11.2 %collective-permute-start.2 = (f32[128,512]{1,0:T(8,128)S(1)}, f32[128,512]{1,0:T(8,128)S(1)}, u32[]{:S(2)}, u32[]{:S(2)}) collective-permute-start(f32[128,512]{1,0:T(8,128)S(1)} %add.177), channel_id=1, source_target_pairs={{0,1},{1,2},{2,3},{3,4},{4,5},{5,6},{6,7},{7,0},{8,9},{9,10},{10,1... | collective-permute-start | bytes 786440 | tf_op jit(solution)/shard_map/ppermute | solution.py:187
  105.0 11.0 %collective-permute-start.9 = (f32[128,512]{1,0:T(8,128)S(1)}, f32[128,512]{1,0:T(8,128)S(1)}, u32[]{:S(2)}, u32[]{:S(2)}) collective-permute-start(f32[128,512]{1,0:T(8,128)S(1)} %add.194), channel_id=1, source_target_pairs={{0,7},{1,0},{2,1},{3,2},{4,3},{5,4},{6,5},{7,6},{8,15},{9,8},{10,9... | collective-permute-start | bytes 786440 | tf_op jit(solution)/shard_map/ppermute | solution.py:187
  110.1 11.2 %collective-permute-start.16 = (f32[128,512]{1,0:T(8,128)S(1)}, f32[128,512]{1,0:T(8,128)S(1)}, u32[]{:S(2)}, u32[]{:S(2)}) collective-permute-start(f32[128,512]{1,0:T(8,128)S(1)} %add.201), channel_id=1, source_target_pairs={{0,1},{1,2},{2,3},{3,4},{4,5},{5,6},{6,7},{7,0},{8,9},{9,10},{10,1... | collective-permute-start | bytes 786440 | tf_op jit(solution)/shard_map/ppermute | solution.py:187
  110.2 11.2 %collective-permute-start.23 = (f32[128,512]{1,0:T(8,128)S(1)}, f32[128,512]{1,0:T(8,128)S(1)}, u32[]{:S(2)}, u32[]{:S(2)}) collective-permute-start(f32[128,512]{1,0:T(8,128)S(1)} %add.208), channel_id=1, source_target_pairs={{0,7},{1,0},{2,1},{3,2},{4,3},{5,4},{6,5},{7,6},{8,15},{9,8},{10,9... | collective-permute-start | bytes 786440 | tf_op jit(solution)/shard_map/ppermute | solution.py:187
  115.7 11.2 %collective-permute-start.3 = (f32[128,512]{1,0:T(8,128)S(1)}, f32[128,512]{1,0:T(8,128)S(1)}, u32[]{:S(2)}, u32[]{:S(2)}) collective-permute-start(f32[128,512]{1,0:T(8,128)S(1)} %add.180), channel_id=1, source_target_pairs={{0,1},{1,2},{2,3},{3,4},{4,5},{5,6},{6,7},{7,0},{8,9},{9,10},{10,1... | collective-permute-start | bytes 786440 | tf_op jit(solution)/shard_map/ppermute | solution.py:187
  116.1 11.2 %collective-permute-start.10 = (f32[128,512]{1,0:T(8,128)S(1)}, f32[128,512]{1,0:T(8,128)S(1)}, u32[]{:S(2)}, u32[]{:S(2)}) collective-permute-start(f32[128,512]{1,0:T(8,128)S(1)} %add.195), channel_id=1, source_target_pairs={{0,7},{1,0},{2,1},{3,2},{4,3},{5,4},{6,5},{7,6},{8,15},{9,8},{10,9... | collective-permute-start | bytes 786440 | tf_op jit(solution)/shard_map/ppermute | solution.py:187
  121.3 11.2 %collective-permute-start.17 = (f32[128,512]{1,0:T(8,128)S(1)}, f32[128,512]{1,0:T(8,128)S(1)}, u32[]{:S(2)}, u32[]{:S(2)}) collective-permute-start(f32[128,512]{1,0:T(8,128)S(1)} %add.202), channel_id=1, source_target_pairs={{0,1},{1,2},{2,3},{3,4},{4,5},{5,6},{6,7},{7,0},{8,9},{9,10},{10,1... | collective-permute-start | bytes 786440 | tf_op jit(solution)/shard_map/ppermute | solution.py:187
  121.5 11.2 %collective-permute-start.24 = (f32[128,512]{1,0:T(8,128)S(1)}, f32[128,512]{1,0:T(8,128)S(1)}, u32[]{:S(2)}, u32[]{:S(2)}) collective-permute-start(f32[128,512]{1,0:T(8,128)S(1)} %add.209), channel_id=1, source_target_pairs={{0,7},{1,0},{2,1},{3,2},{4,3},{5,4},{6,5},{7,6},{8,15},{9,8},{10,9... | collective-permute-start | bytes 786440 | tf_op jit(solution)/shard_map/ppermute | solution.py:187
  126.9 11.2 %collective-permute-start.4 = (f32[128,512]{1,0:T(8,128)S(1)}, f32[128,512]{1,0:T(8,128)S(1)}, u32[]{:S(2)}, u32[]{:S(2)}) collective-permute-start(f32[128,512]{1,0:T(8,128)S(1)} %add.183), channel_id=1, source_target_pairs={{0,1},{1,2},{2,3},{3,4},{4,5},{5,6},{6,7},{7,0},{8,9},{9,10},{10,1... | collective-permute-start | bytes 786440 | tf_op jit(solution)/shard_map/ppermute | solution.py:187
  127.3 11.2 %collective-permute-start.11 = (f32[128,512]{1,0:T(8,128)S(1)}, f32[128,512]{1,0:T(8,128)S(1)}, u32[]{:S(2)}, u32[]{:S(2)}) collective-permute-start(f32[128,512]{1,0:T(8,128)S(1)} %add.196), channel_id=1, source_target_pairs={{0,7},{1,0},{2,1},{3,2},{4,3},{5,4},{6,5},{7,6},{8,15},{9,8},{10,9... | collective-permute-start | bytes 786440 | tf_op jit(solution)/shard_map/ppermute | solution.py:187
  132.5 11.2 %collective-permute-start.18 = (f32[128,512]{1,0:T(8,128)S(1)}, f32[128,512]{1,0:T(8,128)S(1)}, u32[]{:S(2)}, u32[]{:S(2)}) collective-permute-start(f32[128,512]{1,0:T(8,128)S(1)} %add.203), channel_id=1, source_target_pairs={{0,1},{1,2},{2,3},{3,4},{4,5},{5,6},{6,7},{7,0},{8,9},{9,10},{10,1... | collective-permute-start | bytes 786440 | tf_op jit(solution)/shard_map/ppermute | solution.py:187
  132.7 11.2 %collective-permute-start.25 = (f32[128,512]{1,0:T(8,128)S(1)}, f32[128,512]{1,0:T(8,128)S(1)}, u32[]{:S(2)}, u32[]{:S(2)}) collective-permute-start(f32[128,512]{1,0:T(8,128)S(1)} %add.210), channel_id=1, source_target_pairs={{0,7},{1,0},{2,1},{3,2},{4,3},{5,4},{6,5},{7,6},{8,15},{9,8},{10,9... | collective-permute-start | bytes 786440 | tf_op jit(solution)/shard_map/ppermute | solution.py:187
  138.2 11.2 %collective-permute-start.5 = (f32[128,512]{1,0:T(8,128)S(1)}, f32[128,512]{1,0:T(8,128)S(1)}, u32[]{:S(2)}, u32[]{:S(2)}) collective-permute-start(f32[128,512]{1,0:T(8,128)S(1)} %add.186), channel_id=1, source_target_pairs={{0,1},{1,2},{2,3},{3,4},{4,5},{5,6},{6,7},{7,0},{8,9},{9,10},{10,1... | collective-permute-start | bytes 786440 | tf_op jit(solution)/shard_map/ppermute | solution.py:187
  138.6 11.2 %collective-permute-start.12 = (f32[128,512]{1,0:T(8,128)S(1)}, f32[128,512]{1,0:T(8,128)S(1)}, u32[]{:S(2)}, u32[]{:S(2)}) collective-permute-start(f32[128,512]{1,0:T(8,128)S(1)} %add.197), channel_id=1, source_target_pairs={{0,7},{1,0},{2,1},{3,2},{4,3},{5,4},{6,5},{7,6},{8,15},{9,8},{10,9... | collective-permute-start | bytes 786440 | tf_op jit(solution)/shard_map/ppermute | solution.py:187
  143.8 11.2 %collective-permute-start.19 = (f32[128,512]{1,0:T(8,128)S(1)}, f32[128,512]{1,0:T(8,128)S(1)}, u32[]{:S(2)}, u32[]{:S(2)}) collective-permute-start(f32[128,512]{1,0:T(8,128)S(1)} %add.204), channel_id=1, source_target_pairs={{0,1},{1,2},{2,3},{3,4},{4,5},{5,6},{6,7},{7,0},{8,9},{9,10},{10,1... | collective-permute-start | bytes 786440 | tf_op jit(solution)/shard_map/ppermute | solution.py:187
  143.9 11.2 %collective-permute-start.26 = (f32[128,512]{1,0:T(8,128)S(1)}, f32[128,512]{1,0:T(8,128)S(1)}, u32[]{:S(2)}, u32[]{:S(2)}) collective-permute-start(f32[128,512]{1,0:T(8,128)S(1)} %add.211), channel_id=1, source_target_pairs={{0,7},{1,0},{2,1},{3,2},{4,3},{5,4},{6,5},{7,6},{8,15},{9,8},{10,9... | collective-permute-start | bytes 786440 | tf_op jit(solution)/shard_map/ppermute | solution.py:187
  149.4 11.2 %collective-permute-start.6 = (f32[128,512]{1,0:T(8,128)S(1)}, f32[128,512]{1,0:T(8,128)S(1)}, u32[]{:S(2)}, u32[]{:S(2)}) collective-permute-start(f32[128,512]{1,0:T(8,128)S(1)} %add.189), channel_id=1, source_target_pairs={{0,1},{1,2},{2,3},{3,4},{4,5},{5,6},{6,7},{7,0},{8,9},{9,10},{10,1... | collective-permute-start | bytes 786440 | tf_op jit(solution)/shard_map/ppermute | solution.py:187
  149.8 10.8 %collective-permute-start.13 = (f32[128,512]{1,0:T(8,128)S(1)}, f32[128,512]{1,0:T(8,128)S(1)}, u32[]{:S(2)}, u32[]{:S(2)}) collective-permute-start(f32[128,512]{1,0:T(8,128)S(1)} %add.198), channel_id=1, source_target_pairs={{0,7},{1,0},{2,1},{3,2},{4,3},{5,4},{6,5},{7,6},{8,15},{9,8},{10,9... | collective-permute-start | bytes 786440 | tf_op jit(solution)/shard_map/ppermute | solution.py:187
  155.0 11.2 %collective-permute-start.20 = (f32[128,512]{1,0:T(8,128)S(1)}, f32[128,512]{1,0:T(8,128)S(1)}, u32[]{:S(2)}, u32[]{:S(2)}) collective-permute-start(f32[128,512]{1,0:T(8,128)S(1)} %add.205), channel_id=1, source_target_pairs={{0,1},{1,2},{2,3},{3,4},{4,5},{5,6},{6,7},{7,0},{8,9},{9,10},{10,1... | collective-permute-start | bytes 786440 | tf_op jit(solution)/shard_map/ppermute | solution.py:187
  155.2 11.1 %collective-permute-start.27 = (f32[128,512]{1,0:T(8,128)S(1)}, f32[128,512]{1,0:T(8,128)S(1)}, u32[]{:S(2)}, u32[]{:S(2)}) collective-permute-start(f32[128,512]{1,0:T(8,128)S(1)} %add.212), channel_id=1, source_target_pairs={{0,7},{1,0},{2,1},{3,2},{4,3},{5,4},{6,5},{7,6},{8,15},{9,8},{10,9... | collective-permute-start | bytes 786440 | tf_op jit(solution)/shard_map/ppermute | solution.py:187

commit v4 on v3

--- a/solution.py
+++ b/solution.py
@@ -11,6 +11,7 @@
 F32 = jnp.float32
 BF16 = jnp.bfloat16
 VMEM_BYTES = 48 * 1024 * 1024
+GROUP = 8
 
 
 def halves(table):
@@ -47,14 +48,29 @@
     return jnp.dot(left, right, preferred_element_type=F32)
 
 
-def dot_table_left(table_ref, value):
-    head, tail = split(value)
-    return dot(table_ref[0], head) + (dot(table_ref[1], head) + dot(table_ref[0], tail))
-
-
-def dot_table_right(value, table_ref):
-    head, tail = split(value)
-    return dot(head, table_ref[0]) + (dot(head, table_ref[1]) + dot(tail, table_ref[0]))
+def tables_of(n_parts):
+    first, turn_cos, turn_sin, second, second_back, first_back = transform_tables(n_parts)
+
+    def left(table):
+        high, low = halves(table)
+        return jnp.asarray(np.concatenate([high, low, high], 1))
+
+    def right(table):
+        high, low = halves(table)
+        return jnp.asarray(np.concatenate([high, low, high], 0))
+
+    turns = [jnp.asarray(turn_cos.astype(np.float32)), jnp.asarray(turn_sin.astype(np.float32))]
+    return [left(first), *turns, right(second), right(second_back), left(first_back)]
+
+
+def from_left(table, value):
+    high, low = split(value)
+    return dot(table, jnp.concatenate([high, high, low], 0))
+
+
+def from_right(value, table):
+    high, low = split(value)
+    return dot(jnp.concatenate([high, high, low], 1), table)
 
 
 def pack_kernel(key_ref, value_ref, taps_ref, out_ref):
@@ -65,13 +81,10 @@
 
 
 def pack(key_in, value_in, filter_taps, n_parts):
-    tok_rows, channels = key_in.shape
+    tok_rows, span = key_in.shape
     pieces = tok_rows // LANES
-    width = channels // n_parts
-    block = pl.BlockSpec((LANES, channels), lambda j: (j, 0))
-    key_in, value_in, filter_taps = (
-        pltpu.with_memory_space_constraint(x, pltpu.HBM) for x in (key_in, value_in, filter_taps)
-    )
+    width = span // n_parts
+    block = pl.BlockSpec((LANES, span), lambda j: (j, 0))
     return pl.pallas_call(
         pack_kernel,
         grid=(pieces,),
@@ -80,10 +93,10 @@
         out_shape=jax.ShapeDtypeStruct((n_parts, 2, pieces, width, LANES), F32),
         compiler_params=pltpu.CompilerParams(vmem_limit_bytes=VMEM_BYTES),
         name="pack",
-    )(key_in, value_in, filter_taps)
-
-
-def conv_kernel(n_parts, width, x_ref, first_ref, cos_ref, sin_ref, second_ref, back2_ref, back1_ref, out_ref):
+    )(*(pltpu.with_memory_space_constraint(x, pltpu.HBM) for x in (key_in, value_in, filter_taps)))
+
+
+def conv_kernel(n_parts, width, group, x_ref, first_ref, cos_ref, sin_ref, second_ref, back2_ref, back1_ref, out_ref):
     pieces = LANES // n_parts
     rows = pieces * width
     cos_t, sin_t = cos_ref[...], sin_ref[...]
@@ -97,57 +110,51 @@
             0,
         )
 
-    def spectra(channel):
-        both = jnp.concatenate([column(0, channel), column(1, channel)], 1)
-        coarse = dot_table_left(first_ref, both)
-        turned = []
-        for lane in (0, LANES):
-            real = coarse[:LANES, lane : lane + LANES]
-            imag = coarse[LANES:, lane : lane + LANES]
-            turned.append(
-                jnp.concatenate([real * cos_t - imag * sin_t, real * sin_t + imag * cos_t], 1)
-            )
-        full = dot_table_right(jnp.concatenate(turned, 0), second_ref)
-        s_re, s_im = full[:LANES, :LANES], full[:LANES, LANES:]
-        h_re, h_im = full[LANES:, :LANES], full[LANES:, LANES:]
+    def spectrum(coarse, lane):
+        real = coarse[:LANES, lane : lane + LANES]
+        imag = coarse[LANES:, lane : lane + LANES]
+        return jnp.concatenate([real * cos_t - imag * sin_t, real * sin_t + imag * cos_t], 1)
+
+    def product(pair):
+        s_re, s_im = pair[:LANES, :LANES], pair[:LANES, LANES:]
+        h_re, h_im = pair[LANES:, :LANES], pair[LANES:, LANES:]
         return jnp.concatenate([s_re * h_re - s_im * h_im, s_re * h_im + s_im * h_re], 1)
 
-    @pl.loop(0, width // 2)
-    def _(pair):
-        product = jnp.concatenate([spectra(2 * pair), spectra(2 * pair + 1)], 0)
-        back = dot_table_right(product, back2_ref)
-        turned = []
-        for row in (0, LANES):
-            real = back[row : row + LANES, :LANES]
-            imag = back[row : row + LANES, LANES:]
-            turned.append(
-                jnp.concatenate([real * cos_t + imag * sin_t, imag * cos_t - real * sin_t], 0)
-            )
-        result = dot_table_left(back1_ref, jnp.concatenate(turned, 1))
-        for at in range(2):
+    def unturn(back):
+        real, imag = back[:, :LANES], back[:, LANES:]
+        return jnp.concatenate([real * cos_t + imag * sin_t, imag * cos_t - real * sin_t], 0)
+
+    @pl.loop(0, width // group)
+    def _(turn):
+        channels = [turn * group + i for i in range(group)]
+        coarse = [
+            from_left(first_ref[...], jnp.concatenate([column(0, c), column(1, c)], 1))
+            for c in channels
+        ]
+        turned = [spectrum(c, lane) for c in coarse for lane in (0, LANES)]
+        full = from_right(jnp.concatenate(turned, 0), second_ref[...])
+        products = [product(full[2 * k * LANES : 2 * (k + 1) * LANES]) for k in range(group)]
+        back = from_right(jnp.concatenate(products, 0), back2_ref[...])
+        columns = [unturn(back[k * LANES : (k + 1) * LANES]) for k in range(group)]
+        result = from_left(back1_ref[...], jnp.concatenate(columns, 1))
+        for k, channel in enumerate(channels):
             for j in range(pieces):
-                out_ref[pl.ds(j * width + 2 * pair + at, n_parts, stride=rows), :] = result[
-                    j * n_parts : (j + 1) * n_parts, at * LANES : (at + 1) * LANES
+                out_ref[pl.ds(j * width + channel, n_parts, stride=rows), :] = result[
+                    j * n_parts : (j + 1) * n_parts, k * LANES : (k + 1) * LANES
                 ]
 
 
 def convolve(moved, n_parts, width):
-    first, turn_cos, turn_sin, second, back2, back1 = transform_tables(n_parts)
-    tables = [
-        jnp.asarray(np.stack(halves(first))),
-        jnp.asarray(turn_cos.astype(np.float32)),
-        jnp.asarray(turn_sin.astype(np.float32)),
-        jnp.asarray(np.stack(halves(second))),
-        jnp.asarray(np.stack(halves(back2))),
-        jnp.asarray(np.stack(halves(back1))),
-    ]
     pieces = LANES // n_parts
+    group = GROUP if width % GROUP == 0 else 1
+    flops = 2 * 3 * LANES * LANES * LANES * width * 18
     return pl.pallas_call(
-        lambda *refs: conv_kernel(n_parts, width, *refs),
+        lambda *refs: conv_kernel(n_parts, width, group, *refs),
         out_shape=jax.ShapeDtypeStruct((n_parts * pieces * width, LANES), F32),
         compiler_params=pltpu.CompilerParams(vmem_limit_bytes=VMEM_BYTES),
+        cost_estimate=pl.CostEstimate(flops=flops, bytes_accessed=moved.size * 6, transcendentals=0),
         name="convolve",
-    )(moved, *tables)
+    )(moved, *tables_of(n_parts))
 
 
 def gate_kernel(conv_ref, query_ref, key_ref, value_ref, gain_ref, out_ref):
@@ -185,6 +192,7 @@
     total = dot(gated, weights[0])
     for step in range(1, n_chan):
         got = lax.ppermute(total, "chan", hops)
+        got, gated = lax.optimization_barrier((got, gated))
         total = got + dot(gated, weights[step])
     return total
 
@@ -197,7 +205,7 @@
     width = channels // n_parts
     packed = pack(key_in, value_in, filter_taps, n_parts)
     moved = lax.all_to_all(packed, "seq", split_axis=0, concat_axis=0, tiled=True)
-    conv = convolve(moved.reshape(n_parts * 2 * pieces * width, LANES), n_parts, width)
+    conv = convolve(moved.reshape(-1, LANES), n_parts, width)
     conv = conv.reshape(n_parts, pieces, width, LANES)
     me = lax.axis_index("chan")
     out_cols = out_weight.shape[1] // n_chan

time: 167 us -> 160 us (0.958)
  Pallas kernels: 16.6 us -> 12.9 us
  waiting for transfers between devices: 54.6 us -> 51.7 us
  matrix products: 10 us -> 7.5 us
    pallas_call x1, Pallas kernels: 12.9 us -> 9.14 us  [convolve(): pl.pallas_call(lambda *refs: conv_kernel(n_parts, width, group, *refs), o...]
    ppermute x28, waiting for transfers between devices: 37.4 us -> 34.4 us  [ring_sum(): got = lax.ppermute(total, 'chan', hops)]
    dot_general x32, matrix products: 10 us -> 7.5 us  [dot(): return jnp.dot(left, right, preferred_element_type=F32)]
  transfers between devices with their start and end apart: 29 -> 29, of which waited for: 15 -> 15; matrix products, arithmetic and copies ran while one was open for 3% -> 5% of each run, Pallas kernels for 0% -> 0%
where the time goes in v4:
time: 160 us
  waiting for transfers between devices  51.7 us (32%)
  starting transfers between devices  46.6 us (29%)
  blocking collectives  36.8 us (23%)
  Pallas kernels  12.9 us (8%)
  matrix products  7.5 us (5%)
  other arithmetic  1.88 us (1%)
    ppermute x28, starting transfers between devices, ring_sum(): got = lax.ppermute(total, 'chan', hops)  42.6 us
    all_to_all x1, blocking collectives, on_device(): lax.all_to_all(packed, 'seq', split_axis=0, concat_axis=0, tiled=True)  36.8 us
    ppermute x28, waiting for transfers between devices, ring_sum(): got = lax.ppermute(total, 'chan', hops)  34.4 us
    all_to_all x1, waiting for transfers between devices, on_device(): conv = lax.all_to_all(conv, 'seq', split_axis=0, concat_axis=0, tiled=True)  17.2 us
    pallas_call x1, Pallas kernels, convolve(): pl.pallas_call(lambda *refs: conv_kernel(n_parts, width, group, *refs), o...  9.14 us
    dot_general x32, matrix products, dot(): return jnp.dot(left, right, preferred_element_type=F32)  7.5 us
    all_to_all x1, starting transfers between devices, on_device(): conv = lax.all_to_all(conv, 'seq', split_axis=0, concat_axis=0, tiled=True)  3.97 us
  transfers between devices with their start and end apart: 29, of which 15 were waited for; matrix products, arithmetic and copies ran while one was open for 5% of the time, Pallas kernels for 0%

profile of v4, /device:TPU:1, one launch (start us, length us, event | category | flops | bytes accessed | tf_op | source)
XLA Modules:
  0.0 159.6 jit_solution(12778983567187521965)
XLA Ops:
  0.0 3.0 %pack.1 = f32[32,2,4,16,128]{4,3,2,1,0:T(8,128)S(1)} custom-call(bf16[512,512]{1,0:T(8,128)(2,1)} %key_ref.3, bf16[512,512]{1,0:T(8,128)(2,1)} %value_ref.3, f32[512,512]{1,0:T(8,128)} %taps_ref.1), custom_call_target="tpu_custom_call" | custom-call | tf_op jit(solution)/shard_map/pack/pallas_call | solution.py:88
  3.1 36.8 %all_to_all.10 = f32[32,2,4,16,128]{4,3,2,1,0:T(8,128)S(1)} all-to-all(f32[32,2,4,16,128]{4,3,2,1,0:T(8,128)S(1)} %pack.1), channel_id=1, replica_groups=mesh['seq'=32,'chan'=8] {'seq'}, dimensions={0} | all-to-all | bytes 4194304 | tf_op jit(solution)/shard_map/all_to_all | solution.py:207
  40.0 9.1 %convolve.1 = f32[2048,128]{1,0:T(8,128)} custom-call(f32[4096,128]{1,0:T(8,128)S(1)} %bitcast.31, bf16[256,384]{1,0:T(8,128)(2,1)S(1)} %copy-done.6, f32[128,128]{1,0:T(8,128)S(1)} %copy-done.8, f32[128,128]{1,0:T(8,128)S(1)} %copy-done.9, bf16[768,256]{1,0:T(8,128)(2,1)S(1)} %copy-done.4, bf16[768,256]{1,0:T(8,128)(2,1)S(1)} %copy-done.5, ...), custom_call_target="tpu_custom_call" | custom-call | flops 3623878656 | bytes 3145728 | tf_op jit(solution)/shard_map/convolve/pallas_call | solution.py:151
  49.1 4.0 %all-to-all-start.1 = ((f32[32,4,16,128]{3,2,1,0:T(8,128)}), f32[32,4,16,128]{3,2,1,0:T(8,128)S(1)}, u32[]{:S(2)}, u32[]{:S(2)}) async-start(f32[32,4,16,128]{3,2,1,0:T(8,128)} %bitcast.1), calls=%async_computation.1 | async-start | bytes 2097152 | tf_op jit(solution)/shard_map/all_to_all | solution.py:219
  53.2 17.2 %all-to-all-done.1.conv_ref = f32[32,4,16,128]{3,2,1,0:T(8,128)S(1)} async-done(((f32[32,4,16,128]{3,2,1,0:T(8,128)}), f32[32,4,16,128]{3,2,1,0:T(8,128)S(1)}, u32[]{:S(2)}, u32[]{:S(2)}) %all-to-all-start.1) | async-done | bytes 1048608 | tf_op jit(solution)/shard_map/all_to_all | solution.py:219
  70.4 0.7 gate.1
  71.2 1.4 copy-done.10
  72.8 0.2 fusion.58
  73.1 1.7 %collective-permute-start = (f32[128,512]{1,0:T(8,128)S(1)}, f32[128,512]{1,0:T(8,128)S(1)}, u32[]{:S(2)}, u32[]{:S(2)}) collective-permute-start(f32[128,512]{1,0:T(8,128)S(1)} %fusion.62), channel_id=1, source_target_pairs={{0,1},{1,2},{2,3},{3,4},{4,5},{5,6},{6,7},{7,0},{8,9},{9,10},{10,1... | collective-permute-start | bytes 786440 | tf_op jit(solution)/shard_map/ppermute | solution.py:194
  75.0 4.0 %collective-permute-start.7 = (f32[128,512]{1,0:T(8,128)S(1)}, f32[128,512]{1,0:T(8,128)S(1)}, u32[]{:S(2)}, u32[]{:S(2)}) collective-permute-start(f32[128,512]{1,0:T(8,128)S(1)} %fusion.12), channel_id=1, source_target_pairs={{0,7},{1,0},{2,1},{3,2},{4,3},{5,4},{6,5},{7,6},{8,15},{9,8},{10,9... | collective-permute-start | bytes 786440 | tf_op jit(solution)/shard_map/ppermute | solution.py:194
  79.4 2.7 %collective-permute-start.21 = (f32[128,512]{1,0:T(8,128)S(1)}, f32[128,512]{1,0:T(8,128)S(1)}, u32[]{:S(2)}, u32[]{:S(2)}) collective-permute-start(f32[128,512]{1,0:T(8,128)S(1)} %fusion.8), channel_id=1, source_target_pairs={{0,7},{1,0},{2,1},{3,2},{4,3},{5,4},{6,5},{7,6},{8,15},{9,8},{10,9... | collective-permute-start | bytes 786440 | tf_op jit(solution)/shard_map/ppermute | solution.py:194
  82.0 3.0 %collective-permute-done = f32[128,512]{1,0:T(8,128)S(1)} collective-permute-done((f32[128,512]{1,0:T(8,128)S(1)}, f32[128,512]{1,0:T(8,128)S(1)}, u32[]{:S(2)}, u32[]{:S(2)}) %collective-permute-start) | collective-permute-done | bytes 262176 | tf_op jit(solution)/shard_map/ppermute | solution.py:194
  85.4 0.2 fusion.20
  85.7 2.7 %collective-permute-start.8 = (f32[128,512]{1,0:T(8,128)S(1)}, f32[128,512]{1,0:T(8,128)S(1)}, u32[]{:S(2)}, u32[]{:S(2)}) collective-permute-start(f32[128,512]{1,0:T(8,128)S(1)} %add.193), channel_id=1, source_target_pairs={{0,7},{1,0},{2,1},{3,2},{4,3},{5,4},{6,5},{7,6},{8,15},{9,8},{10,9... | collective-permute-start | bytes 786440 | tf_op jit(solution)/shard_map/ppermute | solution.py:194
  88.5 2.2 %collective-permute-done.14 = f32[128,512]{1,0:T(8,128)S(1)} collective-permute-done((f32[128,512]{1,0:T(8,128)S(1)}, f32[128,512]{1,0:T(8,128)S(1)}, u32[]{:S(2)}, u32[]{:S(2)}) %collective-permute-start.14) | collective-permute-done | bytes 262176 | tf_op jit(solution)/shard_map/ppermute | solution.py:194
  91.1 0.2 fusion.16
  91.3 2.9 %collective-permute-start.22 = (f32[128,512]{1,0:T(8,128)S(1)}, f32[128,512]{1,0:T(8,128)S(1)}, u32[]{:S(2)}, u32[]{:S(2)}) collective-permute-start(f32[128,512]{1,0:T(8,128)S(1)} %add.207), channel_id=1, source_target_pairs={{0,7},{1,0},{2,1},{3,2},{4,3},{5,4},{6,5},{7,6},{8,15},{9,8},{10,9... | collective-permute-start | bytes 786440 | tf_op jit(solution)/shard_map/ppermute | solution.py:194
  94.3 2.0 %collective-permute-done.1 = f32[128,512]{1,0:T(8,128)S(1)} collective-permute-done((f32[128,512]{1,0:T(8,128)S(1)}, f32[128,512]{1,0:T(8,128)S(1)}, u32[]{:S(2)}, u32[]{:S(2)}) %collective-permute-start.1) | collective-permute-done | bytes 262176 | tf_op jit(solution)/shard_map/ppermute | solution.py:194
  96.7 0.2 fusion.28
  97.0 2.7 %collective-permute-start.9 = (f32[128,512]{1,0:T(8,128)S(1)}, f32[128,512]{1,0:T(8,128)S(1)}, u32[]{:S(2)}, u32[]{:S(2)}) collective-permute-start(f32[128,512]{1,0:T(8,128)S(1)} %add.194), channel_id=1, source_target_pairs={{0,7},{1,0},{2,1},{3,2},{4,3},{5,4},{6,5},{7,6},{8,15},{9,8},{10,9... | collective-permute-start | bytes 786440 | tf_op jit(solution)/shard_map/ppermute | solution.py:194
  99.7 2.2 %collective-permute-done.15 = f32[128,512]{1,0:T(8,128)S(1)} collective-permute-done((f32[128,512]{1,0:T(8,128)S(1)}, f32[128,512]{1,0:T(8,128)S(1)}, u32[]{:S(2)}, u32[]{:S(2)}) %collective-permute-start.15) | collective-permute-done | bytes 262176 | tf_op jit(solution)/shard_map/ppermute | solution.py:194
  102.3 0.2 fusion.24
  102.6 2.7 %collective-permute-start.23 = (f32[128,512]{1,0:T(8,128)S(1)}, f32[128,512]{1,0:T(8,128)S(1)}, u32[]{:S(2)}, u32[]{:S(2)}) collective-permute-start(f32[128,512]{1,0:T(8,128)S(1)} %add.208), channel_id=1, source_target_pairs={{0,7},{1,0},{2,1},{3,2},{4,3},{5,4},{6,5},{7,6},{8,15},{9,8},{10,9... | collective-permute-start | bytes 786440 | tf_op jit(solution)/shard_map/ppermute | solution.py:194
  105.3 2.2 %collective-permute-done.2 = f32[128,512]{1,0:T(8,128)S(1)} collective-permute-done((f32[128,512]{1,0:T(8,128)S(1)}, f32[128,512]{1,0:T(8,128)S(1)}, u32[]{:S(2)}, u32[]{:S(2)}) %collective-permute-start.2) | collective-permute-done | bytes 262176 | tf_op jit(solution)/shard_map/ppermute | solution.py:194
  108.2 2.7 %collective-permute-start.10 = (f32[128,512]{1,0:T(8,128)S(1)}, f32[128,512]{1,0:T(8,128)S(1)}, u32[]{:S(2)}, u32[]{:S(2)}) collective-permute-start(f32[128,512]{1,0:T(8,128)S(1)} %add.195), channel_id=1, source_target_pairs={{0,7},{1,0},{2,1},{3,2},{4,3},{5,4},{6,5},{7,6},{8,15},{9,8},{10,9... | collective-permute-start | bytes 786440 | tf_op jit(solution)/shard_map/ppermute | solution.py:194
  110.9 2.2 %collective-permute-done.16 = f32[128,512]{1,0:T(8,128)S(1)} collective-permute-done((f32[128,512]{1,0:T(8,128)S(1)}, f32[128,512]{1,0:T(8,128)S(1)}, u32[]{:S(2)}, u32[]{:S(2)}) %collective-permute-start.16) | collective-permute-done | bytes 262176 | tf_op jit(solution)/shard_map/ppermute | solution.py:194
  113.5 0.2 fusion.32
  113.8 2.7 %collective-permute-start.24 = (f32[128,512]{1,0:T(8,128)S(1)}, f32[128,512]{1,0:T(8,128)S(1)}, u32[]{:S(2)}, u32[]{:S(2)}) collective-permute-start(f32[128,512]{1,0:T(8,128)S(1)} %add.209), channel_id=1, source_target_pairs={{0,7},{1,0},{2,1},{3,2},{4,3},{5,4},{6,5},{7,6},{8,15},{9,8},{10,9... | collective-permute-start | bytes 786440 | tf_op jit(solution)/shard_map/ppermute | solution.py:194
  116.5 2.2 %collective-permute-done.3 = f32[128,512]{1,0:T(8,128)S(1)} collective-permute-done((f32[128,512]{1,0:T(8,128)S(1)}, f32[128,512]{1,0:T(8,128)S(1)}, u32[]{:S(2)}, u32[]{:S(2)}) %collective-permute-start.3) | collective-permute-done | bytes 262176 | tf_op jit(solution)/shard_map/ppermute | solution.py:194
  119.4 2.7 %collective-permute-start.11 = (f32[128,512]{1,0:T(8,128)S(1)}, f32[128,512]{1,0:T(8,128)S(1)}, u32[]{:S(2)}, u32[]{:S(2)}) collective-permute-start(f32[128,512]{1,0:T(8,128)S(1)} %add.196), channel_id=1, source_target_pairs={{0,7},{1,0},{2,1},{3,2},{4,3},{5,4},{6,5},{7,6},{8,15},{9,8},{10,9... | collective-permute-start | bytes 786440 | tf_op jit(solution)/shard_map/ppermute | solution.py:194
  122.2 2.2 %collective-permute-done.17 = f32[128,512]{1,0:T(8,128)S(1)} collective-permute-done((f32[128,512]{1,0:T(8,128)S(1)}, f32[128,512]{1,0:T(8,128)S(1)}, u32[]{:S(2)}, u32[]{:S(2)}) %collective-permute-start.17) | collective-permute-done | bytes 262176 | tf_op jit(solution)/shard_map/ppermute | solution.py:194
  125.1 2.7 %collective-permute-start.25 = (f32[128,512]{1,0:T(8,128)S(1)}, f32[128,512]{1,0:T(8,128)S(1)}, u32[]{:S(2)}, u32[]{:S(2)}) collective-permute-start(f32[128,512]{1,0:T(8,128)S(1)} %add.210), channel_id=1, source_target_pairs={{0,7},{1,0},{2,1},{3,2},{4,3},{5,4},{6,5},{7,6},{8,15},{9,8},{10,9... | collective-permute-start | bytes 786440 | tf_op jit(solution)/shard_map/ppermute | solution.py:194
  127.8 2.2 %collective-permute-done.4 = f32[128,512]{1,0:T(8,128)S(1)} collective-permute-done((f32[128,512]{1,0:T(8,128)S(1)}, f32[128,512]{1,0:T(8,128)S(1)}, u32[]{:S(2)}, u32[]{:S(2)}) %collective-permute-start.4) | collective-permute-done | bytes 262176 | tf_op jit(solution)/shard_map/ppermute | solution.py:194
  130.7 2.9 %collective-permute-start.12 = (f32[128,512]{1,0:T(8,128)S(1)}, f32[128,512]{1,0:T(8,128)S(1)}, u32[]{:S(2)}, u32[]{:S(2)}) collective-permute-start(f32[128,512]{1,0:T(8,128)S(1)} %add.197), channel_id=1, source_target_pairs={{0,7},{1,0},{2,1},{3,2},{4,3},{5,4},{6,5},{7,6},{8,15},{9,8},{10,9... | collective-permute-start | bytes 786440 | tf_op jit(solution)/shard_map/ppermute | solution.py:194
  133.6 2.0 %collective-permute-done.18 = f32[128,512]{1,0:T(8,128)S(1)} collective-permute-done((f32[128,512]{1,0:T(8,128)S(1)}, f32[128,512]{1,0:T(8,128)S(1)}, u32[]{:S(2)}, u32[]{:S(2)}) %collective-permute-start.18) | collective-permute-done | bytes 262176 | tf_op jit(solution)/shard_map/ppermute | solution.py:194
  136.0 0.2 fusion.48
  136.3 2.7 %collective-permute-start.26 = (f32[128,512]{1,0:T(8,128)S(1)}, f32[128,512]{1,0:T(8,128)S(1)}, u32[]{:S(2)}, u32[]{:S(2)}) collective-permute-start(f32[128,512]{1,0:T(8,128)S(1)} %add.211), channel_id=1, source_target_pairs={{0,7},{1,0},{2,1},{3,2},{4,3},{5,4},{6,5},{7,6},{8,15},{9,8},{10,9... | collective-permute-start | bytes 786440 | tf_op jit(solution)/shard_map/ppermute | solution.py:194
  139.0 2.2 %collective-permute-done.5 = f32[128,512]{1,0:T(8,128)S(1)} collective-permute-done((f32[128,512]{1,0:T(8,128)S(1)}, f32[128,512]{1,0:T(8,128)S(1)}, u32[]{:S(2)}, u32[]{:S(2)}) %collective-permute-start.5) | collective-permute-done | bytes 262176 | tf_op jit(solution)/shard_map/ppermute | solution.py:194
  141.6 0.2 fusion.60
  141.9 2.7 %collective-permute-start.13 = (f32[128,512]{1,0:T(8,128)S(1)}, f32[128,512]{1,0:T(8,128)S(1)}, u32[]{:S(2)}, u32[]{:S(2)}) collective-permute-start(f32[128,512]{1,0:T(8,128)S(1)} %add.198), channel_id=1, source_target_pairs={{0,7},{1,0},{2,1},{3,2},{4,3},{5,4},{6,5},{7,6},{8,15},{9,8},{10,9... | collective-permute-start | bytes 786440 | tf_op jit(solution)/shard_map/ppermute | solution.py:194
  144.6 2.2 %collective-permute-done.19 = f32[128,512]{1,0:T(8,128)S(1)} collective-permute-done((f32[128,512]{1,0:T(8,128)S(1)}, f32[128,512]{1,0:T(8,128)S(1)}, u32[]{:S(2)}, u32[]{:S(2)}) %collective-permute-start.19) | collective-permute-done | bytes 262176 | tf_op jit(solution)/shard_map/ppermute | solution.py:194
  147.2 0.2 fusion.56
  147.5 2.7 %collective-permute-start.27 = (f32[128,512]{1,0:T(8,128)S(1)}, f32[128,512]{1,0:T(8,128)S(1)}, u32[]{:S(2)}, u32[]{:S(2)}) collective-permute-start(f32[128,512]{1,0:T(8,128)S(1)} %add.212), channel_id=1, source_target_pairs={{0,7},{1,0},{2,1},{3,2},{4,3},{5,4},{6,5},{7,6},{8,15},{9,8},{10,9... | collective-permute-start | bytes 786440 | tf_op jit(solution)/shard_map/ppermute | solution.py:194
  150.2 2.2 %collective-permute-done.6 = f32[128,512]{1,0:T(8,128)S(1)} collective-permute-done((f32[128,512]{1,0:T(8,128)S(1)}, f32[128,512]{1,0:T(8,128)S(1)}, u32[]{:S(2)}, u32[]{:S(2)}) %collective-permute-start.6) | collective-permute-done | bytes 262176 | tf_op jit(solution)/shard_map/ppermute | solution.py:194
  152.7 0.2 fusion.4
  153.0 5.1 %collective-permute-done.20 = f32[128,512]{1,0:T(8,128)S(1)} collective-permute-done((f32[128,512]{1,0:T(8,128)S(1)}, f32[128,512]{1,0:T(8,128)S(1)}, u32[]{:S(2)}, u32[]{:S(2)}) %collective-permute-start.20) | collective-permute-done | bytes 262176 | tf_op jit(solution)/shard_map/ppermute | solution.py:194
  158.3 0.2 fusion
  158.8 0.8 pad_maximum_fusion
  (98 shorter events, 7.1 us)
Async XLA Ops:
  0.0 39.9 %copy-start.4 = (bf16[768,256]{1,0:T(8,128)(2,1)S(1)}, bf16[768,256]{1,0:T(8,128)(2,1)}, u32[]{:S(2)}) copy-start(bf16[768,256]{1,0:T(8,128)(2,1)} %constant.82.clone.refs_4_) | copy-start | bytes 1179652
  0.0 39.9 %copy-start.5 = (bf16[768,256]{1,0:T(8,128)(2,1)S(1)}, bf16[768,256]{1,0:T(8,128)(2,1)}, u32[]{:S(2)}) copy-start(bf16[768,256]{1,0:T(8,128)(2,1)} %constant.83.clone.refs_5_) | copy-start | bytes 1179652
  0.0 39.9 %copy-start.6 = (bf16[256,384]{1,0:T(8,128)(2,1)S(1)}, bf16[256,384]{1,0:T(8,128)(2,1)}, u32[]{:S(2)}) copy-start(bf16[256,384]{1,0:T(8,128)(2,1)} %constant.81.clone.refs_1_) | copy-start | bytes 589828
  0.0 39.9 %copy-start.7 = (bf16[128,768]{1,0:T(8,128)(2,1)S(1)}, bf16[128,768]{1,0:T(8,128)(2,1)}, u32[]{:S(2)}) copy-start(bf16[128,768]{1,0:T(8,128)(2,1)} %constant.84.clone.refs_6_) | copy-start | bytes 589828
  0.0 39.9 %copy-start.8 = (f32[128,128]{1,0:T(8,128)S(1)}, f32[128,128]{1,0:T(8,128)}, u32[]{:S(2)}) copy-start(f32[128,128]{1,0:T(8,128)} %constant.79.clone.refs_2_) | copy-start | bytes 196612
  0.0 39.9 %copy-start.9 = (f32[128,128]{1,0:T(8,128)S(1)}, f32[128,128]{1,0:T(8,128)}, u32[]{:S(2)}) copy-start(f32[128,128]{1,0:T(8,128)} %constant.80.clone.refs_3_) | copy-start | bytes 196612
  39.9 30.5 %copy-start = (bf16[512,512]{1,0:T(8,128)(2,1)S(1)}, bf16[512,512]{1,0:T(8,128)(2,1)}, u32[]{:S(2)}) copy-start(bf16[512,512]{1,0:T(8,128)(2,1)} %key_ref.3) | copy-start | bytes 1572868
  40.0 30.4 %copy-start.1 = (bf16[512,512]{1,0:T(8,128)(2,1)S(1)}, bf16[512,512]{1,0:T(8,128)(2,1)}, u32[]{:S(2)}) copy-start(bf16[512,512]{1,0:T(8,128)(2,1)} %value_ref.3) | copy-start | bytes 1572868
  40.0 30.4 %copy-start.2 = (bf16[512,512]{1,0:T(8,128)(2,1)S(1)}, bf16[512,512]{1,0:T(8,128)(2,1)}, u32[]{:S(2)}) copy-start(bf16[512,512]{1,0:T(8,128)(2,1)} %query_ref.1) | copy-start | bytes 1572868
  40.0 30.4 %copy-start.3 = (f32[512]{0:T(512)S(1)}, f32[512]{0:T(512)}, u32[]{:S(2)}) copy-start(f32[512]{0:T(512)} %param.16) | copy-start | bytes 6148
  49.1 21.3 %all-to-all-start.1 = ((f32[32,4,16,128]{3,2,1,0:T(8,128)}), f32[32,4,16,128]{3,2,1,0:T(8,128)S(1)}, u32[]{:S(2)}, u32[]{:S(2)}) async-start(f32[32,4,16,128]{3,2,1,0:T(8,128)} %bitcast.1), calls=%async_computation.1 | async-start | bytes 2097152 | tf_op jit(solution)/shard_map/all_to_all | solution.py:219
  70.4 2.2 %copy-start.10 = (bf16[512,4096]{1,0:T(8,128)(2,1)S(1)}, bf16[512,4096]{1,0:T(8,128)(2,1)}, u32[]{:S(2)}) copy-start(bf16[512,4096]{1,0:T(8,128)(2,1)} %param.17) | copy-start | bytes 12582916
  73.1 12.0 %collective-permute-start = (f32[128,512]{1,0:T(8,128)S(1)}, f32[128,512]{1,0:T(8,128)S(1)}, u32[]{:S(2)}, u32[]{:S(2)}) collective-permute-start(f32[128,512]{1,0:T(8,128)S(1)} %fusion.62), channel_id=1, source_target_pairs={{0,1},{1,2},{2,3},{3,4},{4,5},{5,6},{6,7},{7,0},{8,9},{9,10},{10,1... | collective-permute-start | bytes 786440 | tf_op jit(solution)/shard_map/ppermute | solution.py:194
  75.0 10.4 %collective-permute-start.7 = (f32[128,512]{1,0:T(8,128)S(1)}, f32[128,512]{1,0:T(8,128)S(1)}, u32[]{:S(2)}, u32[]{:S(2)}) collective-permute-start(f32[128,512]{1,0:T(8,128)S(1)} %fusion.12), channel_id=1, source_target_pairs={{0,7},{1,0},{2,1},{3,2},{4,3},{5,4},{6,5},{7,6},{8,15},{9,8},{10,9... | collective-permute-start | bytes 786440 | tf_op jit(solution)/shard_map/ppermute | solution.py:194
  79.3 11.4 %collective-permute-start.14 = (f32[128,512]{1,0:T(8,128)S(1)}, f32[128,512]{1,0:T(8,128)S(1)}, u32[]{:S(2)}, u32[]{:S(2)}) collective-permute-start(f32[128,512]{1,0:T(8,128)S(1)} %fusion.58), channel_id=1, source_target_pairs={{0,1},{1,2},{2,3},{3,4},{4,5},{5,6},{6,7},{7,0},{8,9},{9,10},{10,1... | collective-permute-start | bytes 786440 | tf_op jit(solution)/shard_map/ppermute | solution.py:194
  79.4 11.7 %collective-permute-start.21 = (f32[128,512]{1,0:T(8,128)S(1)}, f32[128,512]{1,0:T(8,128)S(1)}, u32[]{:S(2)}, u32[]{:S(2)}) collective-permute-start(f32[128,512]{1,0:T(8,128)S(1)} %fusion.8), channel_id=1, source_target_pairs={{0,7},{1,0},{2,1},{3,2},{4,3},{5,4},{6,5},{7,6},{8,15},{9,8},{10,9... | collective-permute-start | bytes 786440 | tf_op jit(solution)/shard_map/ppermute | solution.py:194
  85.3 11.0 %collective-permute-start.1 = (f32[128,512]{1,0:T(8,128)S(1)}, f32[128,512]{1,0:T(8,128)S(1)}, u32[]{:S(2)}, u32[]{:S(2)}) collective-permute-start(f32[128,512]{1,0:T(8,128)S(1)} %add.174), channel_id=1, source_target_pairs={{0,1},{1,2},{2,3},{3,4},{4,5},{5,6},{6,7},{7,0},{8,9},{9,10},{10,1... | collective-permute-start | bytes 786440 | tf_op jit(solution)/shard_map/ppermute | solution.py:194
  85.7 10.9 %collective-permute-start.8 = (f32[128,512]{1,0:T(8,128)S(1)}, f32[128,512]{1,0:T(8,128)S(1)}, u32[]{:S(2)}, u32[]{:S(2)}) collective-permute-start(f32[128,512]{1,0:T(8,128)S(1)} %add.193), channel_id=1, source_target_pairs={{0,7},{1,0},{2,1},{3,2},{4,3},{5,4},{6,5},{7,6},{8,15},{9,8},{10,9... | collective-permute-start | bytes 786440 | tf_op jit(solution)/shard_map/ppermute | solution.py:194
  91.0 11.0 %collective-permute-start.15 = (f32[128,512]{1,0:T(8,128)S(1)}, f32[128,512]{1,0:T(8,128)S(1)}, u32[]{:S(2)}, u32[]{:S(2)}) collective-permute-start(f32[128,512]{1,0:T(8,128)S(1)} %add.200), channel_id=1, source_target_pairs={{0,1},{1,2},{2,3},{3,4},{4,5},{5,6},{6,7},{7,0},{8,9},{9,10},{10,1... | collective-permute-start | bytes 786440 | tf_op jit(solution)/shard_map/ppermute | solution.py:194
  91.3 10.9 %collective-permute-start.22 = (f32[128,512]{1,0:T(8,128)S(1)}, f32[128,512]{1,0:T(8,128)S(1)}, u32[]{:S(2)}, u32[]{:S(2)}) collective-permute-start(f32[128,512]{1,0:T(8,128)S(1)} %add.207), channel_id=1, source_target_pairs={{0,7},{1,0},{2,1},{3,2},{4,3},{5,4},{6,5},{7,6},{8,15},{9,8},{10,9... | collective-permute-start | bytes 786440 | tf_op jit(solution)/shard_map/ppermute | solution.py:194
  96.6 11.0 %collective-permute-start.2 = (f32[128,512]{1,0:T(8,128)S(1)}, f32[128,512]{1,0:T(8,128)S(1)}, u32[]{:S(2)}, u32[]{:S(2)}) collective-permute-start(f32[128,512]{1,0:T(8,128)S(1)} %add.177), channel_id=1, source_target_pairs={{0,1},{1,2},{2,3},{3,4},{4,5},{5,6},{6,7},{7,0},{8,9},{9,10},{10,1... | collective-permute-start | bytes 786440 | tf_op jit(solution)/shard_map/ppermute | solution.py:194
  97.0 10.9 %collective-permute-start.9 = (f32[128,512]{1,0:T(8,128)S(1)}, f32[128,512]{1,0:T(8,128)S(1)}, u32[]{:S(2)}, u32[]{:S(2)}) collective-permute-start(f32[128,512]{1,0:T(8,128)S(1)} %add.194), channel_id=1, source_target_pairs={{0,7},{1,0},{2,1},{3,2},{4,3},{5,4},{6,5},{7,6},{8,15},{9,8},{10,9... | collective-permute-start | bytes 786440 | tf_op jit(solution)/shard_map/ppermute | solution.py:194
  102.2 11.0 %collective-permute-start.16 = (f32[128,512]{1,0:T(8,128)S(1)}, f32[128,512]{1,0:T(8,128)S(1)}, u32[]{:S(2)}, u32[]{:S(2)}) collective-permute-start(f32[128,512]{1,0:T(8,128)S(1)} %add.201), channel_id=1, source_target_pairs={{0,1},{1,2},{2,3},{3,4},{4,5},{5,6},{6,7},{7,0},{8,9},{9,10},{10,1... | collective-permute-start | bytes 786440 | tf_op jit(solution)/shard_map/ppermute | solution.py:194
  102.6 10.9 %collective-permute-start.23 = (f32[128,512]{1,0:T(8,128)S(1)}, f32[128,512]{1,0:T(8,128)S(1)}, u32[]{:S(2)}, u32[]{:S(2)}) collective-permute-start(f32[128,512]{1,0:T(8,128)S(1)} %add.208), channel_id=1, source_target_pairs={{0,7},{1,0},{2,1},{3,2},{4,3},{5,4},{6,5},{7,6},{8,15},{9,8},{10,9... | collective-permute-start | bytes 786440 | tf_op jit(solution)/shard_map/ppermute | solution.py:194
  107.8 11.0 %collective-permute-start.3 = (f32[128,512]{1,0:T(8,128)S(1)}, f32[128,512]{1,0:T(8,128)S(1)}, u32[]{:S(2)}, u32[]{:S(2)}) collective-permute-start(f32[128,512]{1,0:T(8,128)S(1)} %add.180), channel_id=1, source_target_pairs={{0,1},{1,2},{2,3},{3,4},{4,5},{5,6},{6,7},{7,0},{8,9},{9,10},{10,1... | collective-permute-start | bytes 786440 | tf_op jit(solution)/shard_map/ppermute | solution.py:194
  108.2 10.9 %collective-permute-start.10 = (f32[128,512]{1,0:T(8,128)S(1)}, f32[128,512]{1,0:T(8,128)S(1)}, u32[]{:S(2)}, u32[]{:S(2)}) collective-permute-start(f32[128,512]{1,0:T(8,128)S(1)} %add.195), channel_id=1, source_target_pairs={{0,7},{1,0},{2,1},{3,2},{4,3},{5,4},{6,5},{7,6},{8,15},{9,8},{10,9... | collective-permute-start | bytes 786440 | tf_op jit(solution)/shard_map/ppermute | solution.py:194
  113.4 11.0 %collective-permute-start.17 = (f32[128,512]{1,0:T(8,128)S(1)}, f32[128,512]{1,0:T(8,128)S(1)}, u32[]{:S(2)}, u32[]{:S(2)}) collective-permute-start(f32[128,512]{1,0:T(8,128)S(1)} %add.202), channel_id=1, source_target_pairs={{0,1},{1,2},{2,3},{3,4},{4,5},{5,6},{6,7},{7,0},{8,9},{9,10},{10,1... | collective-permute-start | bytes 786440 | tf_op jit(solution)/shard_map/ppermute | solution.py:194
  113.8 10.9 %collective-permute-start.24 = (f32[128,512]{1,0:T(8,128)S(1)}, f32[128,512]{1,0:T(8,128)S(1)}, u32[]{:S(2)}, u32[]{:S(2)}) collective-permute-start(f32[128,512]{1,0:T(8,128)S(1)} %add.209), channel_id=1, source_target_pairs={{0,7},{1,0},{2,1},{3,2},{4,3},{5,4},{6,5},{7,6},{8,15},{9,8},{10,9... | collective-permute-start | bytes 786440 | tf_op jit(solution)/shard_map/ppermute | solution.py:194
  119.0 11.0 %collective-permute-start.4 = (f32[128,512]{1,0:T(8,128)S(1)}, f32[128,512]{1,0:T(8,128)S(1)}, u32[]{:S(2)}, u32[]{:S(2)}) collective-permute-start(f32[128,512]{1,0:T(8,128)S(1)} %add.183), channel_id=1, source_target_pairs={{0,1},{1,2},{2,3},{3,4},{4,5},{5,6},{6,7},{7,0},{8,9},{9,10},{10,1... | collective-permute-start | bytes 786440 | tf_op jit(solution)/shard_map/ppermute | solution.py:194
  119.4 10.9 %collective-permute-start.11 = (f32[128,512]{1,0:T(8,128)S(1)}, f32[128,512]{1,0:T(8,128)S(1)}, u32[]{:S(2)}, u32[]{:S(2)}) collective-permute-start(f32[128,512]{1,0:T(8,128)S(1)} %add.196), channel_id=1, source_target_pairs={{0,7},{1,0},{2,1},{3,2},{4,3},{5,4},{6,5},{7,6},{8,15},{9,8},{10,9... | collective-permute-start | bytes 786440 | tf_op jit(solution)/shard_map/ppermute | solution.py:194
  124.7 11.0 %collective-permute-start.18 = (f32[128,512]{1,0:T(8,128)S(1)}, f32[128,512]{1,0:T(8,128)S(1)}, u32[]{:S(2)}, u32[]{:S(2)}) collective-permute-start(f32[128,512]{1,0:T(8,128)S(1)} %add.203), channel_id=1, source_target_pairs={{0,1},{1,2},{2,3},{3,4},{4,5},{5,6},{6,7},{7,0},{8,9},{9,10},{10,1... | collective-permute-start | bytes 786440 | tf_op jit(solution)/shard_map/ppermute | solution.py:194
  125.1 10.9 %collective-permute-start.25 = (f32[128,512]{1,0:T(8,128)S(1)}, f32[128,512]{1,0:T(8,128)S(1)}, u32[]{:S(2)}, u32[]{:S(2)}) collective-permute-start(f32[128,512]{1,0:T(8,128)S(1)} %add.210), channel_id=1, source_target_pairs={{0,7},{1,0},{2,1},{3,2},{4,3},{5,4},{6,5},{7,6},{8,15},{9,8},{10,9... | collective-permute-start | bytes 786440 | tf_op jit(solution)/shard_map/ppermute | solution.py:194
  130.3 11.0 %collective-permute-start.5 = (f32[128,512]{1,0:T(8,128)S(1)}, f32[128,512]{1,0:T(8,128)S(1)}, u32[]{:S(2)}, u32[]{:S(2)}) collective-permute-start(f32[128,512]{1,0:T(8,128)S(1)} %add.186), channel_id=1, source_target_pairs={{0,1},{1,2},{2,3},{3,4},{4,5},{5,6},{6,7},{7,0},{8,9},{9,10},{10,1... | collective-permute-start | bytes 786440 | tf_op jit(solution)/shard_map/ppermute | solution.py:194
  130.7 10.9 %collective-permute-start.12 = (f32[128,512]{1,0:T(8,128)S(1)}, f32[128,512]{1,0:T(8,128)S(1)}, u32[]{:S(2)}, u32[]{:S(2)}) collective-permute-start(f32[128,512]{1,0:T(8,128)S(1)} %add.197), channel_id=1, source_target_pairs={{0,7},{1,0},{2,1},{3,2},{4,3},{5,4},{6,5},{7,6},{8,15},{9,8},{10,9... | collective-permute-start | bytes 786440 | tf_op jit(solution)/shard_map/ppermute | solution.py:194
  135.9 11.0 %collective-permute-start.19 = (f32[128,512]{1,0:T(8,128)S(1)}, f32[128,512]{1,0:T(8,128)S(1)}, u32[]{:S(2)}, u32[]{:S(2)}) collective-permute-start(f32[128,512]{1,0:T(8,128)S(1)} %add.204), channel_id=1, source_target_pairs={{0,1},{1,2},{2,3},{3,4},{4,5},{5,6},{6,7},{7,0},{8,9},{9,10},{10,1... | collective-permute-start | bytes 786440 | tf_op jit(solution)/shard_map/ppermute | solution.py:194
  136.3 10.9 %collective-permute-start.26 = (f32[128,512]{1,0:T(8,128)S(1)}, f32[128,512]{1,0:T(8,128)S(1)}, u32[]{:S(2)}, u32[]{:S(2)}) collective-permute-start(f32[128,512]{1,0:T(8,128)S(1)} %add.211), channel_id=1, source_target_pairs={{0,7},{1,0},{2,1},{3,2},{4,3},{5,4},{6,5},{7,6},{8,15},{9,8},{10,9... | collective-permute-start | bytes 786440 | tf_op jit(solution)/shard_map/ppermute | solution.py:194
  141.5 11.0 %collective-permute-start.6 = (f32[128,512]{1,0:T(8,128)S(1)}, f32[128,512]{1,0:T(8,128)S(1)}, u32[]{:S(2)}, u32[]{:S(2)}) collective-permute-start(f32[128,512]{1,0:T(8,128)S(1)} %add.189), channel_id=1, source_target_pairs={{0,1},{1,2},{2,3},{3,4},{4,5},{5,6},{6,7},{7,0},{8,9},{9,10},{10,1... | collective-permute-start | bytes 786440 | tf_op jit(solution)/shard_map/ppermute | solution.py:194
  141.9 10.8 %collective-permute-start.13 = (f32[128,512]{1,0:T(8,128)S(1)}, f32[128,512]{1,0:T(8,128)S(1)}, u32[]{:S(2)}, u32[]{:S(2)}) collective-permute-start(f32[128,512]{1,0:T(8,128)S(1)} %add.198), channel_id=1, source_target_pairs={{0,7},{1,0},{2,1},{3,2},{4,3},{5,4},{6,5},{7,6},{8,15},{9,8},{10,9... | collective-permute-start | bytes 786440 | tf_op jit(solution)/shard_map/ppermute | solution.py:194
  147.1 11.0 %collective-permute-start.20 = (f32[128,512]{1,0:T(8,128)S(1)}, f32[128,512]{1,0:T(8,128)S(1)}, u32[]{:S(2)}, u32[]{:S(2)}) collective-permute-start(f32[128,512]{1,0:T(8,128)S(1)} %add.205), channel_id=1, source_target_pairs={{0,1},{1,2},{2,3},{3,4},{4,5},{5,6},{6,7},{7,0},{8,9},{9,10},{10,1... | collective-permute-start | bytes 786440 | tf_op jit(solution)/shard_map/ppermute | solution.py:194
  147.5 10.8 %collective-permute-start.27 = (f32[128,512]{1,0:T(8,128)S(1)}, f32[128,512]{1,0:T(8,128)S(1)}, u32[]{:S(2)}, u32[]{:S(2)}) collective-permute-start(f32[128,512]{1,0:T(8,128)S(1)} %add.212), channel_id=1, source_target_pairs={{0,7},{1,0},{2,1},{3,2},{4,3},{5,4},{6,5},{7,6},{8,15},{9,8},{10,9... | collective-permute-start | bytes 786440 | tf_op jit(solution)/shard_map/ppermute | solution.py:194

commit v5 on v4

--- a/solution.py
+++ b/solution.py
@@ -10,14 +10,28 @@
 LANES = 128
 F32 = jnp.float32
 BF16 = jnp.bfloat16
-VMEM_BYTES = 48 * 1024 * 1024
+SMALL_VMEM = 16 * 1024 * 1024
+VMEM_BYTES = 24 * 1024 * 1024
 GROUP = 8
+SIDE = 4
+CORES = 2
 
 
 def halves(table):
     head = table.astype(ml_dtypes.bfloat16)
     tail = (table - head.astype(np.float64)).astype(ml_dtypes.bfloat16)
     return head, tail
+
+
+def exchange_order(n_parts):
+    gray = (0, 1, 3, 2)
+    order = [(gray[y] * SIDE + gray[x]) * CORES + c for y in range(SIDE) for x in range(SIDE) for c in range(CORES)]
+    return order if len(order) == n_parts else list(range(n_parts))
+
+
+def exchange(value, n_parts):
+    groups = [exchange_order(n_parts)]
+    return lax.all_to_all(value, "seq", split_axis=0, concat_axis=0, tiled=True, axis_index_groups=groups)
 
 
 def transform_tables(n_parts):
@@ -25,7 +39,7 @@
     total = size * size
     place = np.arange(size)
     pieces = size // n_parts
-    a_of = pieces * (place % n_parts) + place // n_parts
+    a_of = pieces * np.array(exchange_order(n_parts))[place % n_parts] + place // n_parts
     k1 = np.arange(size)
     coarse = -2.0 * np.pi * ((a_of[None, :] * (4 * k1[:, None] + 1)) % (4 * size)) / (4 * size)
     first = np.concatenate([np.cos(coarse), np.sin(coarse)], 0)
@@ -74,24 +88,26 @@
 
 
 def pack_kernel(key_ref, value_ref, taps_ref, out_ref):
-    parts, _, _, width, _ = out_ref.shape
-    signal = key_ref[...].astype(F32) * value_ref[...].astype(F32)
-    out_ref[:, 0, 0] = signal.T.reshape(parts, width, LANES)
-    out_ref[:, 1, 0] = taps_ref[...].T.reshape(parts, width, LANES)
+    parts, _, pieces, width, _ = out_ref.shape
+    for j in range(pieces):
+        at = slice(j * LANES, (j + 1) * LANES)
+        signal = key_ref[at].astype(F32) * value_ref[at].astype(F32)
+        out_ref[:, 0, j] = signal.T.reshape(parts, width, LANES)
+        out_ref[:, 1, j] = taps_ref[at].T.reshape(parts, width, LANES)
 
 
 def pack(key_in, value_in, filter_taps, n_parts):
     tok_rows, span = key_in.shape
     pieces = tok_rows // LANES
-    width = span // n_parts
-    block = pl.BlockSpec((LANES, span), lambda j: (j, 0))
+    block = pl.BlockSpec((tok_rows, span), lambda i: (0, 0))
+    shape = (n_parts, 2, pieces, span // n_parts, LANES)
     return pl.pallas_call(
         pack_kernel,
-        grid=(pieces,),
+        grid=(1,),
         in_specs=[block, block, block],
-        out_specs=pl.BlockSpec((n_parts, 2, 1, width, LANES), lambda j: (0, 0, j, 0, 0)),
-        out_shape=jax.ShapeDtypeStruct((n_parts, 2, pieces, width, LANES), F32),
-        compiler_params=pltpu.CompilerParams(vmem_limit_bytes=VMEM_BYTES),
+        out_specs=pl.BlockSpec(shape, lambda i: (0, 0, 0, 0, 0)),
+        out_shape=jax.ShapeDtypeStruct(shape, F32),
+        compiler_params=pltpu.CompilerParams(vmem_limit_bytes=SMALL_VMEM),
         name="pack",
     )(*(pltpu.with_memory_space_constraint(x, pltpu.HBM) for x in (key_in, value_in, filter_taps)))
 
@@ -181,20 +197,21 @@
         ],
         out_specs=pl.BlockSpec((LANES, channels), lambda j: (j, 0)),
         out_shape=jax.ShapeDtypeStruct((pieces * LANES, channels), BF16),
-        compiler_params=pltpu.CompilerParams(vmem_limit_bytes=VMEM_BYTES),
+        compiler_params=pltpu.CompilerParams(vmem_limit_bytes=SMALL_VMEM),
         name="gate",
     )(conv, query_in, key_in, value_in, skip_gain.reshape(1, channels))
 
 
-def ring_sum(gated, weights, way):
+def ring_sum(gated, weights, way, start):
     n_chan = len(weights)
     hops = [(i, (i + way) % n_chan) for i in range(n_chan)]
-    total = dot(gated, weights[0])
-    for step in range(1, n_chan):
+    total = dot(gated, weights[way * start % n_chan])
+    for ahead in range(start - 1, -1, -1):
         got = lax.ppermute(total, "chan", hops)
+        if ahead == 0:
+            return got
         got, gated = lax.optimization_barrier((got, gated))
-        total = got + dot(gated, weights[step])
-    return total
+        total = got + dot(gated, weights[way * ahead % n_chan])
 
 
 def on_device(query_in, key_in, value_in, filter_taps, skip_gain, out_weight):
@@ -204,25 +221,24 @@
     pieces = tok_rows // LANES
     width = channels // n_parts
     packed = pack(key_in, value_in, filter_taps, n_parts)
-    moved = lax.all_to_all(packed, "seq", split_axis=0, concat_axis=0, tiled=True)
+    moved = exchange(packed, n_parts)
     conv = convolve(moved.reshape(-1, LANES), n_parts, width)
     conv = conv.reshape(n_parts, pieces, width, LANES)
     me = lax.axis_index("chan")
     out_cols = out_weight.shape[1] // n_chan
-
-    def columns(of):
-        start = lax.rem(of + 2 * n_chan, n_chan) * out_cols
-        return lax.dynamic_slice(out_weight, (0, start), (channels, out_cols))
-
-    down = [columns(me - 1 - step) for step in range(n_chan)]
-    up = [down[n_chan - 2 - step] for step in range(n_chan - 1)] + [down[n_chan - 1]]
-    conv = lax.all_to_all(conv, "seq", split_axis=0, concat_axis=0, tiled=True)
+    weights = [
+        lax.dynamic_slice(out_weight, (0, (me + k) % n_chan * out_cols), (channels, out_cols))
+        for k in range(n_chan)
+    ]
+    conv = exchange(conv, n_parts)
+    conv, weights = lax.optimization_barrier((conv, weights))
     gated = gate(conv, query_in, key_in, value_in, skip_gain)
-    quarter = tok_rows // 4
-    rows = [
-        ring_sum(gated[i * quarter : (i + 1) * quarter], (down, up)[i % 2], (1, -1)[i % 2])
-        for i in range(4)
-    ]
+    rows = []
+    half, far = tok_rows // 2, n_chan // 2
+    for block, starts in ((gated[:half], (far, far - 1)), (gated[half:], (far - 1, far))):
+        up, down = [ring_sum(block, weights, way, start) for way, start in zip((1, -1), starts)]
+        up, down, block = lax.optimization_barrier((up, down, block))
+        rows.append(up + down + dot(block, weights[0]))
     return jnp.concatenate(rows, 0).astype(BF16)
 
 

time: 160 us -> 158 us (0.988)
  starting transfers between devices: 46.6 us -> 26.9 us
  waiting for transfers between devices: 51.7 us -> 69.4 us
  local copies, waits for them, and re-layouts: 1.52 us -> 4.28 us
  matrix products: 7.5 us -> 5.75 us
    ppermute x28 -> x14, waiting for transfers between devices: 34.4 us -> 56.6 us  [ring_sum(): got = lax.ppermute(total, 'chan', hops)]
    ppermute x28 -> x14, starting transfers between devices: 42.6 us -> 23.2 us  [ring_sum(): got = lax.ppermute(total, 'chan', hops)]
    all_to_all x1, waiting for transfers between devices: 17.2 us -> 12.8 us  [exchange(): lax.all_to_all(value, 'seq', split_axis=0, concat_axis=0, tiled=True, axi...]
    dynamic_slice x0 -> x1, local copies, waits for them, and re-layouts: none -> 4.16 us  [on_device(): lax.dynamic_slice(out_weight, (0, (me + k) % n_chan * out_cols), (channel...]
    dot_general x32 -> x16, matrix products: 7.5 us -> 5.75 us  [dot(): return jnp.dot(left, right, preferred_element_type=F32)]
  transfers between devices with their start and end apart: 29 -> 15, of which waited for: 15 -> 8; matrix products, arithmetic and copies ran while one was open for 5% -> 5% of each run, Pallas kernels for 0% -> 0%
where the time goes in v5:
time: 158 us
  waiting for transfers between devices  69.4 us (44%)
  blocking collectives  37.3 us (24%)
  starting transfers between devices  26.9 us (17%)
  Pallas kernels  12 us (8%)
  matrix products  5.75 us (4%)
  local copies, waits for them, and re-layouts  4.28 us (3%)
  other arithmetic  1.65 us (1%)
    ppermute x14, waiting for transfers between devices, ring_sum(): got = lax.ppermute(total, 'chan', hops)  56.6 us
    all_to_all x1, blocking collectives, exchange(): lax.all_to_all(value, 'seq', split_axis=0, concat_axis=0, tiled=True, axi...  37.3 us
    ppermute x14, starting transfers between devices, ring_sum(): got = lax.ppermute(total, 'chan', hops)  23.2 us
    all_to_all x1, waiting for transfers between devices, exchange(): lax.all_to_all(value, 'seq', split_axis=0, concat_axis=0, tiled=True, axi...  12.8 us
    pallas_call x1, Pallas kernels, convolve(): pl.pallas_call(lambda *refs: conv_kernel(n_parts, width, group, *refs), o...  9.12 us
    dot_general x16, matrix products, dot(): return jnp.dot(left, right, preferred_element_type=F32)  5.75 us
    dynamic_slice x1, local copies, waits for them, and re-layouts, on_device(): lax.dynamic_slice(out_weight, (0, (me + k) % n_chan * out_cols), (channel...  4.16 us
    all_to_all x1, starting transfers between devices, exchange(): lax.all_to_all(value, 'seq', split_axis=0, concat_axis=0, tiled=True, axi...  3.72 us
  transfers between devices with their start and end apart: 15, of which 8 were waited for; matrix products, arithmetic and copies ran while one was open for 5% of the time, Pallas kernels for 0%

profile of v5, /device:TPU:1, one launch (start us, length us, event | category | flops | bytes accessed | tf_op | source)
XLA Modules:
  0.0 157.9 jit_solution(12409094260524010255)
XLA Ops:
  0.0 2.2 %pack.1 = f32[32,2,4,16,128]{4,3,2,1,0:T(8,128)S(1)} custom-call(bf16[512,512]{1,0:T(8,128)(2,1)} %key_ref.3, bf16[512,512]{1,0:T(8,128)(2,1)} %value_ref.3, f32[512,512]{1,0:T(8,128)} %taps_ref.1), custom_call_target="tpu_custom_call" | custom-call | tf_op jit(solution)/shard_map/pack/pallas_call | solution.py:104
  2.3 37.3 %all_to_all.10 = f32[32,2,4,16,128]{4,3,2,1,0:T(8,128)S(1)} all-to-all(f32[32,2,4,16,128]{4,3,2,1,0:T(8,128)S(1)} %pack.1), channel_id=1, replica_groups={{0,8,16,24,48,56,32,40,64,72,80,88,112,120,96,104,192,200,208,216,240,2..., dimensions={0} | all-to-all | bytes 4194304 | tf_op jit(solution)/shard_map/all_to_all | solution.py:34
  39.6 9.1 %convolve.1 = f32[2048,128]{1,0:T(8,128)} custom-call(f32[4096,128]{1,0:T(8,128)S(1)} %bitcast.31, bf16[256,384]{1,0:T(8,128)(2,1)S(1)} %copy-done.7, f32[128,128]{1,0:T(8,128)S(1)} %copy-done.9, f32[128,128]{1,0:T(8,128)S(1)} %copy-done.8, bf16[768,256]{1,0:T(8,128)(2,1)S(1)} %copy-done.5, bf16[768,256]{1,0:T(8,128)(2,1)S(1)} %copy-done.4, ...), custom_call_target="tpu_custom_call" | custom-call | flops 3623878656 | bytes 3145728 | tf_op jit(solution)/shard_map/convolve/pallas_call | solution.py:167
  48.7 3.7 %all-to-all-start.1 = ((f32[32,4,16,128]{3,2,1,0:T(8,128)}), f32[32,4,16,128]{3,2,1,0:T(8,128)S(1)}, u32[]{:S(2)}, u32[]{:S(2)}) async-start(f32[32,4,16,128]{3,2,1,0:T(8,128)} %bitcast.1), calls=%async_computation.1 | async-start | bytes 2097152 | tf_op jit(solution)/shard_map/all_to_all | solution.py:34
  52.6 4.2 %constant_dynamic-slice_fusion = (bf16[512,512]{1,0:T(8,128)(2,1)}, bf16[512,512]{1,0:T(8,128)(2,1)}, bf16[512,512]{1,0:T(8,128)(2,1)}, bf16[512,512]{1,0:T(8,12...) fusion(bf16[512,4096]{1,0:T(8,128)(2,1)} %param.17, ...), kind=kLoop, calls=%fused_computation.3 | loop fusion | bytes 8388640 | tf_op jit(solution)/shard_map/dynamic_slice | solution.py:230
  56.8 12.8 %all-to-all-done.1.conv_ref = f32[32,4,16,128]{3,2,1,0:T(8,128)S(1)} async-done(((f32[32,4,16,128]{3,2,1,0:T(8,128)}), f32[32,4,16,128]{3,2,1,0:T(8,128)S(1)}, u32[]{:S(2)}, u32[]{:S(2)}) %all-to-all-start.1) | async-done | bytes 1048608 | tf_op jit(solution)/shard_map/all_to_all | solution.py:34
  69.7 0.7 gate.1
  70.4 1.3 fusion
  71.7 0.3 fusion.6
  72.0 1.7 %collective-permute-start = (f32[256,512]{1,0:T(8,128)S(1)}, f32[256,512]{1,0:T(8,128)S(1)}, u32[]{:S(2)}, u32[]{:S(2)}) collective-permute-start(f32[256,512]{1,0:T(8,128)S(1)} %fusion.6), channel_id=1, source_target_pairs={{0,1},{1,2},{2,3},{3,4},{4,5},{5,6},{6,7},{7,0},{8,9},{9,10},{10,1... | collective-permute-start | bytes 1572872 | tf_op jit(solution)/shard_map/ppermute | solution.py:210
  73.7 0.3 fusion.4
  74.0 4.0 %collective-permute-start.10 = (f32[256,512]{1,0:T(8,128)S(1)}, f32[256,512]{1,0:T(8,128)S(1)}, u32[]{:S(2)}, u32[]{:S(2)}) collective-permute-start(f32[256,512]{1,0:T(8,128)S(1)} %fusion), channel_id=1, source_target_pairs={{0,7},{1,0},{2,1},{3,2},{4,3},{5,4},{6,5},{7,6},{8,15},{9,8},{10,9... | collective-permute-start | bytes 1572872 | tf_op jit(solution)/shard_map/ppermute | solution.py:210
  78.1 0.3 fusion.2
  78.4 0.1 collective-permute-start.7
  78.5 2.7 %collective-permute-start.4 = (f32[256,512]{1,0:T(8,128)S(1)}, f32[256,512]{1,0:T(8,128)S(1)}, u32[]{:S(2)}, u32[]{:S(2)}) collective-permute-start(f32[256,512]{1,0:T(8,128)S(1)} %fusion.4), channel_id=1, source_target_pairs={{0,7},{1,0},{2,1},{3,2},{4,3},{5,4},{6,5},{7,6},{8,15},{9,8},{10,9... | collective-permute-start | bytes 1572872 | tf_op jit(solution)/shard_map/ppermute | solution.py:210
  81.2 8.9 %collective-permute-done = f32[256,512]{1,0:T(8,128)S(1)} collective-permute-done((f32[256,512]{1,0:T(8,128)S(1)}, f32[256,512]{1,0:T(8,128)S(1)}, u32[]{:S(2)}, u32[]{:S(2)}) %collective-permute-start) | collective-permute-done | bytes 524320 | tf_op jit(solution)/shard_map/ppermute | solution.py:210
  90.2 0.3 fusion.9
  90.5 0.1 collective-permute-start.1
  90.6 0.3 fusion.16
  91.0 2.7 %collective-permute-start.11 = (f32[256,512]{1,0:T(8,128)S(1)}, f32[256,512]{1,0:T(8,128)S(1)}, u32[]{:S(2)}, u32[]{:S(2)}) collective-permute-start(f32[256,512]{1,0:T(8,128)S(1)} %add.144), channel_id=1, source_target_pairs={{0,7},{1,0},{2,1},{3,2},{4,3},{5,4},{6,5},{7,6},{8,15},{9,8},{10,9... | collective-permute-start | bytes 1572872 | tf_op jit(solution)/shard_map/ppermute | solution.py:210
  93.8 7.6 %collective-permute-done.7 = f32[256,512]{1,0:T(8,128)S(1)} collective-permute-done((f32[256,512]{1,0:T(8,128)S(1)}, f32[256,512]{1,0:T(8,128)S(1)}, u32[]{:S(2)}, u32[]{:S(2)}) %collective-permute-start.7) | collective-permute-done | bytes 524320 | tf_op jit(solution)/shard_map/ppermute | solution.py:210
  101.4 0.3 fusion.14
  101.7 0.1 add.142
  101.8 0.3 collective-permute-start.8
  102.1 0.3 fusion.12
  102.5 2.7 %collective-permute-start.5 = (f32[256,512]{1,0:T(8,128)S(1)}, f32[256,512]{1,0:T(8,128)S(1)}, u32[]{:S(2)}, u32[]{:S(2)}) collective-permute-start(f32[256,512]{1,0:T(8,128)S(1)} %add.138), channel_id=1, source_target_pairs={{0,7},{1,0},{2,1},{3,2},{4,3},{5,4},{6,5},{7,6},{8,15},{9,8},{10,9... | collective-permute-start | bytes 1572872 | tf_op jit(solution)/shard_map/ppermute | solution.py:210
  105.2 7.4 %collective-permute-done.1 = f32[256,512]{1,0:T(8,128)S(1)} collective-permute-done((f32[256,512]{1,0:T(8,128)S(1)}, f32[256,512]{1,0:T(8,128)S(1)}, u32[]{:S(2)}, u32[]{:S(2)}) %collective-permute-start.1) | collective-permute-done | bytes 524320 | tf_op jit(solution)/shard_map/ppermute | solution.py:210
  112.6 0.3 fusion.10
  113.0 0.1 collective-permute-start.2
  113.1 0.3 fusion.17
  113.4 0.1 add.145
  113.5 2.7 %collective-permute-start.12 = (f32[256,512]{1,0:T(8,128)S(1)}, f32[256,512]{1,0:T(8,128)S(1)}, u32[]{:S(2)}, u32[]{:S(2)}) collective-permute-start(f32[256,512]{1,0:T(8,128)S(1)} %add.145), channel_id=1, source_target_pairs={{0,7},{1,0},{2,1},{3,2},{4,3},{5,4},{6,5},{7,6},{8,15},{9,8},{10,9... | collective-permute-start | bytes 1572872 | tf_op jit(solution)/shard_map/ppermute | solution.py:210
  116.2 7.6 %collective-permute-done.8 = f32[256,512]{1,0:T(8,128)S(1)} collective-permute-done((f32[256,512]{1,0:T(8,128)S(1)}, f32[256,512]{1,0:T(8,128)S(1)}, u32[]{:S(2)}, u32[]{:S(2)}) %collective-permute-start.8) | collective-permute-done | bytes 524320 | tf_op jit(solution)/shard_map/ppermute | solution.py:210
  123.9 0.3 fusion.15
  124.2 0.1 add.143
  124.3 0.1 collective-permute-start.9
  124.4 0.3 fusion.13
  124.8 2.7 %collective-permute-start.6 = (f32[256,512]{1,0:T(8,128)S(1)}, f32[256,512]{1,0:T(8,128)S(1)}, u32[]{:S(2)}, u32[]{:S(2)}) collective-permute-start(f32[256,512]{1,0:T(8,128)S(1)} %add.139), channel_id=1, source_target_pairs={{0,7},{1,0},{2,1},{3,2},{4,3},{5,4},{6,5},{7,6},{8,15},{9,8},{10,9... | collective-permute-start | bytes 1572872 | tf_op jit(solution)/shard_map/ppermute | solution.py:210
  127.5 7.6 %collective-permute-done.2 = f32[256,512]{1,0:T(8,128)S(1)} collective-permute-done((f32[256,512]{1,0:T(8,128)S(1)}, f32[256,512]{1,0:T(8,128)S(1)}, u32[]{:S(2)}, u32[]{:S(2)}) %collective-permute-start.2) | collective-permute-done | bytes 524320 | tf_op jit(solution)/shard_map/ppermute | solution.py:210
  135.1 0.3 fusion.18
  135.5 3.1 %collective-permute-start.13 = (f32[256,512]{1,0:T(8,128)S(1)}, f32[256,512]{1,0:T(8,128)S(1)}, u32[]{:S(2)}, u32[]{:S(2)}) collective-permute-start(f32[256,512]{1,0:T(8,128)S(1)} %add.146), channel_id=1, source_target_pairs={{0,7},{1,0},{2,1},{3,2},{4,3},{5,4},{6,5},{7,6},{8,15},{9,8},{10,9... | collective-permute-start | bytes 1572872 | tf_op jit(solution)/shard_map/ppermute | solution.py:210
  138.6 0.3 fusion.11
  139.0 0.1 collective-permute-start.3
  139.1 7.2 %collective-permute-done.9 = f32[256,512]{1,0:T(8,128)S(1)} collective-permute-done((f32[256,512]{1,0:T(8,128)S(1)}, f32[256,512]{1,0:T(8,128)S(1)}, u32[]{:S(2)}, u32[]{:S(2)}) %collective-permute-start.9) | collective-permute-done | bytes 524320 | tf_op jit(solution)/shard_map/ppermute | solution.py:210
  146.3 10.1 %collective-permute-done.13 = f32[256,512]{1,0:T(8,128)S(1)} collective-permute-done((f32[256,512]{1,0:T(8,128)S(1)}, f32[256,512]{1,0:T(8,128)S(1)}, u32[]{:S(2)}, u32[]{:S(2)}) %collective-permute-start.13) | collective-permute-done | bytes 524320 | tf_op jit(solution)/shard_map/ppermute | solution.py:210
  156.4 0.3 add_convert_fusion
  156.8 0.3 add_convert_fusion.1
  157.1 0.8 pad_maximum_fusion
  (49 shorter events, 0.7 us)
Async XLA Ops:
  0.0 39.6 %copy-start.4 = (bf16[768,256]{1,0:T(8,128)(2,1)S(1)}, bf16[768,256]{1,0:T(8,128)(2,1)}, u32[]{:S(2)}) copy-start(bf16[768,256]{1,0:T(8,128)(2,1)} %constant.79.clone.refs_5_) | copy-start | bytes 1179652
  0.0 39.6 %copy-start.5 = (bf16[768,256]{1,0:T(8,128)(2,1)S(1)}, bf16[768,256]{1,0:T(8,128)(2,1)}, u32[]{:S(2)}) copy-start(bf16[768,256]{1,0:T(8,128)(2,1)} %constant.78.clone.refs_4_) | copy-start | bytes 1179652
  0.0 39.6 %copy-start.6 = (bf16[128,768]{1,0:T(8,128)(2,1)S(1)}, bf16[128,768]{1,0:T(8,128)(2,1)}, u32[]{:S(2)}) copy-start(bf16[128,768]{1,0:T(8,128)(2,1)} %constant.80.clone.refs_6_) | copy-start | bytes 589828
  0.0 39.6 %copy-start.7 = (bf16[256,384]{1,0:T(8,128)(2,1)S(1)}, bf16[256,384]{1,0:T(8,128)(2,1)}, u32[]{:S(2)}) copy-start(bf16[256,384]{1,0:T(8,128)(2,1)} %constant.77.clone.refs_1_) | copy-start | bytes 589828
  0.0 39.6 %copy-start.8 = (f32[128,128]{1,0:T(8,128)S(1)}, f32[128,128]{1,0:T(8,128)}, u32[]{:S(2)}) copy-start(f32[128,128]{1,0:T(8,128)} %constant.76.clone.refs_3_) | copy-start | bytes 196612
  0.0 39.6 %copy-start.9 = (f32[128,128]{1,0:T(8,128)S(1)}, f32[128,128]{1,0:T(8,128)}, u32[]{:S(2)}) copy-start(f32[128,128]{1,0:T(8,128)} %constant.75.clone.refs_2_) | copy-start | bytes 196612
  48.7 20.9 %all-to-all-start.1 = ((f32[32,4,16,128]{3,2,1,0:T(8,128)}), f32[32,4,16,128]{3,2,1,0:T(8,128)S(1)}, u32[]{:S(2)}, u32[]{:S(2)}) async-start(f32[32,4,16,128]{3,2,1,0:T(8,128)} %bitcast.1), calls=%async_computation.1 | async-start | bytes 2097152 | tf_op jit(solution)/shard_map/all_to_all | solution.py:34
  52.6 17.1 %copy-start = (bf16[512,512]{1,0:T(8,128)(2,1)S(1)}, bf16[512,512]{1,0:T(8,128)(2,1)}, u32[]{:S(2)}) copy-start(bf16[512,512]{1,0:T(8,128)(2,1)} %key_ref.3) | copy-start | bytes 1572868
  52.6 17.0 %copy-start.1 = (bf16[512,512]{1,0:T(8,128)(2,1)S(1)}, bf16[512,512]{1,0:T(8,128)(2,1)}, u32[]{:S(2)}) copy-start(bf16[512,512]{1,0:T(8,128)(2,1)} %value_ref.3) | copy-start | bytes 1572868
  52.6 17.0 %copy-start.2 = (bf16[512,512]{1,0:T(8,128)(2,1)S(1)}, bf16[512,512]{1,0:T(8,128)(2,1)}, u32[]{:S(2)}) copy-start(bf16[512,512]{1,0:T(8,128)(2,1)} %query_ref.1) | copy-start | bytes 1572868
  52.6 17.0 %copy-start.3 = (f32[512]{0:T(512)S(1)}, f32[512]{0:T(512)}, u32[]{:S(2)}) copy-start(f32[512]{0:T(512)} %param.16) | copy-start | bytes 6148
  69.6 2.1 %copy-start.15 = (bf16[512,512]{1,0:T(8,128)(2,1)S(1)}, bf16[512,512]{1,0:T(8,128)(2,1)}, u32[]{:S(2)}) copy-start(bf16[512,512]{1,0:T(8,128)(2,1)} %get-tuple-element.41) | copy-start | bytes 1572868
  69.6 4.1 %copy-start.13 = (bf16[512,512]{1,0:T(8,128)(2,1)S(1)}, bf16[512,512]{1,0:T(8,128)(2,1)}, u32[]{:S(2)}) copy-start(bf16[512,512]{1,0:T(8,128)(2,1)} %get-tuple-element.51) | copy-start | bytes 1572868
  69.6 8.5 %copy-start.14 = (bf16[512,512]{1,0:T(8,128)(2,1)S(1)}, bf16[512,512]{1,0:T(8,128)(2,1)}, u32[]{:S(2)}) copy-start(bf16[512,512]{1,0:T(8,128)(2,1)} %get-tuple-element.44) | copy-start | bytes 1572868
  72.0 18.1 %collective-permute-start = (f32[256,512]{1,0:T(8,128)S(1)}, f32[256,512]{1,0:T(8,128)S(1)}, u32[]{:S(2)}, u32[]{:S(2)}) collective-permute-start(f32[256,512]{1,0:T(8,128)S(1)} %fusion.6), channel_id=1, source_target_pairs={{0,1},{1,2},{2,3},{3,4},{4,5},{5,6},{6,7},{7,0},{8,9},{9,10},{10,1... | collective-permute-start | bytes 1572872 | tf_op jit(solution)/shard_map/ppermute | solution.py:210
  74.0 27.4 %copy-start.12 = (bf16[512,512]{1,0:T(8,128)(2,1)S(1)}, bf16[512,512]{1,0:T(8,128)(2,1)}, u32[]{:S(2)}) copy-start(bf16[512,512]{1,0:T(8,128)(2,1)} %get-tuple-element.47) | copy-start | bytes 1572868
  74.0 16.6 %collective-permute-start.10 = (f32[256,512]{1,0:T(8,128)S(1)}, f32[256,512]{1,0:T(8,128)S(1)}, u32[]{:S(2)}, u32[]{:S(2)}) collective-permute-start(f32[256,512]{1,0:T(8,128)S(1)} %fusion), channel_id=1, source_target_pairs={{0,7},{1,0},{2,1},{3,2},{4,3},{5,4},{6,5},{7,6},{8,15},{9,8},{10,9... | collective-permute-start | bytes 1572872 | tf_op jit(solution)/shard_map/ppermute | solution.py:210
  78.4 23.0 %collective-permute-start.7 = (f32[256,512]{1,0:T(8,128)S(1)}, f32[256,512]{1,0:T(8,128)S(1)}, u32[]{:S(2)}, u32[]{:S(2)}) collective-permute-start(f32[256,512]{1,0:T(8,128)S(1)} %fusion.2), channel_id=1, source_target_pairs={{0,1},{1,2},{2,3},{3,4},{4,5},{5,6},{6,7},{7,0},{8,9},{9,10},{10,1... | collective-permute-start | bytes 1572872 | tf_op jit(solution)/shard_map/ppermute | solution.py:210
  78.5 23.5 %collective-permute-start.4 = (f32[256,512]{1,0:T(8,128)S(1)}, f32[256,512]{1,0:T(8,128)S(1)}, u32[]{:S(2)}, u32[]{:S(2)}) collective-permute-start(f32[256,512]{1,0:T(8,128)S(1)} %fusion.4), channel_id=1, source_target_pairs={{0,7},{1,0},{2,1},{3,2},{4,3},{5,4},{6,5},{7,6},{8,15},{9,8},{10,9... | collective-permute-start | bytes 1572872 | tf_op jit(solution)/shard_map/ppermute | solution.py:210
  90.1 11.9 %copy-start.11 = (bf16[512,512]{1,0:T(8,128)(2,1)S(1)}, bf16[512,512]{1,0:T(8,128)(2,1)}, u32[]{:S(2)}) copy-start(bf16[512,512]{1,0:T(8,128)(2,1)} %get-tuple-element.54) | copy-start | bytes 1572868
  90.5 22.1 %collective-permute-start.1 = (f32[256,512]{1,0:T(8,128)S(1)}, f32[256,512]{1,0:T(8,128)S(1)}, u32[]{:S(2)}, u32[]{:S(2)}) collective-permute-start(f32[256,512]{1,0:T(8,128)S(1)} %add.135), channel_id=1, source_target_pairs={{0,1},{1,2},{2,3},{3,4},{4,5},{5,6},{6,7},{7,0},{8,9},{9,10},{10,1... | collective-permute-start | bytes 1572872 | tf_op jit(solution)/shard_map/ppermute | solution.py:210
  91.0 22.1 %collective-permute-start.11 = (f32[256,512]{1,0:T(8,128)S(1)}, f32[256,512]{1,0:T(8,128)S(1)}, u32[]{:S(2)}, u32[]{:S(2)}) collective-permute-start(f32[256,512]{1,0:T(8,128)S(1)} %add.144), channel_id=1, source_target_pairs={{0,7},{1,0},{2,1},{3,2},{4,3},{5,4},{6,5},{7,6},{8,15},{9,8},{10,9... | collective-permute-start | bytes 1572872 | tf_op jit(solution)/shard_map/ppermute | solution.py:210
  101.8 22.1 %collective-permute-start.8 = (f32[256,512]{1,0:T(8,128)S(1)}, f32[256,512]{1,0:T(8,128)S(1)}, u32[]{:S(2)}, u32[]{:S(2)}) collective-permute-start(f32[256,512]{1,0:T(8,128)S(1)} %add.142), channel_id=1, source_target_pairs={{0,1},{1,2},{2,3},{3,4},{4,5},{5,6},{6,7},{7,0},{8,9},{9,10},{10,1... | collective-permute-start | bytes 1572872 | tf_op jit(solution)/shard_map/ppermute | solution.py:210
  102.5 21.9 %copy-start.10 = (bf16[512,512]{1,0:T(8,128)(2,1)S(1)}, bf16[512,512]{1,0:T(8,128)(2,1)}, u32[]{:S(2)}) copy-start(bf16[512,512]{1,0:T(8,128)(2,1)} %get-tuple-element.57) | copy-start | bytes 1572868
  102.5 21.9 %collective-permute-start.5 = (f32[256,512]{1,0:T(8,128)S(1)}, f32[256,512]{1,0:T(8,128)S(1)}, u32[]{:S(2)}, u32[]{:S(2)}) collective-permute-start(f32[256,512]{1,0:T(8,128)S(1)} %add.138), channel_id=1, source_target_pairs={{0,7},{1,0},{2,1},{3,2},{4,3},{5,4},{6,5},{7,6},{8,15},{9,8},{10,9... | collective-permute-start | bytes 1572872 | tf_op jit(solution)/shard_map/ppermute | solution.py:210
  113.0 22.1 %collective-permute-start.2 = (f32[256,512]{1,0:T(8,128)S(1)}, f32[256,512]{1,0:T(8,128)S(1)}, u32[]{:S(2)}, u32[]{:S(2)}) collective-permute-start(f32[256,512]{1,0:T(8,128)S(1)} %add.136), channel_id=1, source_target_pairs={{0,1},{1,2},{2,3},{3,4},{4,5},{5,6},{6,7},{7,0},{8,9},{9,10},{10,1... | collective-permute-start | bytes 1572872 | tf_op jit(solution)/shard_map/ppermute | solution.py:210
  113.5 21.6 %collective-permute-start.12 = (f32[256,512]{1,0:T(8,128)S(1)}, f32[256,512]{1,0:T(8,128)S(1)}, u32[]{:S(2)}, u32[]{:S(2)}) collective-permute-start(f32[256,512]{1,0:T(8,128)S(1)} %add.145), channel_id=1, source_target_pairs={{0,7},{1,0},{2,1},{3,2},{4,3},{5,4},{6,5},{7,6},{8,15},{9,8},{10,9... | collective-permute-start | bytes 1572872 | tf_op jit(solution)/shard_map/ppermute | solution.py:210
  124.2 32.2 %copy-start.16 = (bf16[512,512]{1,0:T(8,128)(2,1)S(1)}, bf16[512,512]{1,0:T(8,128)(2,1)}, u32[]{:S(2)}) copy-start(bf16[512,512]{1,0:T(8,128)(2,1)} %get-tuple-element.61) | copy-start | bytes 1572868
  124.3 22.1 %collective-permute-start.9 = (f32[256,512]{1,0:T(8,128)S(1)}, f32[256,512]{1,0:T(8,128)S(1)}, u32[]{:S(2)}, u32[]{:S(2)}) collective-permute-start(f32[256,512]{1,0:T(8,128)S(1)} %add.143), channel_id=1, source_target_pairs={{0,1},{1,2},{2,3},{3,4},{4,5},{5,6},{6,7},{7,0},{8,9},{9,10},{10,1... | collective-permute-start | bytes 1572872 | tf_op jit(solution)/shard_map/ppermute | solution.py:210
  124.8 31.7 %collective-permute-start.6 = (f32[256,512]{1,0:T(8,128)S(1)}, f32[256,512]{1,0:T(8,128)S(1)}, u32[]{:S(2)}, u32[]{:S(2)}) collective-permute-start(f32[256,512]{1,0:T(8,128)S(1)} %add.139), channel_id=1, source_target_pairs={{0,7},{1,0},{2,1},{3,2},{4,3},{5,4},{6,5},{7,6},{8,15},{9,8},{10,9... | collective-permute-start | bytes 1572872 | tf_op jit(solution)/shard_map/ppermute | solution.py:210
  135.5 21.0 %collective-permute-start.13 = (f32[256,512]{1,0:T(8,128)S(1)}, f32[256,512]{1,0:T(8,128)S(1)}, u32[]{:S(2)}, u32[]{:S(2)}) collective-permute-start(f32[256,512]{1,0:T(8,128)S(1)} %add.146), channel_id=1, source_target_pairs={{0,7},{1,0},{2,1},{3,2},{4,3},{5,4},{6,5},{7,6},{8,15},{9,8},{10,9... | collective-permute-start | bytes 1572872 | tf_op jit(solution)/shard_map/ppermute | solution.py:210
  139.0 17.5 %collective-permute-start.3 = (f32[256,512]{1,0:T(8,128)S(1)}, f32[256,512]{1,0:T(8,128)S(1)}, u32[]{:S(2)}, u32[]{:S(2)}) collective-permute-start(f32[256,512]{1,0:T(8,128)S(1)} %add.137), channel_id=1, source_target_pairs={{0,1},{1,2},{2,3},{3,4},{4,5},{5,6},{6,7},{7,0},{8,9},{9,10},{10,1... | collective-permute-start | bytes 1572872 | tf_op jit(solution)/shard_map/ppermute | solution.py:210

commit v6 on v5

--- a/solution.py
+++ b/solution.py
@@ -12,7 +12,7 @@
 BF16 = jnp.bfloat16
 SMALL_VMEM = 16 * 1024 * 1024
 VMEM_BYTES = 24 * 1024 * 1024
-GROUP = 8
+GROUP = 16
 SIDE = 4
 CORES = 2
 
@@ -87,29 +87,39 @@
     return dot(jnp.concatenate([high, high, low], 1), table)
 
 
-def pack_kernel(key_ref, value_ref, taps_ref, out_ref):
+def pack_kernel(key_ref, value_ref, taps_ref, out_ref, key_vmem, value_vmem, taps_vmem, sems):
     parts, _, pieces, width, _ = out_ref.shape
-    for j in range(pieces):
-        at = slice(j * LANES, (j + 1) * LANES)
-        signal = key_ref[at].astype(F32) * value_ref[at].astype(F32)
+    pairs = ((key_ref, key_vmem), (value_ref, value_vmem), (taps_ref, taps_vmem))
+    rows = [pl.ds(j * LANES, LANES) for j in range(pieces)]
+    copies = [
+        [pltpu.make_async_copy(x.at[at], y.at[at], sems.at[k, j]) for k, (x, y) in enumerate(pairs)]
+        for j, at in enumerate(rows)
+    ]
+    for piece in copies:
+        for copy in piece:
+            copy.start()
+    for j, at in enumerate(rows):
+        for copy in copies[j]:
+            copy.wait()
+        signal = key_vmem[at].astype(F32) * value_vmem[at].astype(F32)
         out_ref[:, 0, j] = signal.T.reshape(parts, width, LANES)
-        out_ref[:, 1, j] = taps_ref[at].T.reshape(parts, width, LANES)
+        out_ref[:, 1, j] = taps_vmem[at].T.reshape(parts, width, LANES)
 
 
 def pack(key_in, value_in, filter_taps, n_parts):
     tok_rows, span = key_in.shape
     pieces = tok_rows // LANES
-    block = pl.BlockSpec((tok_rows, span), lambda i: (0, 0))
-    shape = (n_parts, 2, pieces, span // n_parts, LANES)
+    arrays = (key_in, value_in, filter_taps)
     return pl.pallas_call(
         pack_kernel,
-        grid=(1,),
-        in_specs=[block, block, block],
-        out_specs=pl.BlockSpec(shape, lambda i: (0, 0, 0, 0, 0)),
-        out_shape=jax.ShapeDtypeStruct(shape, F32),
+        in_specs=[pl.BlockSpec(memory_space=pltpu.HBM)] * 3,
+        out_specs=pl.BlockSpec(memory_space=pltpu.VMEM),
+        out_shape=jax.ShapeDtypeStruct((n_parts, 2, pieces, span // n_parts, LANES), F32),
+        scratch_shapes=[pltpu.VMEM(x.shape, x.dtype) for x in arrays]
+        + [pltpu.SemaphoreType.DMA((3, pieces))],
         compiler_params=pltpu.CompilerParams(vmem_limit_bytes=SMALL_VMEM),
         name="pack",
-    )(*(pltpu.with_memory_space_constraint(x, pltpu.HBM) for x in (key_in, value_in, filter_taps)))
+    )(*(pltpu.with_memory_space_constraint(x, pltpu.HBM) for x in arrays))
 
 
 def conv_kernel(n_parts, width, group, x_ref, first_ref, cos_ref, sin_ref, second_ref, back2_ref, back1_ref, out_ref):
@@ -202,6 +212,26 @@
     )(conv, query_in, key_in, value_in, skip_gain.reshape(1, channels))
 
 
+def columns_kernel(_, weight_ref, out_ref):
+    out_ref[...] = weight_ref[...]
+
+
+def columns(out_weight, device, out_cols):
+    rows = out_weight.shape[0]
+    return pl.pallas_call(
+        columns_kernel,
+        grid_spec=pltpu.PrefetchScalarGridSpec(
+            num_scalar_prefetch=1,
+            grid=(1,),
+            in_specs=[pl.BlockSpec((rows, out_cols), lambda i, at: (0, at[0]))],
+            out_specs=pl.BlockSpec((rows, out_cols), lambda i, at: (0, 0)),
+        ),
+        out_shape=jax.ShapeDtypeStruct((rows, out_cols), out_weight.dtype),
+        compiler_params=pltpu.CompilerParams(vmem_limit_bytes=SMALL_VMEM),
+        name="columns",
+    )(device.astype(jnp.int32).reshape(1), pltpu.with_memory_space_constraint(out_weight, pltpu.HBM))
+
+
 def ring_sum(gated, weights, way, start):
     n_chan = len(weights)
     hops = [(i, (i + way) % n_chan) for i in range(n_chan)]
@@ -230,6 +260,7 @@
         lax.dynamic_slice(out_weight, (0, (me + k) % n_chan * out_cols), (channels, out_cols))
         for k in range(n_chan)
     ]
+    weights[n_chan // 2] = columns(out_weight, (me + n_chan // 2) % n_chan, out_cols)
     conv = exchange(conv, n_parts)
     conv, weights = lax.optimization_barrier((conv, weights))
     gated = gate(conv, query_in, key_in, value_in, skip_gain)

time: 158 us -> 157 us (level)
    dynamic_slice x1, local copies, waits for them, and re-layouts: 4.16 us -> 1.9 us  [on_device(): lax.dynamic_slice(out_weight, (0, (me + k) % n_chan * out_cols), (channel...]
    pallas_call x1 -> x2, Pallas kernels: 2.23 us -> 3.34 us  [the longest x1 2.11 us: pack(): pl.pallas_call(pack_kernel, in_specs=[pl.BlockSpec(memory_space=pltpu.HBM...]
  transfers between devices with their start and end apart: 15 -> 15, of which waited for: 8 -> 8; matrix products, arithmetic and copies ran while one was open for 5% -> 4% of each run, Pallas kernels for 0% -> 1%
where the time goes in v6:
time: 157 us; the launch traced here: 156 us
  waiting for transfers between devices  69.3 us (44%)
  blocking collectives  37.3 us (24%)
  starting transfers between devices  26.9 us (17%)
  Pallas kernels  12.9 us (8%)
  matrix products  4.72 us (3%)
  local copies, waits for them, and re-layouts  3.13 us (2%)
  other arithmetic  1.66 us (1%)
    ppermute x14, waiting for transfers between devices, ring_sum(): got = lax.ppermute(total, 'chan', hops)  56.5 us
    all_to_all x1, blocking collectives, exchange(): lax.all_to_all(value, 'seq', split_axis=0, concat_axis=0, tiled=True, axi...  37.3 us
    ppermute x14, starting transfers between devices, ring_sum(): got = lax.ppermute(total, 'chan', hops)  23.2 us
    all_to_all x1, waiting for transfers between devices, exchange(): lax.all_to_all(value, 'seq', split_axis=0, concat_axis=0, tiled=True, axi...  12.8 us
    pallas_call x1, Pallas kernels, convolve(): pl.pallas_call(lambda *refs: conv_kernel(n_parts, width, group, *refs), o...  8.84 us
    dot_general x16, matrix products, dot(): return jnp.dot(left, right, preferred_element_type=F32)  4.72 us
    all_to_all x1, starting transfers between devices, exchange(): lax.all_to_all(value, 'seq', split_axis=0, concat_axis=0, tiled=True, axi...  3.72 us
  transfers between devices with their start and end apart: 15, of which 8 were waited for; matrix products, arithmetic and copies ran while one was open for 4% of the time, Pallas kernels for 1%

profile of v6, /device:TPU:1, one launch (start us, length us, event | category | flops | bytes accessed | tf_op | source)
XLA Modules:
  0.0 156.4 jit_solution(6697573657437455344)
XLA Ops:
  0.0 2.1 %pack.1 = f32[32,2,4,16,128]{4,3,2,1,0:T(8,128)S(1)} custom-call(bf16[512,512]{1,0:T(8,128)(2,1)} %key_ref.3, bf16[512,512]{1,0:T(8,128)(2,1)} %value_ref.3, f32[512,512]{1,0:T(8,128)} %taps_ref.1), custom_call_target="tpu_custom_call" | custom-call | tf_op jit(solution)/shard_map/pack/pallas_call | solution.py:113
  2.2 37.3 %all_to_all.10 = f32[32,2,4,16,128]{4,3,2,1,0:T(8,128)S(1)} all-to-all(f32[32,2,4,16,128]{4,3,2,1,0:T(8,128)S(1)} %pack.1), channel_id=1, replica_groups={{0,8,16,24,48,56,32,40,64,72,80,88,112,120,96,104,192,200,208,216,240,2..., dimensions={0} | all-to-all | bytes 4194304 | tf_op jit(solution)/shard_map/all_to_all | solution.py:34
  39.5 8.8 %convolve.1 = f32[2048,128]{1,0:T(8,128)} custom-call(f32[4096,128]{1,0:T(8,128)S(1)} %bitcast.32, bf16[256,384]{1,0:T(8,128)(2,1)S(1)} %copy-done.7, f32[128,128]{1,0:T(8,128)S(1)} %copy-done.9, f32[128,128]{1,0:T(8,128)S(1)} %copy-done.8, bf16[768,256]{1,0:T(8,128)(2,1)S(1)} %copy-done.5, bf16[768,256]{1,0:T(8,128)(2,1)S(1)} %copy-done.4, ...), custom_call_target="tpu_custom_call" | custom-call | flops 3623878656 | bytes 3145728 | tf_op jit(solution)/shard_map/convolve/pallas_call | solution.py:177
  48.3 3.7 %all-to-all-start.1 = ((f32[32,4,16,128]{3,2,1,0:T(8,128)}), f32[32,4,16,128]{3,2,1,0:T(8,128)S(1)}, u32[]{:S(2)}, u32[]{:S(2)}) async-start(f32[32,4,16,128]{3,2,1,0:T(8,128)} %bitcast.1), calls=%async_computation.1 | async-start | bytes 2097152 | tf_op jit(solution)/shard_map/all_to_all | solution.py:34
  52.2 1.2 columns.1
  53.4 1.1 copy-done.10
  54.5 1.9 %constant_dynamic-slice_fusion = (bf16[512,512]{1,0:T(8,128)(2,1)}, bf16[512,512]{1,0:T(8,128)(2,1)}, bf16[512,512]{1,0:T(8,128)(2,1)}, bf16[512,512]{1,0:T(8,12...) fusion(bf16[512,4096]{1,0:T(8,128)(2,1)S(1)} %copy-done.10, ...), kind=kLoop, calls=%fused_computation.3 | loop fusion | bytes 7340060 | tf_op jit(solution)/shard_map/dynamic_slice | solution.py:260
  56.4 12.8 %all-to-all-done.1.conv_ref = f32[32,4,16,128]{3,2,1,0:T(8,128)S(1)} async-done(((f32[32,4,16,128]{3,2,1,0:T(8,128)}), f32[32,4,16,128]{3,2,1,0:T(8,128)S(1)}, u32[]{:S(2)}, u32[]{:S(2)}) %all-to-all-start.1) | async-done | bytes 1048608 | tf_op jit(solution)/shard_map/all_to_all | solution.py:34
  69.2 0.7 gate.1
  69.9 0.3 fusion
  70.2 0.3 fusion.6
  70.5 1.7 %collective-permute-start = (f32[256,512]{1,0:T(8,128)S(1)}, f32[256,512]{1,0:T(8,128)S(1)}, u32[]{:S(2)}, u32[]{:S(2)}) collective-permute-start(f32[256,512]{1,0:T(8,128)S(1)} %fusion.6), channel_id=1, source_target_pairs={{0,1},{1,2},{2,3},{3,4},{4,5},{5,6},{6,7},{7,0},{8,9},{9,10},{10,1... | collective-permute-start | bytes 1572872 | tf_op jit(solution)/shard_map/ppermute | solution.py:240
  72.3 0.3 fusion.4
  72.6 4.0 %collective-permute-start.10 = (f32[256,512]{1,0:T(8,128)S(1)}, f32[256,512]{1,0:T(8,128)S(1)}, u32[]{:S(2)}, u32[]{:S(2)}) collective-permute-start(f32[256,512]{1,0:T(8,128)S(1)} %fusion), channel_id=1, source_target_pairs={{0,7},{1,0},{2,1},{3,2},{4,3},{5,4},{6,5},{7,6},{8,15},{9,8},{10,9... | collective-permute-start | bytes 1572872 | tf_op jit(solution)/shard_map/ppermute | solution.py:240
  76.6 0.3 fusion.2
  76.9 0.3 collective-permute-start.7
  77.2 2.7 %collective-permute-start.4 = (f32[256,512]{1,0:T(8,128)S(1)}, f32[256,512]{1,0:T(8,128)S(1)}, u32[]{:S(2)}, u32[]{:S(2)}) collective-permute-start(f32[256,512]{1,0:T(8,128)S(1)} %fusion.4), channel_id=1, source_target_pairs={{0,7},{1,0},{2,1},{3,2},{4,3},{5,4},{6,5},{7,6},{8,15},{9,8},{10,9... | collective-permute-start | bytes 1572872 | tf_op jit(solution)/shard_map/ppermute | solution.py:240
  80.0 8.7 %collective-permute-done = f32[256,512]{1,0:T(8,128)S(1)} collective-permute-done((f32[256,512]{1,0:T(8,128)S(1)}, f32[256,512]{1,0:T(8,128)S(1)}, u32[]{:S(2)}, u32[]{:S(2)}) %collective-permute-start) | collective-permute-done | bytes 524320 | tf_op jit(solution)/shard_map/ppermute | solution.py:240
  88.7 0.3 fusion.9
  89.1 0.1 collective-permute-start.1
  89.2 0.3 fusion.16
  89.5 0.1 add.140
  89.6 2.7 %collective-permute-start.11 = (f32[256,512]{1,0:T(8,128)S(1)}, f32[256,512]{1,0:T(8,128)S(1)}, u32[]{:S(2)}, u32[]{:S(2)}) collective-permute-start(f32[256,512]{1,0:T(8,128)S(1)} %add.140), channel_id=1, source_target_pairs={{0,7},{1,0},{2,1},{3,2},{4,3},{5,4},{6,5},{7,6},{8,15},{9,8},{10,9... | collective-permute-start | bytes 1572872 | tf_op jit(solution)/shard_map/ppermute | solution.py:240
  92.3 7.6 %collective-permute-done.7 = f32[256,512]{1,0:T(8,128)S(1)} collective-permute-done((f32[256,512]{1,0:T(8,128)S(1)}, f32[256,512]{1,0:T(8,128)S(1)}, u32[]{:S(2)}, u32[]{:S(2)}) %collective-permute-start.7) | collective-permute-done | bytes 524320 | tf_op jit(solution)/shard_map/ppermute | solution.py:240
  99.9 0.3 fusion.14
  100.3 0.1 collective-permute-start.8
  100.4 0.3 fusion.12
  100.8 2.7 %collective-permute-start.5 = (f32[256,512]{1,0:T(8,128)S(1)}, f32[256,512]{1,0:T(8,128)S(1)}, u32[]{:S(2)}, u32[]{:S(2)}) collective-permute-start(f32[256,512]{1,0:T(8,128)S(1)} %add.134), channel_id=1, source_target_pairs={{0,7},{1,0},{2,1},{3,2},{4,3},{5,4},{6,5},{7,6},{8,15},{9,8},{10,9... | collective-permute-start | bytes 1572872 | tf_op jit(solution)/shard_map/ppermute | solution.py:240
  103.6 7.6 %collective-permute-done.1 = f32[256,512]{1,0:T(8,128)S(1)} collective-permute-done((f32[256,512]{1,0:T(8,128)S(1)}, f32[256,512]{1,0:T(8,128)S(1)}, u32[]{:S(2)}, u32[]{:S(2)}) %collective-permute-start.1) | collective-permute-done | bytes 524320 | tf_op jit(solution)/shard_map/ppermute | solution.py:240
  111.2 0.3 fusion.10
  111.6 0.3 fusion.17
  112.0 2.7 %collective-permute-start.12 = (f32[256,512]{1,0:T(8,128)S(1)}, f32[256,512]{1,0:T(8,128)S(1)}, u32[]{:S(2)}, u32[]{:S(2)}) collective-permute-start(f32[256,512]{1,0:T(8,128)S(1)} %add.141), channel_id=1, source_target_pairs={{0,7},{1,0},{2,1},{3,2},{4,3},{5,4},{6,5},{7,6},{8,15},{9,8},{10,9... | collective-permute-start | bytes 1572872 | tf_op jit(solution)/shard_map/ppermute | solution.py:240
  114.8 7.6 %collective-permute-done.8 = f32[256,512]{1,0:T(8,128)S(1)} collective-permute-done((f32[256,512]{1,0:T(8,128)S(1)}, f32[256,512]{1,0:T(8,128)S(1)}, u32[]{:S(2)}, u32[]{:S(2)}) %collective-permute-start.8) | collective-permute-done | bytes 524320 | tf_op jit(solution)/shard_map/ppermute | solution.py:240
  122.4 0.3 fusion.15
  122.7 0.1 add.139
  122.9 0.3 fusion.13
  123.2 0.1 add.135
  123.3 2.7 %collective-permute-start.6 = (f32[256,512]{1,0:T(8,128)S(1)}, f32[256,512]{1,0:T(8,128)S(1)}, u32[]{:S(2)}, u32[]{:S(2)}) collective-permute-start(f32[256,512]{1,0:T(8,128)S(1)} %add.135), channel_id=1, source_target_pairs={{0,7},{1,0},{2,1},{3,2},{4,3},{5,4},{6,5},{7,6},{8,15},{9,8},{10,9... | collective-permute-start | bytes 1572872 | tf_op jit(solution)/shard_map/ppermute | solution.py:240
  126.0 7.6 %collective-permute-done.2 = f32[256,512]{1,0:T(8,128)S(1)} collective-permute-done((f32[256,512]{1,0:T(8,128)S(1)}, f32[256,512]{1,0:T(8,128)S(1)}, u32[]{:S(2)}, u32[]{:S(2)}) %collective-permute-start.2) | collective-permute-done | bytes 524320 | tf_op jit(solution)/shard_map/ppermute | solution.py:240
  133.6 0.3 fusion.18
  133.9 0.1 add.142
  134.0 3.1 %collective-permute-start.13 = (f32[256,512]{1,0:T(8,128)S(1)}, f32[256,512]{1,0:T(8,128)S(1)}, u32[]{:S(2)}, u32[]{:S(2)}) collective-permute-start(f32[256,512]{1,0:T(8,128)S(1)} %add.142), channel_id=1, source_target_pairs={{0,7},{1,0},{2,1},{3,2},{4,3},{5,4},{6,5},{7,6},{8,15},{9,8},{10,9... | collective-permute-start | bytes 1572872 | tf_op jit(solution)/shard_map/ppermute | solution.py:240
  137.1 0.3 fusion.11
  137.6 7.2 %collective-permute-done.9 = f32[256,512]{1,0:T(8,128)S(1)} collective-permute-done((f32[256,512]{1,0:T(8,128)S(1)}, f32[256,512]{1,0:T(8,128)S(1)}, u32[]{:S(2)}, u32[]{:S(2)}) %collective-permute-start.9) | collective-permute-done | bytes 524320 | tf_op jit(solution)/shard_map/ppermute | solution.py:240
  144.9 10.1 %collective-permute-done.13 = f32[256,512]{1,0:T(8,128)S(1)} collective-permute-done((f32[256,512]{1,0:T(8,128)S(1)}, f32[256,512]{1,0:T(8,128)S(1)}, u32[]{:S(2)}, u32[]{:S(2)}) %collective-permute-start.13) | collective-permute-done | bytes 524320 | tf_op jit(solution)/shard_map/ppermute | solution.py:240
  155.0 0.3 add_convert_fusion
  155.3 0.3 add_convert_fusion.1
  155.6 0.8 pad_maximum_fusion
  (52 shorter events, 0.9 us)
Async XLA Ops:
  0.0 39.4 %copy-start.4 = (bf16[768,256]{1,0:T(8,128)(2,1)S(1)}, bf16[768,256]{1,0:T(8,128)(2,1)}, u32[]{:S(2)}) copy-start(bf16[768,256]{1,0:T(8,128)(2,1)} %constant.79.clone.refs_5_) | copy-start | bytes 1179652
  0.0 39.4 %copy-start.5 = (bf16[768,256]{1,0:T(8,128)(2,1)S(1)}, bf16[768,256]{1,0:T(8,128)(2,1)}, u32[]{:S(2)}) copy-start(bf16[768,256]{1,0:T(8,128)(2,1)} %constant.78.clone.refs_4_) | copy-start | bytes 1179652
  0.0 39.4 %copy-start.6 = (bf16[128,768]{1,0:T(8,128)(2,1)S(1)}, bf16[128,768]{1,0:T(8,128)(2,1)}, u32[]{:S(2)}) copy-start(bf16[128,768]{1,0:T(8,128)(2,1)} %constant.80.clone.refs_6_) | copy-start | bytes 589828
  0.0 39.5 %copy-start.7 = (bf16[256,384]{1,0:T(8,128)(2,1)S(1)}, bf16[256,384]{1,0:T(8,128)(2,1)}, u32[]{:S(2)}) copy-start(bf16[256,384]{1,0:T(8,128)(2,1)} %constant.77.clone.refs_1_) | copy-start | bytes 589828
  0.0 39.4 %copy-start.8 = (f32[128,128]{1,0:T(8,128)S(1)}, f32[128,128]{1,0:T(8,128)}, u32[]{:S(2)}) copy-start(f32[128,128]{1,0:T(8,128)} %constant.76.clone.refs_3_) | copy-start | bytes 196612
  0.0 39.4 %copy-start.9 = (f32[128,128]{1,0:T(8,128)S(1)}, f32[128,128]{1,0:T(8,128)}, u32[]{:S(2)}) copy-start(f32[128,128]{1,0:T(8,128)} %constant.75.clone.refs_2_) | copy-start | bytes 196612
  48.3 20.9 %all-to-all-start.1 = ((f32[32,4,16,128]{3,2,1,0:T(8,128)}), f32[32,4,16,128]{3,2,1,0:T(8,128)S(1)}, u32[]{:S(2)}, u32[]{:S(2)}) async-start(f32[32,4,16,128]{3,2,1,0:T(8,128)} %bitcast.1), calls=%async_computation.1 | async-start | bytes 2097152 | tf_op jit(solution)/shard_map/all_to_all | solution.py:34
  52.2 2.4 %copy-start.10 = (bf16[512,4096]{1,0:T(8,128)(2,1)S(1)}, bf16[512,4096]{1,0:T(8,128)(2,1)}, u32[]{:S(2)}) copy-start(bf16[512,4096]{1,0:T(8,128)(2,1)} %weight_ref.1) | copy-start | bytes 12582916
  54.5 14.7 %copy-start = (bf16[512,512]{1,0:T(8,128)(2,1)S(1)}, bf16[512,512]{1,0:T(8,128)(2,1)}, u32[]{:S(2)}) copy-start(bf16[512,512]{1,0:T(8,128)(2,1)} %key_ref.3) | copy-start | bytes 1572868
  54.5 14.7 %copy-start.1 = (bf16[512,512]{1,0:T(8,128)(2,1)S(1)}, bf16[512,512]{1,0:T(8,128)(2,1)}, u32[]{:S(2)}) copy-start(bf16[512,512]{1,0:T(8,128)(2,1)} %value_ref.3) | copy-start | bytes 1572868
  54.5 14.7 %copy-start.2 = (bf16[512,512]{1,0:T(8,128)(2,1)S(1)}, bf16[512,512]{1,0:T(8,128)(2,1)}, u32[]{:S(2)}) copy-start(bf16[512,512]{1,0:T(8,128)(2,1)} %query_ref.1) | copy-start | bytes 1572868
  54.5 14.7 %copy-start.3 = (f32[512]{0:T(512)S(1)}, f32[512]{0:T(512)}, u32[]{:S(2)}) copy-start(f32[512]{0:T(512)} %param.16) | copy-start | bytes 6148
  69.2 3.1 %copy-start.15 = (bf16[512,512]{1,0:T(8,128)(2,1)S(1)}, bf16[512,512]{1,0:T(8,128)(2,1)}, u32[]{:S(2)}) copy-start(bf16[512,512]{1,0:T(8,128)(2,1)} %get-tuple-element.51) | copy-start | bytes 1572868
  69.2 7.4 %copy-start.16 = (bf16[512,512]{1,0:T(8,128)(2,1)S(1)}, bf16[512,512]{1,0:T(8,128)(2,1)}, u32[]{:S(2)}) copy-start(bf16[512,512]{1,0:T(8,128)(2,1)} %get-tuple-element.44) | copy-start | bytes 1572868
  70.5 18.1 %collective-permute-start = (f32[256,512]{1,0:T(8,128)S(1)}, f32[256,512]{1,0:T(8,128)S(1)}, u32[]{:S(2)}, u32[]{:S(2)}) collective-permute-start(f32[256,512]{1,0:T(8,128)S(1)} %fusion.6), channel_id=1, source_target_pairs={{0,1},{1,2},{2,3},{3,4},{4,5},{5,6},{6,7},{7,0},{8,9},{9,10},{10,1... | collective-permute-start | bytes 1572872 | tf_op jit(solution)/shard_map/ppermute | solution.py:240
  72.6 27.4 %copy-start.14 = (bf16[512,512]{1,0:T(8,128)(2,1)S(1)}, bf16[512,512]{1,0:T(8,128)(2,1)}, u32[]{:S(2)}) copy-start(bf16[512,512]{1,0:T(8,128)(2,1)} %get-tuple-element.47) | copy-start | bytes 1572868
  72.6 16.6 %collective-permute-start.10 = (f32[256,512]{1,0:T(8,128)S(1)}, f32[256,512]{1,0:T(8,128)S(1)}, u32[]{:S(2)}, u32[]{:S(2)}) collective-permute-start(f32[256,512]{1,0:T(8,128)S(1)} %fusion), channel_id=1, source_target_pairs={{0,7},{1,0},{2,1},{3,2},{4,3},{5,4},{6,5},{7,6},{8,15},{9,8},{10,9... | collective-permute-start | bytes 1572872 | tf_op jit(solution)/shard_map/ppermute | solution.py:240
  76.9 23.0 %collective-permute-start.7 = (f32[256,512]{1,0:T(8,128)S(1)}, f32[256,512]{1,0:T(8,128)S(1)}, u32[]{:S(2)}, u32[]{:S(2)}) collective-permute-start(f32[256,512]{1,0:T(8,128)S(1)} %fusion.2), channel_id=1, source_target_pairs={{0,1},{1,2},{2,3},{3,4},{4,5},{5,6},{6,7},{7,0},{8,9},{9,10},{10,1... | collective-permute-start | bytes 1572872 | tf_op jit(solution)/shard_map/ppermute | solution.py:240
  77.2 23.2 %collective-permute-start.4 = (f32[256,512]{1,0:T(8,128)S(1)}, f32[256,512]{1,0:T(8,128)S(1)}, u32[]{:S(2)}, u32[]{:S(2)}) collective-permute-start(f32[256,512]{1,0:T(8,128)S(1)} %fusion.4), channel_id=1, source_target_pairs={{0,7},{1,0},{2,1},{3,2},{4,3},{5,4},{6,5},{7,6},{8,15},{9,8},{10,9... | collective-permute-start | bytes 1572872 | tf_op jit(solution)/shard_map/ppermute | solution.py:240
  88.7 11.7 %copy-start.13 = (bf16[512,512]{1,0:T(8,128)(2,1)S(1)}, bf16[512,512]{1,0:T(8,128)(2,1)}, u32[]{:S(2)}) copy-start(bf16[512,512]{1,0:T(8,128)(2,1)} %get-tuple-element.54) | copy-start | bytes 1572868
  89.1 22.1 %collective-permute-start.1 = (f32[256,512]{1,0:T(8,128)S(1)}, f32[256,512]{1,0:T(8,128)S(1)}, u32[]{:S(2)}, u32[]{:S(2)}) collective-permute-start(f32[256,512]{1,0:T(8,128)S(1)} %add.131), channel_id=1, source_target_pairs={{0,1},{1,2},{2,3},{3,4},{4,5},{5,6},{6,7},{7,0},{8,9},{9,10},{10,1... | collective-permute-start | bytes 1572872 | tf_op jit(solution)/shard_map/ppermute | solution.py:240
  89.6 22.1 %collective-permute-start.11 = (f32[256,512]{1,0:T(8,128)S(1)}, f32[256,512]{1,0:T(8,128)S(1)}, u32[]{:S(2)}, u32[]{:S(2)}) collective-permute-start(f32[256,512]{1,0:T(8,128)S(1)} %add.140), channel_id=1, source_target_pairs={{0,7},{1,0},{2,1},{3,2},{4,3},{5,4},{6,5},{7,6},{8,15},{9,8},{10,9... | collective-permute-start | bytes 1572872 | tf_op jit(solution)/shard_map/ppermute | solution.py:240
  100.3 22.1 %copy-start.11 = (bf16[512,512]{1,0:T(8,128)(2,1)S(1)}, bf16[512,512]{1,0:T(8,128)(2,1)}, u32[]{:S(2)}) copy-start(bf16[512,512]{1,0:T(8,128)(2,1)} %get-tuple-element.50) | copy-start | bytes 1572868
  100.3 22.1 %collective-permute-start.8 = (f32[256,512]{1,0:T(8,128)S(1)}, f32[256,512]{1,0:T(8,128)S(1)}, u32[]{:S(2)}, u32[]{:S(2)}) collective-permute-start(f32[256,512]{1,0:T(8,128)S(1)} %add.138), channel_id=1, source_target_pairs={{0,1},{1,2},{2,3},{3,4},{4,5},{5,6},{6,7},{7,0},{8,9},{9,10},{10,1... | collective-permute-start | bytes 1572872 | tf_op jit(solution)/shard_map/ppermute | solution.py:240
  100.8 22.1 %copy-start.12 = (bf16[512,512]{1,0:T(8,128)(2,1)S(1)}, bf16[512,512]{1,0:T(8,128)(2,1)}, u32[]{:S(2)}) copy-start(bf16[512,512]{1,0:T(8,128)(2,1)} %get-tuple-element.57) | copy-start | bytes 1572868
  100.8 22.1 %collective-permute-start.5 = (f32[256,512]{1,0:T(8,128)S(1)}, f32[256,512]{1,0:T(8,128)S(1)}, u32[]{:S(2)}, u32[]{:S(2)}) collective-permute-start(f32[256,512]{1,0:T(8,128)S(1)} %add.134), channel_id=1, source_target_pairs={{0,7},{1,0},{2,1},{3,2},{4,3},{5,4},{6,5},{7,6},{8,15},{9,8},{10,9... | collective-permute-start | bytes 1572872 | tf_op jit(solution)/shard_map/ppermute | solution.py:240
  111.5 22.1 %collective-permute-start.2 = (f32[256,512]{1,0:T(8,128)S(1)}, f32[256,512]{1,0:T(8,128)S(1)}, u32[]{:S(2)}, u32[]{:S(2)}) collective-permute-start(f32[256,512]{1,0:T(8,128)S(1)} %add.132), channel_id=1, source_target_pairs={{0,1},{1,2},{2,3},{3,4},{4,5},{5,6},{6,7},{7,0},{8,9},{9,10},{10,1... | collective-permute-start | bytes 1572872 | tf_op jit(solution)/shard_map/ppermute | solution.py:240
  112.0 21.6 %collective-permute-start.12 = (f32[256,512]{1,0:T(8,128)S(1)}, f32[256,512]{1,0:T(8,128)S(1)}, u32[]{:S(2)}, u32[]{:S(2)}) collective-permute-start(f32[256,512]{1,0:T(8,128)S(1)} %add.141), channel_id=1, source_target_pairs={{0,7},{1,0},{2,1},{3,2},{4,3},{5,4},{6,5},{7,6},{8,15},{9,8},{10,9... | collective-permute-start | bytes 1572872 | tf_op jit(solution)/shard_map/ppermute | solution.py:240
  122.8 32.2 %copy-start.17 = (bf16[512,512]{1,0:T(8,128)(2,1)S(1)}, bf16[512,512]{1,0:T(8,128)(2,1)}, u32[]{:S(2)}) copy-start(bf16[512,512]{1,0:T(8,128)(2,1)} %get-tuple-element.61) | copy-start | bytes 1572868
  122.8 22.1 %collective-permute-start.9 = (f32[256,512]{1,0:T(8,128)S(1)}, f32[256,512]{1,0:T(8,128)S(1)}, u32[]{:S(2)}, u32[]{:S(2)}) collective-permute-start(f32[256,512]{1,0:T(8,128)S(1)} %add.139), channel_id=1, source_target_pairs={{0,1},{1,2},{2,3},{3,4},{4,5},{5,6},{6,7},{7,0},{8,9},{9,10},{10,1... | collective-permute-start | bytes 1572872 | tf_op jit(solution)/shard_map/ppermute | solution.py:240
  123.3 31.7 %collective-permute-start.6 = (f32[256,512]{1,0:T(8,128)S(1)}, f32[256,512]{1,0:T(8,128)S(1)}, u32[]{:S(2)}, u32[]{:S(2)}) collective-permute-start(f32[256,512]{1,0:T(8,128)S(1)} %add.135), channel_id=1, source_target_pairs={{0,7},{1,0},{2,1},{3,2},{4,3},{5,4},{6,5},{7,6},{8,15},{9,8},{10,9... | collective-permute-start | bytes 1572872 | tf_op jit(solution)/shard_map/ppermute | solution.py:240
  134.0 21.0 %collective-permute-start.13 = (f32[256,512]{1,0:T(8,128)S(1)}, f32[256,512]{1,0:T(8,128)S(1)}, u32[]{:S(2)}, u32[]{:S(2)}) collective-permute-start(f32[256,512]{1,0:T(8,128)S(1)} %add.142), channel_id=1, source_target_pairs={{0,7},{1,0},{2,1},{3,2},{4,3},{5,4},{6,5},{7,6},{8,15},{9,8},{10,9... | collective-permute-start | bytes 1572872 | tf_op jit(solution)/shard_map/ppermute | solution.py:240
  137.5 17.5 %collective-permute-start.3 = (f32[256,512]{1,0:T(8,128)S(1)}, f32[256,512]{1,0:T(8,128)S(1)}, u32[]{:S(2)}, u32[]{:S(2)}) collective-permute-start(f32[256,512]{1,0:T(8,128)S(1)} %add.133), channel_id=1, source_target_pairs={{0,1},{1,2},{2,3},{3,4},{4,5},{5,6},{6,7},{7,0},{8,9},{9,10},{10,1... | collective-permute-start | bytes 1572872 | tf_op jit(solution)/shard_map/ppermute | solution.py:240

commit v7 on v6

--- a/solution.py
+++ b/solution.py
@@ -157,12 +157,10 @@
             from_left(first_ref[...], jnp.concatenate([column(0, c), column(1, c)], 1))
             for c in channels
         ]
-        turned = [spectrum(c, lane) for c in coarse for lane in (0, LANES)]
-        full = from_right(jnp.concatenate(turned, 0), second_ref[...])
-        products = [product(full[2 * k * LANES : 2 * (k + 1) * LANES]) for k in range(group)]
-        back = from_right(jnp.concatenate(products, 0), back2_ref[...])
-        columns = [unturn(back[k * LANES : (k + 1) * LANES]) for k in range(group)]
-        result = from_left(back1_ref[...], jnp.concatenate(columns, 1))
+        turned = [jnp.concatenate([spectrum(c, lane) for lane in (0, LANES)], 0) for c in coarse]
+        full = [from_right(t, second_ref[...]) for t in turned]
+        back = [from_right(product(f), back2_ref[...]) for f in full]
+        result = from_left(back1_ref[...], jnp.concatenate([unturn(b) for b in back], 1))
         for k, channel in enumerate(channels):
             for j in range(pieces):
                 out_ref[pl.ds(j * width + channel, n_parts, stride=rows), :] = result[
@@ -184,32 +182,25 @@
 
 
 def gate_kernel(conv_ref, query_ref, key_ref, value_ref, gain_ref, out_ref):
-    parts, _, width, _ = conv_ref.shape
-    conv = conv_ref[:, 0].reshape(parts * width, LANES).T
-    signal = key_ref[...].astype(F32) * value_ref[...].astype(F32)
-    response = conv + gain_ref[...] * signal
-    out_ref[...] = (query_ref[...].astype(F32) * response).astype(BF16)
+    parts, pieces, width, _ = conv_ref.shape
+    for j in range(pieces):
+        at = slice(j * LANES, (j + 1) * LANES)
+        conv = conv_ref[:, j].reshape(parts * width, LANES).T
+        signal = key_ref[at].astype(F32) * value_ref[at].astype(F32)
+        response = conv + gain_ref[...] * signal
+        out_ref[at] = (query_ref[at].astype(F32) * response).astype(BF16)
 
 
 def gate(conv, query_in, key_in, value_in, skip_gain):
-    n_parts, pieces, width, _ = conv.shape
-    channels = query_in.shape[1]
-    block = pl.BlockSpec((LANES, channels), lambda j: (j, 0))
+    whole = pl.BlockSpec(memory_space=pltpu.VMEM)
     return pl.pallas_call(
         gate_kernel,
-        grid=(pieces,),
-        in_specs=[
-            pl.BlockSpec((n_parts, 1, width, LANES), lambda j: (0, j, 0, 0)),
-            block,
-            block,
-            block,
-            pl.BlockSpec((1, channels), lambda j: (0, 0)),
-        ],
-        out_specs=pl.BlockSpec((LANES, channels), lambda j: (j, 0)),
-        out_shape=jax.ShapeDtypeStruct((pieces * LANES, channels), BF16),
+        in_specs=[whole] * 5,
+        out_specs=whole,
+        out_shape=jax.ShapeDtypeStruct(query_in.shape, BF16),
         compiler_params=pltpu.CompilerParams(vmem_limit_bytes=SMALL_VMEM),
         name="gate",
-    )(conv, query_in, key_in, value_in, skip_gain.reshape(1, channels))
+    )(conv, query_in, key_in, value_in, skip_gain.reshape(1, query_in.shape[1]))
 
 
 def columns_kernel(_, weight_ref, out_ref):

time: 157 us -> 154 us (0.981)
  Pallas kernels: 12.9 us -> 10.6 us
    pallas_call x1, Pallas kernels: 8.84 us -> 6.9 us  [convolve(): pl.pallas_call(lambda *refs: conv_kernel(n_parts, width, group, *refs), o...]
where the time goes in v7:
time: 154 us
  waiting for transfers between devices  69.3 us (45%)
  blocking collectives  37.3 us (24%)
  starting transfers between devices  26.9 us (17%)
  Pallas kernels  10.6 us (7%)
  matrix products  4.72 us (3%)
  local copies, waits for them, and re-layouts  3.13 us (2%)
  other arithmetic  1.66 us (1%)
    ppermute x14, waiting for transfers between devices, ring_sum(): got = lax.ppermute(total, 'chan', hops)  56.5 us
    all_to_all x1, blocking collectives, exchange(): lax.all_to_all(value, 'seq', split_axis=0, concat_axis=0, tiled=True, axi...  37.3 us
    ppermute x14, starting transfers between devices, ring_sum(): got = lax.ppermute(total, 'chan', hops)  23.2 us
    all_to_all x1, waiting for transfers between devices, exchange(): lax.all_to_all(value, 'seq', split_axis=0, concat_axis=0, tiled=True, axi...  12.8 us
    pallas_call x1, Pallas kernels, convolve(): pl.pallas_call(lambda *refs: conv_kernel(n_parts, width, group, *refs), o...  6.9 us
    dot_general x16, matrix products, dot(): return jnp.dot(left, right, preferred_element_type=F32)  4.72 us
    all_to_all x1, starting transfers between devices, exchange(): lax.all_to_all(value, 'seq', split_axis=0, concat_axis=0, tiled=True, axi...  3.72 us
  transfers between devices with their start and end apart: 15, of which 8 were waited for; matrix products, arithmetic and copies ran while one was open for 4% of the time, Pallas kernels for 1%

profile of v7, /device:TPU:1, one launch (start us, length us, event | category | flops | bytes accessed | tf_op | source)
XLA Modules:
  0.0 154.1 jit_solution(9512793431551542726)
XLA Ops:
  0.0 2.1 %pack.1 = f32[32,2,4,16,128]{4,3,2,1,0:T(8,128)S(1)} custom-call(bf16[512,512]{1,0:T(8,128)(2,1)} %key_ref.3, bf16[512,512]{1,0:T(8,128)(2,1)} %value_ref.3, f32[512,512]{1,0:T(8,128)} %taps_ref.1), custom_call_target="tpu_custom_call" | custom-call | tf_op jit(solution)/shard_map/pack/pallas_call | solution.py:113
  2.2 37.3 %all_to_all.10 = f32[32,2,4,16,128]{4,3,2,1,0:T(8,128)S(1)} all-to-all(f32[32,2,4,16,128]{4,3,2,1,0:T(8,128)S(1)} %pack.1), channel_id=1, replica_groups={{0,8,16,24,48,56,32,40,64,72,80,88,112,120,96,104,192,200,208,216,240,2..., dimensions={0} | all-to-all | bytes 4194304 | tf_op jit(solution)/shard_map/all_to_all | solution.py:34
  39.5 6.9 %convolve.1 = f32[2048,128]{1,0:T(8,128)} custom-call(f32[4096,128]{1,0:T(8,128)S(1)} %bitcast.32, bf16[256,384]{1,0:T(8,128)(2,1)S(1)} %copy-done.7, f32[128,128]{1,0:T(8,128)S(1)} %copy-done.9, f32[128,128]{1,0:T(8,128)S(1)} %copy-done.8, bf16[768,256]{1,0:T(8,128)(2,1)S(1)} %copy-done.5, bf16[768,256]{1,0:T(8,128)(2,1)S(1)} %copy-done.4, ...), custom_call_target="tpu_custom_call" | custom-call | flops 3623878656 | bytes 3145728 | tf_op jit(solution)/shard_map/convolve/pallas_call | solution.py:175
  46.4 3.7 %all-to-all-start.1 = ((f32[32,4,16,128]{3,2,1,0:T(8,128)}), f32[32,4,16,128]{3,2,1,0:T(8,128)S(1)}, u32[]{:S(2)}, u32[]{:S(2)}) async-start(f32[32,4,16,128]{3,2,1,0:T(8,128)} %bitcast.1), calls=%async_computation.1 | async-start | bytes 2097152 | tf_op jit(solution)/shard_map/all_to_all | solution.py:34
  50.2 1.2 columns.1
  51.5 1.1 copy-done.10
  52.6 1.9 %constant_dynamic-slice_fusion = (bf16[512,512]{1,0:T(8,128)(2,1)}, bf16[512,512]{1,0:T(8,128)(2,1)}, bf16[512,512]{1,0:T(8,128)(2,1)}, bf16[512,512]{1,0:T(8,12...) fusion(bf16[512,4096]{1,0:T(8,128)(2,1)S(1)} %copy-done.10, ...), kind=kLoop, calls=%fused_computation.3 | loop fusion | bytes 7340060 | tf_op jit(solution)/shard_map/dynamic_slice | solution.py:251
  54.5 12.8 %all-to-all-done.1.conv_ref = f32[32,4,16,128]{3,2,1,0:T(8,128)S(1)} async-done(((f32[32,4,16,128]{3,2,1,0:T(8,128)}), f32[32,4,16,128]{3,2,1,0:T(8,128)S(1)}, u32[]{:S(2)}, u32[]{:S(2)}) %all-to-all-start.1) | async-done | bytes 1048608 | tf_op jit(solution)/shard_map/all_to_all | solution.py:34
  67.3 0.3 gate.1
  67.6 0.3 fusion
  67.9 0.3 fusion.6
  68.2 1.7 %collective-permute-start = (f32[256,512]{1,0:T(8,128)S(1)}, f32[256,512]{1,0:T(8,128)S(1)}, u32[]{:S(2)}, u32[]{:S(2)}) collective-permute-start(f32[256,512]{1,0:T(8,128)S(1)} %fusion.6), channel_id=1, source_target_pairs={{0,1},{1,2},{2,3},{3,4},{4,5},{5,6},{6,7},{7,0},{8,9},{9,10},{10,1... | collective-permute-start | bytes 1572872 | tf_op jit(solution)/shard_map/ppermute | solution.py:231
  70.0 0.3 fusion.4
  70.3 4.0 %collective-permute-start.10 = (f32[256,512]{1,0:T(8,128)S(1)}, f32[256,512]{1,0:T(8,128)S(1)}, u32[]{:S(2)}, u32[]{:S(2)}) collective-permute-start(f32[256,512]{1,0:T(8,128)S(1)} %fusion), channel_id=1, source_target_pairs={{0,7},{1,0},{2,1},{3,2},{4,3},{5,4},{6,5},{7,6},{8,15},{9,8},{10,9... | collective-permute-start | bytes 1572872 | tf_op jit(solution)/shard_map/ppermute | solution.py:231
  74.3 0.3 fusion.2
  74.6 0.1 collective-permute-start.7
  74.8 2.9 %collective-permute-start.4 = (f32[256,512]{1,0:T(8,128)S(1)}, f32[256,512]{1,0:T(8,128)S(1)}, u32[]{:S(2)}, u32[]{:S(2)}) collective-permute-start(f32[256,512]{1,0:T(8,128)S(1)} %fusion.4), channel_id=1, source_target_pairs={{0,7},{1,0},{2,1},{3,2},{4,3},{5,4},{6,5},{7,6},{8,15},{9,8},{10,9... | collective-permute-start | bytes 1572872 | tf_op jit(solution)/shard_map/ppermute | solution.py:231
  77.7 8.7 %collective-permute-done = f32[256,512]{1,0:T(8,128)S(1)} collective-permute-done((f32[256,512]{1,0:T(8,128)S(1)}, f32[256,512]{1,0:T(8,128)S(1)}, u32[]{:S(2)}, u32[]{:S(2)}) %collective-permute-start) | collective-permute-done | bytes 524320 | tf_op jit(solution)/shard_map/ppermute | solution.py:231
  86.4 0.3 fusion.9
  86.8 0.1 collective-permute-start.1
  86.9 0.3 fusion.16
  87.2 0.1 add.140
  87.3 2.7 %collective-permute-start.11 = (f32[256,512]{1,0:T(8,128)S(1)}, f32[256,512]{1,0:T(8,128)S(1)}, u32[]{:S(2)}, u32[]{:S(2)}) collective-permute-start(f32[256,512]{1,0:T(8,128)S(1)} %add.140), channel_id=1, source_target_pairs={{0,7},{1,0},{2,1},{3,2},{4,3},{5,4},{6,5},{7,6},{8,15},{9,8},{10,9... | collective-permute-start | bytes 1572872 | tf_op jit(solution)/shard_map/ppermute | solution.py:231
  90.0 7.6 %collective-permute-done.7 = f32[256,512]{1,0:T(8,128)S(1)} collective-permute-done((f32[256,512]{1,0:T(8,128)S(1)}, f32[256,512]{1,0:T(8,128)S(1)}, u32[]{:S(2)}, u32[]{:S(2)}) %collective-permute-start.7) | collective-permute-done | bytes 524320 | tf_op jit(solution)/shard_map/ppermute | solution.py:231
  97.6 0.3 fusion.14
  98.0 0.1 collective-permute-start.8
  98.1 0.3 fusion.12
  98.5 2.7 %collective-permute-start.5 = (f32[256,512]{1,0:T(8,128)S(1)}, f32[256,512]{1,0:T(8,128)S(1)}, u32[]{:S(2)}, u32[]{:S(2)}) collective-permute-start(f32[256,512]{1,0:T(8,128)S(1)} %add.134), channel_id=1, source_target_pairs={{0,7},{1,0},{2,1},{3,2},{4,3},{5,4},{6,5},{7,6},{8,15},{9,8},{10,9... | collective-permute-start | bytes 1572872 | tf_op jit(solution)/shard_map/ppermute | solution.py:231
  101.3 7.6 %collective-permute-done.1 = f32[256,512]{1,0:T(8,128)S(1)} collective-permute-done((f32[256,512]{1,0:T(8,128)S(1)}, f32[256,512]{1,0:T(8,128)S(1)}, u32[]{:S(2)}, u32[]{:S(2)}) %collective-permute-start.1) | collective-permute-done | bytes 524320 | tf_op jit(solution)/shard_map/ppermute | solution.py:231
  108.9 0.3 fusion.10
  109.4 0.3 fusion.17
  109.7 2.7 %collective-permute-start.12 = (f32[256,512]{1,0:T(8,128)S(1)}, f32[256,512]{1,0:T(8,128)S(1)}, u32[]{:S(2)}, u32[]{:S(2)}) collective-permute-start(f32[256,512]{1,0:T(8,128)S(1)} %add.141), channel_id=1, source_target_pairs={{0,7},{1,0},{2,1},{3,2},{4,3},{5,4},{6,5},{7,6},{8,15},{9,8},{10,9... | collective-permute-start | bytes 1572872 | tf_op jit(solution)/shard_map/ppermute | solution.py:231
  112.5 7.6 %collective-permute-done.8 = f32[256,512]{1,0:T(8,128)S(1)} collective-permute-done((f32[256,512]{1,0:T(8,128)S(1)}, f32[256,512]{1,0:T(8,128)S(1)}, u32[]{:S(2)}, u32[]{:S(2)}) %collective-permute-start.8) | collective-permute-done | bytes 524320 | tf_op jit(solution)/shard_map/ppermute | solution.py:231
  120.1 0.3 fusion.15
  120.4 0.1 add.139
  120.6 0.3 fusion.13
  120.9 0.1 add.135
  121.0 2.7 %collective-permute-start.6 = (f32[256,512]{1,0:T(8,128)S(1)}, f32[256,512]{1,0:T(8,128)S(1)}, u32[]{:S(2)}, u32[]{:S(2)}) collective-permute-start(f32[256,512]{1,0:T(8,128)S(1)} %add.135), channel_id=1, source_target_pairs={{0,7},{1,0},{2,1},{3,2},{4,3},{5,4},{6,5},{7,6},{8,15},{9,8},{10,9... | collective-permute-start | bytes 1572872 | tf_op jit(solution)/shard_map/ppermute | solution.py:231
  123.7 7.6 %collective-permute-done.2 = f32[256,512]{1,0:T(8,128)S(1)} collective-permute-done((f32[256,512]{1,0:T(8,128)S(1)}, f32[256,512]{1,0:T(8,128)S(1)}, u32[]{:S(2)}, u32[]{:S(2)}) %collective-permute-start.2) | collective-permute-done | bytes 524320 | tf_op jit(solution)/shard_map/ppermute | solution.py:231
  131.3 0.3 fusion.18
  131.6 0.1 add.142
  131.7 3.1 %collective-permute-start.13 = (f32[256,512]{1,0:T(8,128)S(1)}, f32[256,512]{1,0:T(8,128)S(1)}, u32[]{:S(2)}, u32[]{:S(2)}) collective-permute-start(f32[256,512]{1,0:T(8,128)S(1)} %add.142), channel_id=1, source_target_pairs={{0,7},{1,0},{2,1},{3,2},{4,3},{5,4},{6,5},{7,6},{8,15},{9,8},{10,9... | collective-permute-start | bytes 1572872 | tf_op jit(solution)/shard_map/ppermute | solution.py:231
  134.8 0.3 fusion.11
  135.3 7.2 %collective-permute-done.9 = f32[256,512]{1,0:T(8,128)S(1)} collective-permute-done((f32[256,512]{1,0:T(8,128)S(1)}, f32[256,512]{1,0:T(8,128)S(1)}, u32[]{:S(2)}, u32[]{:S(2)}) %collective-permute-start.9) | collective-permute-done | bytes 524320 | tf_op jit(solution)/shard_map/ppermute | solution.py:231
  142.6 10.1 %collective-permute-done.13 = f32[256,512]{1,0:T(8,128)S(1)} collective-permute-done((f32[256,512]{1,0:T(8,128)S(1)}, f32[256,512]{1,0:T(8,128)S(1)}, u32[]{:S(2)}, u32[]{:S(2)}) %collective-permute-start.13) | collective-permute-done | bytes 524320 | tf_op jit(solution)/shard_map/ppermute | solution.py:231
  152.7 0.3 add_convert_fusion
  153.0 0.3 add_convert_fusion.1
  153.3 0.8 pad_maximum_fusion
  (52 shorter events, 0.9 us)
Async XLA Ops:
  0.0 39.4 %copy-start.4 = (bf16[768,256]{1,0:T(8,128)(2,1)S(1)}, bf16[768,256]{1,0:T(8,128)(2,1)}, u32[]{:S(2)}) copy-start(bf16[768,256]{1,0:T(8,128)(2,1)} %constant.79.clone.refs_5_) | copy-start | bytes 1179652
  0.0 39.4 %copy-start.5 = (bf16[768,256]{1,0:T(8,128)(2,1)S(1)}, bf16[768,256]{1,0:T(8,128)(2,1)}, u32[]{:S(2)}) copy-start(bf16[768,256]{1,0:T(8,128)(2,1)} %constant.78.clone.refs_4_) | copy-start | bytes 1179652
  0.0 39.4 %copy-start.6 = (bf16[128,768]{1,0:T(8,128)(2,1)S(1)}, bf16[128,768]{1,0:T(8,128)(2,1)}, u32[]{:S(2)}) copy-start(bf16[128,768]{1,0:T(8,128)(2,1)} %constant.80.clone.refs_6_) | copy-start | bytes 589828
  0.0 39.5 %copy-start.7 = (bf16[256,384]{1,0:T(8,128)(2,1)S(1)}, bf16[256,384]{1,0:T(8,128)(2,1)}, u32[]{:S(2)}) copy-start(bf16[256,384]{1,0:T(8,128)(2,1)} %constant.77.clone.refs_1_) | copy-start | bytes 589828
  0.0 39.4 %copy-start.8 = (f32[128,128]{1,0:T(8,128)S(1)}, f32[128,128]{1,0:T(8,128)}, u32[]{:S(2)}) copy-start(f32[128,128]{1,0:T(8,128)} %constant.76.clone.refs_3_) | copy-start | bytes 196612
  0.0 39.4 %copy-start.9 = (f32[128,128]{1,0:T(8,128)S(1)}, f32[128,128]{1,0:T(8,128)}, u32[]{:S(2)}) copy-start(f32[128,128]{1,0:T(8,128)} %constant.75.clone.refs_2_) | copy-start | bytes 196612
  46.4 20.9 %all-to-all-start.1 = ((f32[32,4,16,128]{3,2,1,0:T(8,128)}), f32[32,4,16,128]{3,2,1,0:T(8,128)S(1)}, u32[]{:S(2)}, u32[]{:S(2)}) async-start(f32[32,4,16,128]{3,2,1,0:T(8,128)} %bitcast.1), calls=%async_computation.1 | async-start | bytes 2097152 | tf_op jit(solution)/shard_map/all_to_all | solution.py:34
  50.2 2.4 %copy-start.10 = (bf16[512,4096]{1,0:T(8,128)(2,1)S(1)}, bf16[512,4096]{1,0:T(8,128)(2,1)}, u32[]{:S(2)}) copy-start(bf16[512,4096]{1,0:T(8,128)(2,1)} %weight_ref.1) | copy-start | bytes 12582916
  52.6 14.7 %copy-start = (bf16[512,512]{1,0:T(8,128)(2,1)S(1)}, bf16[512,512]{1,0:T(8,128)(2,1)}, u32[]{:S(2)}) copy-start(bf16[512,512]{1,0:T(8,128)(2,1)} %key_ref.3) | copy-start | bytes 1572868
  52.6 14.7 %copy-start.1 = (bf16[512,512]{1,0:T(8,128)(2,1)S(1)}, bf16[512,512]{1,0:T(8,128)(2,1)}, u32[]{:S(2)}) copy-start(bf16[512,512]{1,0:T(8,128)(2,1)} %value_ref.3) | copy-start | bytes 1572868
  52.6 14.7 %copy-start.2 = (bf16[512,512]{1,0:T(8,128)(2,1)S(1)}, bf16[512,512]{1,0:T(8,128)(2,1)}, u32[]{:S(2)}) copy-start(bf16[512,512]{1,0:T(8,128)(2,1)} %query_ref.1) | copy-start | bytes 1572868
  52.6 14.7 %copy-start.3 = (f32[512]{0:T(512)S(1)}, f32[512]{0:T(512)}, u32[]{:S(2)}) copy-start(f32[512]{0:T(512)} %param.16) | copy-start | bytes 6148
  67.3 2.7 %copy-start.15 = (bf16[512,512]{1,0:T(8,128)(2,1)S(1)}, bf16[512,512]{1,0:T(8,128)(2,1)}, u32[]{:S(2)}) copy-start(bf16[512,512]{1,0:T(8,128)(2,1)} %get-tuple-element.51) | copy-start | bytes 1572868
  67.3 7.1 %copy-start.16 = (bf16[512,512]{1,0:T(8,128)(2,1)S(1)}, bf16[512,512]{1,0:T(8,128)(2,1)}, u32[]{:S(2)}) copy-start(bf16[512,512]{1,0:T(8,128)(2,1)} %get-tuple-element.44) | copy-start | bytes 1572868
  68.2 18.1 %collective-permute-start = (f32[256,512]{1,0:T(8,128)S(1)}, f32[256,512]{1,0:T(8,128)S(1)}, u32[]{:S(2)}, u32[]{:S(2)}) collective-permute-start(f32[256,512]{1,0:T(8,128)S(1)} %fusion.6), channel_id=1, source_target_pairs={{0,1},{1,2},{2,3},{3,4},{4,5},{5,6},{6,7},{7,0},{8,9},{9,10},{10,1... | collective-permute-start | bytes 1572872 | tf_op jit(solution)/shard_map/ppermute | solution.py:231
  70.3 27.4 %copy-start.14 = (bf16[512,512]{1,0:T(8,128)(2,1)S(1)}, bf16[512,512]{1,0:T(8,128)(2,1)}, u32[]{:S(2)}) copy-start(bf16[512,512]{1,0:T(8,128)(2,1)} %get-tuple-element.47) | copy-start | bytes 1572868
  70.3 16.6 %collective-permute-start.10 = (f32[256,512]{1,0:T(8,128)S(1)}, f32[256,512]{1,0:T(8,128)S(1)}, u32[]{:S(2)}, u32[]{:S(2)}) collective-permute-start(f32[256,512]{1,0:T(8,128)S(1)} %fusion), channel_id=1, source_target_pairs={{0,7},{1,0},{2,1},{3,2},{4,3},{5,4},{6,5},{7,6},{8,15},{9,8},{10,9... | collective-permute-start | bytes 1572872 | tf_op jit(solution)/shard_map/ppermute | solution.py:231
  74.6 23.0 %collective-permute-start.7 = (f32[256,512]{1,0:T(8,128)S(1)}, f32[256,512]{1,0:T(8,128)S(1)}, u32[]{:S(2)}, u32[]{:S(2)}) collective-permute-start(f32[256,512]{1,0:T(8,128)S(1)} %fusion.2), channel_id=1, source_target_pairs={{0,1},{1,2},{2,3},{3,4},{4,5},{5,6},{6,7},{7,0},{8,9},{9,10},{10,1... | collective-permute-start | bytes 1572872 | tf_op jit(solution)/shard_map/ppermute | solution.py:231
  74.8 23.4 %collective-permute-start.4 = (f32[256,512]{1,0:T(8,128)S(1)}, f32[256,512]{1,0:T(8,128)S(1)}, u32[]{:S(2)}, u32[]{:S(2)}) collective-permute-start(f32[256,512]{1,0:T(8,128)S(1)} %fusion.4), channel_id=1, source_target_pairs={{0,7},{1,0},{2,1},{3,2},{4,3},{5,4},{6,5},{7,6},{8,15},{9,8},{10,9... | collective-permute-start | bytes 1572872 | tf_op jit(solution)/shard_map/ppermute | solution.py:231
  86.4 11.7 %copy-start.13 = (bf16[512,512]{1,0:T(8,128)(2,1)S(1)}, bf16[512,512]{1,0:T(8,128)(2,1)}, u32[]{:S(2)}) copy-start(bf16[512,512]{1,0:T(8,128)(2,1)} %get-tuple-element.54) | copy-start | bytes 1572868
  86.8 22.1 %collective-permute-start.1 = (f32[256,512]{1,0:T(8,128)S(1)}, f32[256,512]{1,0:T(8,128)S(1)}, u32[]{:S(2)}, u32[]{:S(2)}) collective-permute-start(f32[256,512]{1,0:T(8,128)S(1)} %add.131), channel_id=1, source_target_pairs={{0,1},{1,2},{2,3},{3,4},{4,5},{5,6},{6,7},{7,0},{8,9},{9,10},{10,1... | collective-permute-start | bytes 1572872 | tf_op jit(solution)/shard_map/ppermute | solution.py:231
  87.3 22.1 %collective-permute-start.11 = (f32[256,512]{1,0:T(8,128)S(1)}, f32[256,512]{1,0:T(8,128)S(1)}, u32[]{:S(2)}, u32[]{:S(2)}) collective-permute-start(f32[256,512]{1,0:T(8,128)S(1)} %add.140), channel_id=1, source_target_pairs={{0,7},{1,0},{2,1},{3,2},{4,3},{5,4},{6,5},{7,6},{8,15},{9,8},{10,9... | collective-permute-start | bytes 1572872 | tf_op jit(solution)/shard_map/ppermute | solution.py:231
  98.0 22.1 %copy-start.11 = (bf16[512,512]{1,0:T(8,128)(2,1)S(1)}, bf16[512,512]{1,0:T(8,128)(2,1)}, u32[]{:S(2)}) copy-start(bf16[512,512]{1,0:T(8,128)(2,1)} %get-tuple-element.50) | copy-start | bytes 1572868
  98.0 22.1 %collective-permute-start.8 = (f32[256,512]{1,0:T(8,128)S(1)}, f32[256,512]{1,0:T(8,128)S(1)}, u32[]{:S(2)}, u32[]{:S(2)}) collective-permute-start(f32[256,512]{1,0:T(8,128)S(1)} %add.138), channel_id=1, source_target_pairs={{0,1},{1,2},{2,3},{3,4},{4,5},{5,6},{6,7},{7,0},{8,9},{9,10},{10,1... | collective-permute-start | bytes 1572872 | tf_op jit(solution)/shard_map/ppermute | solution.py:231
  98.5 22.1 %copy-start.12 = (bf16[512,512]{1,0:T(8,128)(2,1)S(1)}, bf16[512,512]{1,0:T(8,128)(2,1)}, u32[]{:S(2)}) copy-start(bf16[512,512]{1,0:T(8,128)(2,1)} %get-tuple-element.57) | copy-start | bytes 1572868
  98.5 22.1 %collective-permute-start.5 = (f32[256,512]{1,0:T(8,128)S(1)}, f32[256,512]{1,0:T(8,128)S(1)}, u32[]{:S(2)}, u32[]{:S(2)}) collective-permute-start(f32[256,512]{1,0:T(8,128)S(1)} %add.134), channel_id=1, source_target_pairs={{0,7},{1,0},{2,1},{3,2},{4,3},{5,4},{6,5},{7,6},{8,15},{9,8},{10,9... | collective-permute-start | bytes 1572872 | tf_op jit(solution)/shard_map/ppermute | solution.py:231
  109.3 22.1 %collective-permute-start.2 = (f32[256,512]{1,0:T(8,128)S(1)}, f32[256,512]{1,0:T(8,128)S(1)}, u32[]{:S(2)}, u32[]{:S(2)}) collective-permute-start(f32[256,512]{1,0:T(8,128)S(1)} %add.132), channel_id=1, source_target_pairs={{0,1},{1,2},{2,3},{3,4},{4,5},{5,6},{6,7},{7,0},{8,9},{9,10},{10,1... | collective-permute-start | bytes 1572872 | tf_op jit(solution)/shard_map/ppermute | solution.py:231
  109.7 21.6 %collective-permute-start.12 = (f32[256,512]{1,0:T(8,128)S(1)}, f32[256,512]{1,0:T(8,128)S(1)}, u32[]{:S(2)}, u32[]{:S(2)}) collective-permute-start(f32[256,512]{1,0:T(8,128)S(1)} %add.141), channel_id=1, source_target_pairs={{0,7},{1,0},{2,1},{3,2},{4,3},{5,4},{6,5},{7,6},{8,15},{9,8},{10,9... | collective-permute-start | bytes 1572872 | tf_op jit(solution)/shard_map/ppermute | solution.py:231
  120.5 32.2 %copy-start.17 = (bf16[512,512]{1,0:T(8,128)(2,1)S(1)}, bf16[512,512]{1,0:T(8,128)(2,1)}, u32[]{:S(2)}) copy-start(bf16[512,512]{1,0:T(8,128)(2,1)} %get-tuple-element.61) | copy-start | bytes 1572868
  120.5 22.1 %collective-permute-start.9 = (f32[256,512]{1,0:T(8,128)S(1)}, f32[256,512]{1,0:T(8,128)S(1)}, u32[]{:S(2)}, u32[]{:S(2)}) collective-permute-start(f32[256,512]{1,0:T(8,128)S(1)} %add.139), channel_id=1, source_target_pairs={{0,1},{1,2},{2,3},{3,4},{4,5},{5,6},{6,7},{7,0},{8,9},{9,10},{10,1... | collective-permute-start | bytes 1572872 | tf_op jit(solution)/shard_map/ppermute | solution.py:231
  121.0 31.7 %collective-permute-start.6 = (f32[256,512]{1,0:T(8,128)S(1)}, f32[256,512]{1,0:T(8,128)S(1)}, u32[]{:S(2)}, u32[]{:S(2)}) collective-permute-start(f32[256,512]{1,0:T(8,128)S(1)} %add.135), channel_id=1, source_target_pairs={{0,7},{1,0},{2,1},{3,2},{4,3},{5,4},{6,5},{7,6},{8,15},{9,8},{10,9... | collective-permute-start | bytes 1572872 | tf_op jit(solution)/shard_map/ppermute | solution.py:231
  131.7 21.0 %collective-permute-start.13 = (f32[256,512]{1,0:T(8,128)S(1)}, f32[256,512]{1,0:T(8,128)S(1)}, u32[]{:S(2)}, u32[]{:S(2)}) collective-permute-start(f32[256,512]{1,0:T(8,128)S(1)} %add.142), channel_id=1, source_target_pairs={{0,7},{1,0},{2,1},{3,2},{4,3},{5,4},{6,5},{7,6},{8,15},{9,8},{10,9... | collective-permute-start | bytes 1572872 | tf_op jit(solution)/shard_map/ppermute | solution.py:231
  135.2 17.5 %collective-permute-start.3 = (f32[256,512]{1,0:T(8,128)S(1)}, f32[256,512]{1,0:T(8,128)S(1)}, u32[]{:S(2)}, u32[]{:S(2)}) collective-permute-start(f32[256,512]{1,0:T(8,128)S(1)} %add.133), channel_id=1, source_target_pairs={{0,1},{1,2},{2,3},{3,4},{4,5},{5,6},{6,7},{7,0},{8,9},{9,10},{10,1... | collective-permute-start | bytes 1572872 | tf_op jit(solution)/shard_map/ppermute | solution.py:231

commit v8 on v7

--- a/solution.py
+++ b/solution.py
@@ -233,6 +233,24 @@
             return got
         got, gated = lax.optimization_barrier((got, gated))
         total = got + dot(gated, weights[way * ahead % n_chan])
+
+
+def join_kernel(upper_ref, lower_ref, out_ref):
+    half = upper_ref.shape[0]
+    out_ref[:half] = upper_ref[...]
+    out_ref[half:] = lower_ref[...]
+
+
+def join(upper, lower):
+    whole = pl.BlockSpec(memory_space=pltpu.VMEM)
+    return pl.pallas_call(
+        join_kernel,
+        in_specs=[whole] * 2,
+        out_specs=whole,
+        out_shape=jax.ShapeDtypeStruct((2 * upper.shape[0], upper.shape[1]), upper.dtype),
+        compiler_params=pltpu.CompilerParams(vmem_limit_bytes=SMALL_VMEM),
+        name="join",
+    )(upper, lower)
 
 
 def on_device(query_in, key_in, value_in, filter_taps, skip_gain, out_weight):
@@ -260,8 +278,8 @@
     for block, starts in ((gated[:half], (far, far - 1)), (gated[half:], (far - 1, far))):
         up, down = [ring_sum(block, weights, way, start) for way, start in zip((1, -1), starts)]
         up, down, block = lax.optimization_barrier((up, down, block))
-        rows.append(up + down + dot(block, weights[0]))
-    return jnp.concatenate(rows, 0).astype(BF16)
+        rows.append((up + down + dot(block, weights[0])).astype(BF16))
+    return join(*rows)
 
 
 def solution(mesh):

time: 154 us -> 154 us (level)
  no operation moved by 1% of the time
where the time goes in v8:
time: 154 us
  waiting for transfers between devices  69.3 us (45%)
  blocking collectives  37.3 us (24%)
  starting transfers between devices  26.9 us (17%)
  Pallas kernels  11.4 us (7%)
  matrix products  4.75 us (3%)
  local copies, waits for them, and re-layouts  3.13 us (2%)
    ppermute x14, waiting for transfers between devices, ring_sum(): got = lax.ppermute(total, 'chan', hops)  56.5 us
    all_to_all x1, blocking collectives, exchange(): lax.all_to_all(value, 'seq', split_axis=0, concat_axis=0, tiled=True, axi...  37.3 us
    ppermute x14, starting transfers between devices, ring_sum(): got = lax.ppermute(total, 'chan', hops)  23.2 us
    all_to_all x1, waiting for transfers between devices, exchange(): lax.all_to_all(value, 'seq', split_axis=0, concat_axis=0, tiled=True, axi...  12.8 us
    pallas_call x1, Pallas kernels, convolve(): pl.pallas_call(lambda *refs: conv_kernel(n_parts, width, group, *refs), o...  6.9 us
    dot_general x16, matrix products, dot(): return jnp.dot(left, right, preferred_element_type=F32)  4.75 us
    all_to_all x1, starting transfers between devices, exchange(): lax.all_to_all(value, 'seq', split_axis=0, concat_axis=0, tiled=True, axi...  3.72 us
  transfers between devices with their start and end apart: 15, of which 8 were waited for; matrix products, arithmetic and copies ran while one was open for 4% of the time, Pallas kernels for 1%

profile of v8, /device:TPU:1, one launch (start us, length us, event | category | flops | bytes accessed | tf_op | source)
XLA Modules:
  0.0 154.2 jit_solution(7257194752433176791)
XLA Ops:
  0.0 2.1 %pack.1 = f32[32,2,4,16,128]{4,3,2,1,0:T(8,128)S(1)} custom-call(bf16[512,512]{1,0:T(8,128)(2,1)} %key_ref.3, bf16[512,512]{1,0:T(8,128)(2,1)} %value_ref.3, f32[512,512]{1,0:T(8,128)} %taps_ref.1), custom_call_target="tpu_custom_call" | custom-call | tf_op jit(solution)/shard_map/pack/pallas_call | solution.py:113
  2.2 37.3 %all_to_all.10 = f32[32,2,4,16,128]{4,3,2,1,0:T(8,128)S(1)} all-to-all(f32[32,2,4,16,128]{4,3,2,1,0:T(8,128)S(1)} %pack.1), channel_id=1, replica_groups={{0,8,16,24,48,56,32,40,64,72,80,88,112,120,96,104,192,200,208,216,240,2..., dimensions={0} | all-to-all | bytes 4194304 | tf_op jit(solution)/shard_map/all_to_all | solution.py:34
  39.5 6.9 %convolve.1 = f32[2048,128]{1,0:T(8,128)} custom-call(f32[4096,128]{1,0:T(8,128)S(1)} %bitcast.32, bf16[256,384]{1,0:T(8,128)(2,1)S(1)} %copy-done.7, f32[128,128]{1,0:T(8,128)S(1)} %copy-done.9, f32[128,128]{1,0:T(8,128)S(1)} %copy-done.8, bf16[768,256]{1,0:T(8,128)(2,1)S(1)} %copy-done.5, bf16[768,256]{1,0:T(8,128)(2,1)S(1)} %copy-done.4, ...), custom_call_target="tpu_custom_call" | custom-call | flops 3623878656 | bytes 3145728 | tf_op jit(solution)/shard_map/convolve/pallas_call | solution.py:175
  46.4 3.7 %all-to-all-start.1 = ((f32[32,4,16,128]{3,2,1,0:T(8,128)}), f32[32,4,16,128]{3,2,1,0:T(8,128)S(1)}, u32[]{:S(2)}, u32[]{:S(2)}) async-start(f32[32,4,16,128]{3,2,1,0:T(8,128)} %bitcast.1), calls=%async_computation.1 | async-start | bytes 2097152 | tf_op jit(solution)/shard_map/all_to_all | solution.py:34
  50.2 1.2 columns.1
  51.5 1.1 copy-done.10
  52.6 1.9 %constant_dynamic-slice_fusion = (bf16[512,512]{1,0:T(8,128)(2,1)}, bf16[512,512]{1,0:T(8,128)(2,1)}, bf16[512,512]{1,0:T(8,128)(2,1)}, bf16[512,512]{1,0:T(8,12...) fusion(bf16[512,4096]{1,0:T(8,128)(2,1)S(1)} %copy-done.10, ...), kind=kLoop, calls=%fused_computation.2 | loop fusion | bytes 7340060 | tf_op jit(solution)/shard_map/dynamic_slice | solution.py:269
  54.5 12.8 %all-to-all-done.1.conv_ref = f32[32,4,16,128]{3,2,1,0:T(8,128)S(1)} async-done(((f32[32,4,16,128]{3,2,1,0:T(8,128)}), f32[32,4,16,128]{3,2,1,0:T(8,128)S(1)}, u32[]{:S(2)}, u32[]{:S(2)}) %all-to-all-start.1) | async-done | bytes 1048608 | tf_op jit(solution)/shard_map/all_to_all | solution.py:34
  67.3 0.3 gate.1
  67.6 0.3 fusion
  67.9 0.3 fusion.6
  68.2 1.7 %collective-permute-start = (f32[256,512]{1,0:T(8,128)S(1)}, f32[256,512]{1,0:T(8,128)S(1)}, u32[]{:S(2)}, u32[]{:S(2)}) collective-permute-start(f32[256,512]{1,0:T(8,128)S(1)} %fusion.6), channel_id=1, source_target_pairs={{0,1},{1,2},{2,3},{3,4},{4,5},{5,6},{6,7},{7,0},{8,9},{9,10},{10,1... | collective-permute-start | bytes 1572872 | tf_op jit(solution)/shard_map/ppermute | solution.py:231
  70.0 0.3 fusion.4
  70.3 4.0 %collective-permute-start.10 = (f32[256,512]{1,0:T(8,128)S(1)}, f32[256,512]{1,0:T(8,128)S(1)}, u32[]{:S(2)}, u32[]{:S(2)}) collective-permute-start(f32[256,512]{1,0:T(8,128)S(1)} %fusion), channel_id=1, source_target_pairs={{0,7},{1,0},{2,1},{3,2},{4,3},{5,4},{6,5},{7,6},{8,15},{9,8},{10,9... | collective-permute-start | bytes 1572872 | tf_op jit(solution)/shard_map/ppermute | solution.py:231
  74.3 0.3 fusion.2
  74.6 0.1 collective-permute-start.7
  74.8 2.9 %collective-permute-start.4 = (f32[256,512]{1,0:T(8,128)S(1)}, f32[256,512]{1,0:T(8,128)S(1)}, u32[]{:S(2)}, u32[]{:S(2)}) collective-permute-start(f32[256,512]{1,0:T(8,128)S(1)} %fusion.4), channel_id=1, source_target_pairs={{0,7},{1,0},{2,1},{3,2},{4,3},{5,4},{6,5},{7,6},{8,15},{9,8},{10,9... | collective-permute-start | bytes 1572872 | tf_op jit(solution)/shard_map/ppermute | solution.py:231
  77.7 8.7 %collective-permute-done = f32[256,512]{1,0:T(8,128)S(1)} collective-permute-done((f32[256,512]{1,0:T(8,128)S(1)}, f32[256,512]{1,0:T(8,128)S(1)}, u32[]{:S(2)}, u32[]{:S(2)}) %collective-permute-start) | collective-permute-done | bytes 524320 | tf_op jit(solution)/shard_map/ppermute | solution.py:231
  86.4 0.3 fusion.9
  86.8 0.1 collective-permute-start.1
  86.9 0.3 fusion.16
  87.2 0.1 add.140
  87.3 2.7 %collective-permute-start.11 = (f32[256,512]{1,0:T(8,128)S(1)}, f32[256,512]{1,0:T(8,128)S(1)}, u32[]{:S(2)}, u32[]{:S(2)}) collective-permute-start(f32[256,512]{1,0:T(8,128)S(1)} %add.140), channel_id=1, source_target_pairs={{0,7},{1,0},{2,1},{3,2},{4,3},{5,4},{6,5},{7,6},{8,15},{9,8},{10,9... | collective-permute-start | bytes 1572872 | tf_op jit(solution)/shard_map/ppermute | solution.py:231
  90.0 7.6 %collective-permute-done.7 = f32[256,512]{1,0:T(8,128)S(1)} collective-permute-done((f32[256,512]{1,0:T(8,128)S(1)}, f32[256,512]{1,0:T(8,128)S(1)}, u32[]{:S(2)}, u32[]{:S(2)}) %collective-permute-start.7) | collective-permute-done | bytes 524320 | tf_op jit(solution)/shard_map/ppermute | solution.py:231
  97.6 0.3 fusion.14
  98.0 0.1 collective-permute-start.8
  98.1 0.3 fusion.12
  98.5 2.7 %collective-permute-start.5 = (f32[256,512]{1,0:T(8,128)S(1)}, f32[256,512]{1,0:T(8,128)S(1)}, u32[]{:S(2)}, u32[]{:S(2)}) collective-permute-start(f32[256,512]{1,0:T(8,128)S(1)} %add.134), channel_id=1, source_target_pairs={{0,7},{1,0},{2,1},{3,2},{4,3},{5,4},{6,5},{7,6},{8,15},{9,8},{10,9... | collective-permute-start | bytes 1572872 | tf_op jit(solution)/shard_map/ppermute | solution.py:231
  101.3 7.6 %collective-permute-done.1 = f32[256,512]{1,0:T(8,128)S(1)} collective-permute-done((f32[256,512]{1,0:T(8,128)S(1)}, f32[256,512]{1,0:T(8,128)S(1)}, u32[]{:S(2)}, u32[]{:S(2)}) %collective-permute-start.1) | collective-permute-done | bytes 524320 | tf_op jit(solution)/shard_map/ppermute | solution.py:231
  108.9 0.3 fusion.10
  109.3 0.1 collective-permute-start.2
  109.4 0.3 fusion.17
  109.7 2.7 %collective-permute-start.12 = (f32[256,512]{1,0:T(8,128)S(1)}, f32[256,512]{1,0:T(8,128)S(1)}, u32[]{:S(2)}, u32[]{:S(2)}) collective-permute-start(f32[256,512]{1,0:T(8,128)S(1)} %add.141), channel_id=1, source_target_pairs={{0,7},{1,0},{2,1},{3,2},{4,3},{5,4},{6,5},{7,6},{8,15},{9,8},{10,9... | collective-permute-start | bytes 1572872 | tf_op jit(solution)/shard_map/ppermute | solution.py:231
  112.5 7.6 %collective-permute-done.8 = f32[256,512]{1,0:T(8,128)S(1)} collective-permute-done((f32[256,512]{1,0:T(8,128)S(1)}, f32[256,512]{1,0:T(8,128)S(1)}, u32[]{:S(2)}, u32[]{:S(2)}) %collective-permute-start.8) | collective-permute-done | bytes 524320 | tf_op jit(solution)/shard_map/ppermute | solution.py:231
  120.1 0.3 fusion.15
  120.4 0.1 add.139
  120.6 0.3 fusion.13
  120.9 0.1 add.135
  121.0 2.7 %collective-permute-start.6 = (f32[256,512]{1,0:T(8,128)S(1)}, f32[256,512]{1,0:T(8,128)S(1)}, u32[]{:S(2)}, u32[]{:S(2)}) collective-permute-start(f32[256,512]{1,0:T(8,128)S(1)} %add.135), channel_id=1, source_target_pairs={{0,7},{1,0},{2,1},{3,2},{4,3},{5,4},{6,5},{7,6},{8,15},{9,8},{10,9... | collective-permute-start | bytes 1572872 | tf_op jit(solution)/shard_map/ppermute | solution.py:231
  123.7 7.6 %collective-permute-done.2 = f32[256,512]{1,0:T(8,128)S(1)} collective-permute-done((f32[256,512]{1,0:T(8,128)S(1)}, f32[256,512]{1,0:T(8,128)S(1)}, u32[]{:S(2)}, u32[]{:S(2)}) %collective-permute-start.2) | collective-permute-done | bytes 524320 | tf_op jit(solution)/shard_map/ppermute | solution.py:231
  131.3 0.3 fusion.18
  131.7 3.1 %collective-permute-start.13 = (f32[256,512]{1,0:T(8,128)S(1)}, f32[256,512]{1,0:T(8,128)S(1)}, u32[]{:S(2)}, u32[]{:S(2)}) collective-permute-start(f32[256,512]{1,0:T(8,128)S(1)} %add.142), channel_id=1, source_target_pairs={{0,7},{1,0},{2,1},{3,2},{4,3},{5,4},{6,5},{7,6},{8,15},{9,8},{10,9... | collective-permute-start | bytes 1572872 | tf_op jit(solution)/shard_map/ppermute | solution.py:231
  134.8 0.3 fusion.11
  135.3 7.2 %collective-permute-done.9 = f32[256,512]{1,0:T(8,128)S(1)} collective-permute-done((f32[256,512]{1,0:T(8,128)S(1)}, f32[256,512]{1,0:T(8,128)S(1)}, u32[]{:S(2)}, u32[]{:S(2)}) %collective-permute-start.9) | collective-permute-done | bytes 524320 | tf_op jit(solution)/shard_map/ppermute | solution.py:231
  142.6 10.1 %collective-permute-done.13 = f32[256,512]{1,0:T(8,128)S(1)} collective-permute-done((f32[256,512]{1,0:T(8,128)S(1)}, f32[256,512]{1,0:T(8,128)S(1)}, u32[]{:S(2)}, u32[]{:S(2)}) %collective-permute-start.13) | collective-permute-done | bytes 524320 | tf_op jit(solution)/shard_map/ppermute | solution.py:231
  152.7 0.3 add_convert_fusion.lower_ref
  153.0 0.3 add_convert_fusion.1.upper_ref
  153.3 0.8 join.1
  (52 shorter events, 0.9 us)
Async XLA Ops:
  0.0 39.4 %copy-start.4 = (bf16[768,256]{1,0:T(8,128)(2,1)S(1)}, bf16[768,256]{1,0:T(8,128)(2,1)}, u32[]{:S(2)}) copy-start(bf16[768,256]{1,0:T(8,128)(2,1)} %constant.79.clone.refs_5_) | copy-start | bytes 1179652
  0.0 39.4 %copy-start.5 = (bf16[768,256]{1,0:T(8,128)(2,1)S(1)}, bf16[768,256]{1,0:T(8,128)(2,1)}, u32[]{:S(2)}) copy-start(bf16[768,256]{1,0:T(8,128)(2,1)} %constant.78.clone.refs_4_) | copy-start | bytes 1179652
  0.0 39.4 %copy-start.6 = (bf16[128,768]{1,0:T(8,128)(2,1)S(1)}, bf16[128,768]{1,0:T(8,128)(2,1)}, u32[]{:S(2)}) copy-start(bf16[128,768]{1,0:T(8,128)(2,1)} %constant.80.clone.refs_6_) | copy-start | bytes 589828
  0.0 39.5 %copy-start.7 = (bf16[256,384]{1,0:T(8,128)(2,1)S(1)}, bf16[256,384]{1,0:T(8,128)(2,1)}, u32[]{:S(2)}) copy-start(bf16[256,384]{1,0:T(8,128)(2,1)} %constant.77.clone.refs_1_) | copy-start | bytes 589828
  0.0 39.4 %copy-start.8 = (f32[128,128]{1,0:T(8,128)S(1)}, f32[128,128]{1,0:T(8,128)}, u32[]{:S(2)}) copy-start(f32[128,128]{1,0:T(8,128)} %constant.76.clone.refs_3_) | copy-start | bytes 196612
  0.0 39.4 %copy-start.9 = (f32[128,128]{1,0:T(8,128)S(1)}, f32[128,128]{1,0:T(8,128)}, u32[]{:S(2)}) copy-start(f32[128,128]{1,0:T(8,128)} %constant.75.clone.refs_2_) | copy-start | bytes 196612
  46.4 20.9 %all-to-all-start.1 = ((f32[32,4,16,128]{3,2,1,0:T(8,128)}), f32[32,4,16,128]{3,2,1,0:T(8,128)S(1)}, u32[]{:S(2)}, u32[]{:S(2)}) async-start(f32[32,4,16,128]{3,2,1,0:T(8,128)} %bitcast.1), calls=%async_computation.1 | async-start | bytes 2097152 | tf_op jit(solution)/shard_map/all_to_all | solution.py:34
  50.2 2.4 %copy-start.10 = (bf16[512,4096]{1,0:T(8,128)(2,1)S(1)}, bf16[512,4096]{1,0:T(8,128)(2,1)}, u32[]{:S(2)}) copy-start(bf16[512,4096]{1,0:T(8,128)(2,1)} %weight_ref.1) | copy-start | bytes 12582916
  52.6 14.7 %copy-start = (bf16[512,512]{1,0:T(8,128)(2,1)S(1)}, bf16[512,512]{1,0:T(8,128)(2,1)}, u32[]{:S(2)}) copy-start(bf16[512,512]{1,0:T(8,128)(2,1)} %key_ref.3) | copy-start | bytes 1572868
  52.6 14.7 %copy-start.1 = (bf16[512,512]{1,0:T(8,128)(2,1)S(1)}, bf16[512,512]{1,0:T(8,128)(2,1)}, u32[]{:S(2)}) copy-start(bf16[512,512]{1,0:T(8,128)(2,1)} %value_ref.3) | copy-start | bytes 1572868
  52.6 14.7 %copy-start.2 = (bf16[512,512]{1,0:T(8,128)(2,1)S(1)}, bf16[512,512]{1,0:T(8,128)(2,1)}, u32[]{:S(2)}) copy-start(bf16[512,512]{1,0:T(8,128)(2,1)} %query_ref.1) | copy-start | bytes 1572868
  52.6 14.7 %copy-start.3 = (f32[512]{0:T(512)S(1)}, f32[512]{0:T(512)}, u32[]{:S(2)}) copy-start(f32[512]{0:T(512)} %param.16) | copy-start | bytes 6148
  67.3 2.7 %copy-start.15 = (bf16[512,512]{1,0:T(8,128)(2,1)S(1)}, bf16[512,512]{1,0:T(8,128)(2,1)}, u32[]{:S(2)}) copy-start(bf16[512,512]{1,0:T(8,128)(2,1)} %get-tuple-element.51) | copy-start | bytes 1572868
  67.3 7.1 %copy-start.16 = (bf16[512,512]{1,0:T(8,128)(2,1)S(1)}, bf16[512,512]{1,0:T(8,128)(2,1)}, u32[]{:S(2)}) copy-start(bf16[512,512]{1,0:T(8,128)(2,1)} %get-tuple-element.44) | copy-start | bytes 1572868
  68.2 18.1 %collective-permute-start = (f32[256,512]{1,0:T(8,128)S(1)}, f32[256,512]{1,0:T(8,128)S(1)}, u32[]{:S(2)}, u32[]{:S(2)}) collective-permute-start(f32[256,512]{1,0:T(8,128)S(1)} %fusion.6), channel_id=1, source_target_pairs={{0,1},{1,2},{2,3},{3,4},{4,5},{5,6},{6,7},{7,0},{8,9},{9,10},{10,1... | collective-permute-start | bytes 1572872 | tf_op jit(solution)/shard_map/ppermute | solution.py:231
  70.3 27.4 %copy-start.14 = (bf16[512,512]{1,0:T(8,128)(2,1)S(1)}, bf16[512,512]{1,0:T(8,128)(2,1)}, u32[]{:S(2)}) copy-start(bf16[512,512]{1,0:T(8,128)(2,1)} %get-tuple-element.47) | copy-start | bytes 1572868
  70.3 16.6 %collective-permute-start.10 = (f32[256,512]{1,0:T(8,128)S(1)}, f32[256,512]{1,0:T(8,128)S(1)}, u32[]{:S(2)}, u32[]{:S(2)}) collective-permute-start(f32[256,512]{1,0:T(8,128)S(1)} %fusion), channel_id=1, source_target_pairs={{0,7},{1,0},{2,1},{3,2},{4,3},{5,4},{6,5},{7,6},{8,15},{9,8},{10,9... | collective-permute-start | bytes 1572872 | tf_op jit(solution)/shard_map/ppermute | solution.py:231
  74.6 23.0 %collective-permute-start.7 = (f32[256,512]{1,0:T(8,128)S(1)}, f32[256,512]{1,0:T(8,128)S(1)}, u32[]{:S(2)}, u32[]{:S(2)}) collective-permute-start(f32[256,512]{1,0:T(8,128)S(1)} %fusion.2), channel_id=1, source_target_pairs={{0,1},{1,2},{2,3},{3,4},{4,5},{5,6},{6,7},{7,0},{8,9},{9,10},{10,1... | collective-permute-start | bytes 1572872 | tf_op jit(solution)/shard_map/ppermute | solution.py:231
  74.8 23.4 %collective-permute-start.4 = (f32[256,512]{1,0:T(8,128)S(1)}, f32[256,512]{1,0:T(8,128)S(1)}, u32[]{:S(2)}, u32[]{:S(2)}) collective-permute-start(f32[256,512]{1,0:T(8,128)S(1)} %fusion.4), channel_id=1, source_target_pairs={{0,7},{1,0},{2,1},{3,2},{4,3},{5,4},{6,5},{7,6},{8,15},{9,8},{10,9... | collective-permute-start | bytes 1572872 | tf_op jit(solution)/shard_map/ppermute | solution.py:231
  86.4 11.7 %copy-start.13 = (bf16[512,512]{1,0:T(8,128)(2,1)S(1)}, bf16[512,512]{1,0:T(8,128)(2,1)}, u32[]{:S(2)}) copy-start(bf16[512,512]{1,0:T(8,128)(2,1)} %get-tuple-element.54) | copy-start | bytes 1572868
  86.8 22.1 %collective-permute-start.1 = (f32[256,512]{1,0:T(8,128)S(1)}, f32[256,512]{1,0:T(8,128)S(1)}, u32[]{:S(2)}, u32[]{:S(2)}) collective-permute-start(f32[256,512]{1,0:T(8,128)S(1)} %add.131), channel_id=1, source_target_pairs={{0,1},{1,2},{2,3},{3,4},{4,5},{5,6},{6,7},{7,0},{8,9},{9,10},{10,1... | collective-permute-start | bytes 1572872 | tf_op jit(solution)/shard_map/ppermute | solution.py:231
  87.3 22.1 %collective-permute-start.11 = (f32[256,512]{1,0:T(8,128)S(1)}, f32[256,512]{1,0:T(8,128)S(1)}, u32[]{:S(2)}, u32[]{:S(2)}) collective-permute-start(f32[256,512]{1,0:T(8,128)S(1)} %add.140), channel_id=1, source_target_pairs={{0,7},{1,0},{2,1},{3,2},{4,3},{5,4},{6,5},{7,6},{8,15},{9,8},{10,9... | collective-permute-start | bytes 1572872 | tf_op jit(solution)/shard_map/ppermute | solution.py:231
  98.0 22.1 %copy-start.11 = (bf16[512,512]{1,0:T(8,128)(2,1)S(1)}, bf16[512,512]{1,0:T(8,128)(2,1)}, u32[]{:S(2)}) copy-start(bf16[512,512]{1,0:T(8,128)(2,1)} %get-tuple-element.50) | copy-start | bytes 1572868
  98.0 22.1 %collective-permute-start.8 = (f32[256,512]{1,0:T(8,128)S(1)}, f32[256,512]{1,0:T(8,128)S(1)}, u32[]{:S(2)}, u32[]{:S(2)}) collective-permute-start(f32[256,512]{1,0:T(8,128)S(1)} %add.138), channel_id=1, source_target_pairs={{0,1},{1,2},{2,3},{3,4},{4,5},{5,6},{6,7},{7,0},{8,9},{9,10},{10,1... | collective-permute-start | bytes 1572872 | tf_op jit(solution)/shard_map/ppermute | solution.py:231
  98.5 22.1 %copy-start.12 = (bf16[512,512]{1,0:T(8,128)(2,1)S(1)}, bf16[512,512]{1,0:T(8,128)(2,1)}, u32[]{:S(2)}) copy-start(bf16[512,512]{1,0:T(8,128)(2,1)} %get-tuple-element.57) | copy-start | bytes 1572868
  98.5 22.1 %collective-permute-start.5 = (f32[256,512]{1,0:T(8,128)S(1)}, f32[256,512]{1,0:T(8,128)S(1)}, u32[]{:S(2)}, u32[]{:S(2)}) collective-permute-start(f32[256,512]{1,0:T(8,128)S(1)} %add.134), channel_id=1, source_target_pairs={{0,7},{1,0},{2,1},{3,2},{4,3},{5,4},{6,5},{7,6},{8,15},{9,8},{10,9... | collective-permute-start | bytes 1572872 | tf_op jit(solution)/shard_map/ppermute | solution.py:231
  109.3 22.1 %collective-permute-start.2 = (f32[256,512]{1,0:T(8,128)S(1)}, f32[256,512]{1,0:T(8,128)S(1)}, u32[]{:S(2)}, u32[]{:S(2)}) collective-permute-start(f32[256,512]{1,0:T(8,128)S(1)} %add.132), channel_id=1, source_target_pairs={{0,1},{1,2},{2,3},{3,4},{4,5},{5,6},{6,7},{7,0},{8,9},{9,10},{10,1... | collective-permute-start | bytes 1572872 | tf_op jit(solution)/shard_map/ppermute | solution.py:231
  109.7 21.6 %collective-permute-start.12 = (f32[256,512]{1,0:T(8,128)S(1)}, f32[256,512]{1,0:T(8,128)S(1)}, u32[]{:S(2)}, u32[]{:S(2)}) collective-permute-start(f32[256,512]{1,0:T(8,128)S(1)} %add.141), channel_id=1, source_target_pairs={{0,7},{1,0},{2,1},{3,2},{4,3},{5,4},{6,5},{7,6},{8,15},{9,8},{10,9... | collective-permute-start | bytes 1572872 | tf_op jit(solution)/shard_map/ppermute | solution.py:231
  120.5 32.2 %copy-start.17 = (bf16[512,512]{1,0:T(8,128)(2,1)S(1)}, bf16[512,512]{1,0:T(8,128)(2,1)}, u32[]{:S(2)}) copy-start(bf16[512,512]{1,0:T(8,128)(2,1)} %get-tuple-element.61) | copy-start | bytes 1572868
  120.5 22.1 %collective-permute-start.9 = (f32[256,512]{1,0:T(8,128)S(1)}, f32[256,512]{1,0:T(8,128)S(1)}, u32[]{:S(2)}, u32[]{:S(2)}) collective-permute-start(f32[256,512]{1,0:T(8,128)S(1)} %add.139), channel_id=1, source_target_pairs={{0,1},{1,2},{2,3},{3,4},{4,5},{5,6},{6,7},{7,0},{8,9},{9,10},{10,1... | collective-permute-start | bytes 1572872 | tf_op jit(solution)/shard_map/ppermute | solution.py:231
  121.0 31.7 %collective-permute-start.6 = (f32[256,512]{1,0:T(8,128)S(1)}, f32[256,512]{1,0:T(8,128)S(1)}, u32[]{:S(2)}, u32[]{:S(2)}) collective-permute-start(f32[256,512]{1,0:T(8,128)S(1)} %add.135), channel_id=1, source_target_pairs={{0,7},{1,0},{2,1},{3,2},{4,3},{5,4},{6,5},{7,6},{8,15},{9,8},{10,9... | collective-permute-start | bytes 1572872 | tf_op jit(solution)/shard_map/ppermute | solution.py:231
  131.7 21.0 %collective-permute-start.13 = (f32[256,512]{1,0:T(8,128)S(1)}, f32[256,512]{1,0:T(8,128)S(1)}, u32[]{:S(2)}, u32[]{:S(2)}) collective-permute-start(f32[256,512]{1,0:T(8,128)S(1)} %add.142), channel_id=1, source_target_pairs={{0,7},{1,0},{2,1},{3,2},{4,3},{5,4},{6,5},{7,6},{8,15},{9,8},{10,9... | collective-permute-start | bytes 1572872 | tf_op jit(solution)/shard_map/ppermute | solution.py:231
  135.2 17.5 %collective-permute-start.3 = (f32[256,512]{1,0:T(8,128)S(1)}, f32[256,512]{1,0:T(8,128)S(1)}, u32[]{:S(2)}, u32[]{:S(2)}) collective-permute-start(f32[256,512]{1,0:T(8,128)S(1)} %add.133), channel_id=1, source_target_pairs={{0,1},{1,2},{2,3},{3,4},{4,5},{5,6},{6,7},{7,0},{8,9},{9,10},{10,1... | collective-permute-start | bytes 1572872 | tf_op jit(solution)/shard_map/ppermute | solution.py:231

commit v9 on v8

--- a/solution.py
+++ b/solution.py
@@ -25,7 +25,7 @@
 
 def exchange_order(n_parts):
     gray = (0, 1, 3, 2)
-    order = [(gray[y] * SIDE + gray[x]) * CORES + c for y in range(SIDE) for x in range(SIDE) for c in range(CORES)]
+    order = [(y * SIDE + gray[x]) * CORES + c for y in range(SIDE) for x in range(SIDE) for c in range(CORES)]
     return order if len(order) == n_parts else list(range(n_parts))
 
 

time: 154 us -> 155 us (level)
  no operation moved by 1% of the time
where the time goes in v9:
time: 155 us; the launch traced here: 154 us
  waiting for transfers between devices  69.4 us (45%)
  blocking collectives  37 us (24%)
  starting transfers between devices  27.3 us (18%)
  Pallas kernels  11.4 us (7%)
  matrix products  4.75 us (3%)
  local copies, waits for them, and re-layouts  3.13 us (2%)
    ppermute x14, waiting for transfers between devices, ring_sum(): got = lax.ppermute(total, 'chan', hops)  56.4 us
    all_to_all x1, blocking collectives, exchange(): lax.all_to_all(value, 'seq', split_axis=0, concat_axis=0, tiled=True, axi...  37 us
    ppermute x14, starting transfers between devices, ring_sum(): got = lax.ppermute(total, 'chan', hops)  23.2 us
    all_to_all x1, waiting for transfers between devices, exchange(): lax.all_to_all(value, 'seq', split_axis=0, concat_axis=0, tiled=True, axi...  13 us
    pallas_call x1, Pallas kernels, convolve(): pl.pallas_call(lambda *refs: conv_kernel(n_parts, width, group, *refs), o...  6.89 us
    dot_general x16, matrix products, dot(): return jnp.dot(left, right, preferred_element_type=F32)  4.75 us
    all_to_all x1, starting transfers between devices, exchange(): lax.all_to_all(value, 'seq', split_axis=0, concat_axis=0, tiled=True, axi...  4.07 us
  transfers between devices with their start and end apart: 15, of which 8 were waited for; matrix products, arithmetic and copies ran while one was open for 4% of the time, Pallas kernels for 1%

profile of v9, /device:TPU:1, one launch (start us, length us, event | category | flops | bytes accessed | tf_op | source)
XLA Modules:
  0.0 154.3 jit_solution(12159076762233040297)
XLA Ops:
  0.0 2.1 %pack.1 = f32[32,2,4,16,128]{4,3,2,1,0:T(8,128)S(1)} custom-call(bf16[512,512]{1,0:T(8,128)(2,1)} %key_ref.3, bf16[512,512]{1,0:T(8,128)(2,1)} %value_ref.3, f32[512,512]{1,0:T(8,128)} %taps_ref.1), custom_call_target="tpu_custom_call" | custom-call | tf_op jit(solution)/shard_map/pack/pallas_call | solution.py:113
  2.2 37.0 %all_to_all.10 = f32[32,2,4,16,128]{4,3,2,1,0:T(8,128)S(1)} all-to-all(f32[32,2,4,16,128]{4,3,2,1,0:T(8,128)S(1)} %pack.1), channel_id=1, replica_groups={{0,8,16,24,48,56,32,40,64,72,80,88,112,120,96,104,128,136,144,152,176,1..., dimensions={0} | all-to-all | bytes 4194304 | tf_op jit(solution)/shard_map/all_to_all | solution.py:34
  39.2 6.9 %convolve.1 = f32[2048,128]{1,0:T(8,128)} custom-call(f32[4096,128]{1,0:T(8,128)S(1)} %bitcast.32, bf16[256,384]{1,0:T(8,128)(2,1)S(1)} %copy-done.7, f32[128,128]{1,0:T(8,128)S(1)} %copy-done.9, f32[128,128]{1,0:T(8,128)S(1)} %copy-done.8, bf16[768,256]{1,0:T(8,128)(2,1)S(1)} %copy-done.5, bf16[768,256]{1,0:T(8,128)(2,1)S(1)} %copy-done.4, ...), custom_call_target="tpu_custom_call" | custom-call | flops 3623878656 | bytes 3145728 | tf_op jit(solution)/shard_map/convolve/pallas_call | solution.py:175
  46.1 4.1 %all-to-all-start.1 = ((f32[32,4,16,128]{3,2,1,0:T(8,128)}), f32[32,4,16,128]{3,2,1,0:T(8,128)S(1)}, u32[]{:S(2)}, u32[]{:S(2)}) async-start(f32[32,4,16,128]{3,2,1,0:T(8,128)} %bitcast.1), calls=%async_computation.1 | async-start | bytes 2097152 | tf_op jit(solution)/shard_map/all_to_all | solution.py:34
  50.3 1.2 columns.1
  51.5 1.1 copy-done.10
  52.6 1.9 %constant_dynamic-slice_fusion = (bf16[512,512]{1,0:T(8,128)(2,1)}, bf16[512,512]{1,0:T(8,128)(2,1)}, bf16[512,512]{1,0:T(8,128)(2,1)}, bf16[512,512]{1,0:T(8,12...) fusion(bf16[512,4096]{1,0:T(8,128)(2,1)S(1)} %copy-done.10, ...), kind=kLoop, calls=%fused_computation.2 | loop fusion | bytes 7340060 | tf_op jit(solution)/shard_map/dynamic_slice | solution.py:269
  54.5 13.0 %all-to-all-done.1.conv_ref = f32[32,4,16,128]{3,2,1,0:T(8,128)S(1)} async-done(((f32[32,4,16,128]{3,2,1,0:T(8,128)}), f32[32,4,16,128]{3,2,1,0:T(8,128)S(1)}, u32[]{:S(2)}, u32[]{:S(2)}) %all-to-all-start.1) | async-done | bytes 1048608 | tf_op jit(solution)/shard_map/all_to_all | solution.py:34
  67.6 0.3 gate.1
  67.9 0.3 fusion
  68.2 0.3 fusion.6
  68.5 1.7 %collective-permute-start = (f32[256,512]{1,0:T(8,128)S(1)}, f32[256,512]{1,0:T(8,128)S(1)}, u32[]{:S(2)}, u32[]{:S(2)}) collective-permute-start(f32[256,512]{1,0:T(8,128)S(1)} %fusion.6), channel_id=1, source_target_pairs={{0,1},{1,2},{2,3},{3,4},{4,5},{5,6},{6,7},{7,0},{8,9},{9,10},{10,1... | collective-permute-start | bytes 1572872 | tf_op jit(solution)/shard_map/ppermute | solution.py:231
  70.2 0.3 fusion.4
  70.5 4.0 %collective-permute-start.10 = (f32[256,512]{1,0:T(8,128)S(1)}, f32[256,512]{1,0:T(8,128)S(1)}, u32[]{:S(2)}, u32[]{:S(2)}) collective-permute-start(f32[256,512]{1,0:T(8,128)S(1)} %fusion), channel_id=1, source_target_pairs={{0,7},{1,0},{2,1},{3,2},{4,3},{5,4},{6,5},{7,6},{8,15},{9,8},{10,9... | collective-permute-start | bytes 1572872 | tf_op jit(solution)/shard_map/ppermute | solution.py:231
  74.6 0.3 fusion.2
  74.9 0.1 collective-permute-start.7
  75.0 2.9 %collective-permute-start.4 = (f32[256,512]{1,0:T(8,128)S(1)}, f32[256,512]{1,0:T(8,128)S(1)}, u32[]{:S(2)}, u32[]{:S(2)}) collective-permute-start(f32[256,512]{1,0:T(8,128)S(1)} %fusion.4), channel_id=1, source_target_pairs={{0,7},{1,0},{2,1},{3,2},{4,3},{5,4},{6,5},{7,6},{8,15},{9,8},{10,9... | collective-permute-start | bytes 1572872 | tf_op jit(solution)/shard_map/ppermute | solution.py:231
  78.0 8.7 %collective-permute-done = f32[256,512]{1,0:T(8,128)S(1)} collective-permute-done((f32[256,512]{1,0:T(8,128)S(1)}, f32[256,512]{1,0:T(8,128)S(1)}, u32[]{:S(2)}, u32[]{:S(2)}) %collective-permute-start) | collective-permute-done | bytes 524320 | tf_op jit(solution)/shard_map/ppermute | solution.py:231
  86.7 0.3 fusion.9
  87.1 0.1 collective-permute-start.1
  87.2 0.3 fusion.16
  87.5 0.1 add.140
  87.6 2.7 %collective-permute-start.11 = (f32[256,512]{1,0:T(8,128)S(1)}, f32[256,512]{1,0:T(8,128)S(1)}, u32[]{:S(2)}, u32[]{:S(2)}) collective-permute-start(f32[256,512]{1,0:T(8,128)S(1)} %add.140), channel_id=1, source_target_pairs={{0,7},{1,0},{2,1},{3,2},{4,3},{5,4},{6,5},{7,6},{8,15},{9,8},{10,9... | collective-permute-start | bytes 1572872 | tf_op jit(solution)/shard_map/ppermute | solution.py:231
  90.3 7.6 %collective-permute-done.7 = f32[256,512]{1,0:T(8,128)S(1)} collective-permute-done((f32[256,512]{1,0:T(8,128)S(1)}, f32[256,512]{1,0:T(8,128)S(1)}, u32[]{:S(2)}, u32[]{:S(2)}) %collective-permute-start.7) | collective-permute-done | bytes 524320 | tf_op jit(solution)/shard_map/ppermute | solution.py:231
  97.9 0.3 fusion.14
  98.3 0.1 collective-permute-start.8
  98.4 0.3 fusion.12
  98.8 2.7 %collective-permute-start.5 = (f32[256,512]{1,0:T(8,128)S(1)}, f32[256,512]{1,0:T(8,128)S(1)}, u32[]{:S(2)}, u32[]{:S(2)}) collective-permute-start(f32[256,512]{1,0:T(8,128)S(1)} %add.134), channel_id=1, source_target_pairs={{0,7},{1,0},{2,1},{3,2},{4,3},{5,4},{6,5},{7,6},{8,15},{9,8},{10,9... | collective-permute-start | bytes 1572872 | tf_op jit(solution)/shard_map/ppermute | solution.py:231
  101.6 7.6 %collective-permute-done.1 = f32[256,512]{1,0:T(8,128)S(1)} collective-permute-done((f32[256,512]{1,0:T(8,128)S(1)}, f32[256,512]{1,0:T(8,128)S(1)}, u32[]{:S(2)}, u32[]{:S(2)}) %collective-permute-start.1) | collective-permute-done | bytes 524320 | tf_op jit(solution)/shard_map/ppermute | solution.py:231
  109.2 0.3 fusion.10
  109.5 0.1 collective-permute-start.2
  109.6 0.3 fusion.17
  110.0 2.7 %collective-permute-start.12 = (f32[256,512]{1,0:T(8,128)S(1)}, f32[256,512]{1,0:T(8,128)S(1)}, u32[]{:S(2)}, u32[]{:S(2)}) collective-permute-start(f32[256,512]{1,0:T(8,128)S(1)} %add.141), channel_id=1, source_target_pairs={{0,7},{1,0},{2,1},{3,2},{4,3},{5,4},{6,5},{7,6},{8,15},{9,8},{10,9... | collective-permute-start | bytes 1572872 | tf_op jit(solution)/shard_map/ppermute | solution.py:231
  112.8 7.6 %collective-permute-done.8 = f32[256,512]{1,0:T(8,128)S(1)} collective-permute-done((f32[256,512]{1,0:T(8,128)S(1)}, f32[256,512]{1,0:T(8,128)S(1)}, u32[]{:S(2)}, u32[]{:S(2)}) %collective-permute-start.8) | collective-permute-done | bytes 524320 | tf_op jit(solution)/shard_map/ppermute | solution.py:231
  120.4 0.3 fusion.15
  120.7 0.1 add.139
  120.9 0.3 fusion.13
  121.2 0.1 add.135
  121.3 2.7 %collective-permute-start.6 = (f32[256,512]{1,0:T(8,128)S(1)}, f32[256,512]{1,0:T(8,128)S(1)}, u32[]{:S(2)}, u32[]{:S(2)}) collective-permute-start(f32[256,512]{1,0:T(8,128)S(1)} %add.135), channel_id=1, source_target_pairs={{0,7},{1,0},{2,1},{3,2},{4,3},{5,4},{6,5},{7,6},{8,15},{9,8},{10,9... | collective-permute-start | bytes 1572872 | tf_op jit(solution)/shard_map/ppermute | solution.py:231
  124.0 7.6 %collective-permute-done.2 = f32[256,512]{1,0:T(8,128)S(1)} collective-permute-done((f32[256,512]{1,0:T(8,128)S(1)}, f32[256,512]{1,0:T(8,128)S(1)}, u32[]{:S(2)}, u32[]{:S(2)}) %collective-permute-start.2) | collective-permute-done | bytes 524320 | tf_op jit(solution)/shard_map/ppermute | solution.py:231
  131.6 0.3 fusion.18
  132.0 3.1 %collective-permute-start.13 = (f32[256,512]{1,0:T(8,128)S(1)}, f32[256,512]{1,0:T(8,128)S(1)}, u32[]{:S(2)}, u32[]{:S(2)}) collective-permute-start(f32[256,512]{1,0:T(8,128)S(1)} %add.142), channel_id=1, source_target_pairs={{0,7},{1,0},{2,1},{3,2},{4,3},{5,4},{6,5},{7,6},{8,15},{9,8},{10,9... | collective-permute-start | bytes 1572872 | tf_op jit(solution)/shard_map/ppermute | solution.py:231
  135.1 0.3 fusion.11
  135.6 7.2 %collective-permute-done.9 = f32[256,512]{1,0:T(8,128)S(1)} collective-permute-done((f32[256,512]{1,0:T(8,128)S(1)}, f32[256,512]{1,0:T(8,128)S(1)}, u32[]{:S(2)}, u32[]{:S(2)}) %collective-permute-start.9) | collective-permute-done | bytes 524320 | tf_op jit(solution)/shard_map/ppermute | solution.py:231
  142.9 10.0 %collective-permute-done.13 = f32[256,512]{1,0:T(8,128)S(1)} collective-permute-done((f32[256,512]{1,0:T(8,128)S(1)}, f32[256,512]{1,0:T(8,128)S(1)}, u32[]{:S(2)}, u32[]{:S(2)}) %collective-permute-start.13) | collective-permute-done | bytes 524320 | tf_op jit(solution)/shard_map/ppermute | solution.py:231
  152.9 0.3 add_convert_fusion.lower_ref
  153.2 0.3 add_convert_fusion.1.upper_ref
  153.5 0.8 join.1
  (52 shorter events, 0.9 us)
Async XLA Ops:
  0.0 39.2 %copy-start.4 = (bf16[768,256]{1,0:T(8,128)(2,1)S(1)}, bf16[768,256]{1,0:T(8,128)(2,1)}, u32[]{:S(2)}) copy-start(bf16[768,256]{1,0:T(8,128)(2,1)} %constant.79.clone.refs_5_) | copy-start | bytes 1179652
  0.0 39.2 %copy-start.5 = (bf16[768,256]{1,0:T(8,128)(2,1)S(1)}, bf16[768,256]{1,0:T(8,128)(2,1)}, u32[]{:S(2)}) copy-start(bf16[768,256]{1,0:T(8,128)(2,1)} %constant.78.clone.refs_4_) | copy-start | bytes 1179652
  0.0 39.2 %copy-start.6 = (bf16[128,768]{1,0:T(8,128)(2,1)S(1)}, bf16[128,768]{1,0:T(8,128)(2,1)}, u32[]{:S(2)}) copy-start(bf16[128,768]{1,0:T(8,128)(2,1)} %constant.80.clone.refs_6_) | copy-start | bytes 589828
  0.0 39.2 %copy-start.7 = (bf16[256,384]{1,0:T(8,128)(2,1)S(1)}, bf16[256,384]{1,0:T(8,128)(2,1)}, u32[]{:S(2)}) copy-start(bf16[256,384]{1,0:T(8,128)(2,1)} %constant.77.clone.refs_1_) | copy-start | bytes 589828
  0.0 39.2 %copy-start.8 = (f32[128,128]{1,0:T(8,128)S(1)}, f32[128,128]{1,0:T(8,128)}, u32[]{:S(2)}) copy-start(f32[128,128]{1,0:T(8,128)} %constant.76.clone.refs_3_) | copy-start | bytes 196612
  0.0 39.2 %copy-start.9 = (f32[128,128]{1,0:T(8,128)S(1)}, f32[128,128]{1,0:T(8,128)}, u32[]{:S(2)}) copy-start(f32[128,128]{1,0:T(8,128)} %constant.75.clone.refs_2_) | copy-start | bytes 196612
  46.1 21.4 %all-to-all-start.1 = ((f32[32,4,16,128]{3,2,1,0:T(8,128)}), f32[32,4,16,128]{3,2,1,0:T(8,128)S(1)}, u32[]{:S(2)}, u32[]{:S(2)}) async-start(f32[32,4,16,128]{3,2,1,0:T(8,128)} %bitcast.1), calls=%async_computation.1 | async-start | bytes 2097152 | tf_op jit(solution)/shard_map/all_to_all | solution.py:34
  50.3 2.4 %copy-start.10 = (bf16[512,4096]{1,0:T(8,128)(2,1)S(1)}, bf16[512,4096]{1,0:T(8,128)(2,1)}, u32[]{:S(2)}) copy-start(bf16[512,4096]{1,0:T(8,128)(2,1)} %weight_ref.1) | copy-start | bytes 12582916
  52.6 14.9 %copy-start = (bf16[512,512]{1,0:T(8,128)(2,1)S(1)}, bf16[512,512]{1,0:T(8,128)(2,1)}, u32[]{:S(2)}) copy-start(bf16[512,512]{1,0:T(8,128)(2,1)} %key_ref.3) | copy-start | bytes 1572868
  52.6 14.9 %copy-start.1 = (bf16[512,512]{1,0:T(8,128)(2,1)S(1)}, bf16[512,512]{1,0:T(8,128)(2,1)}, u32[]{:S(2)}) copy-start(bf16[512,512]{1,0:T(8,128)(2,1)} %value_ref.3) | copy-start | bytes 1572868
  52.6 14.9 %copy-start.2 = (bf16[512,512]{1,0:T(8,128)(2,1)S(1)}, bf16[512,512]{1,0:T(8,128)(2,1)}, u32[]{:S(2)}) copy-start(bf16[512,512]{1,0:T(8,128)(2,1)} %query_ref.1) | copy-start | bytes 1572868
  52.6 14.9 %copy-start.3 = (f32[512]{0:T(512)S(1)}, f32[512]{0:T(512)}, u32[]{:S(2)}) copy-start(f32[512]{0:T(512)} %param.16) | copy-start | bytes 6148
  67.5 2.7 %copy-start.15 = (bf16[512,512]{1,0:T(8,128)(2,1)S(1)}, bf16[512,512]{1,0:T(8,128)(2,1)}, u32[]{:S(2)}) copy-start(bf16[512,512]{1,0:T(8,128)(2,1)} %get-tuple-element.51) | copy-start | bytes 1572868
  67.5 7.1 %copy-start.16 = (bf16[512,512]{1,0:T(8,128)(2,1)S(1)}, bf16[512,512]{1,0:T(8,128)(2,1)}, u32[]{:S(2)}) copy-start(bf16[512,512]{1,0:T(8,128)(2,1)} %get-tuple-element.44) | copy-start | bytes 1572868
  68.5 18.2 %collective-permute-start = (f32[256,512]{1,0:T(8,128)S(1)}, f32[256,512]{1,0:T(8,128)S(1)}, u32[]{:S(2)}, u32[]{:S(2)}) collective-permute-start(f32[256,512]{1,0:T(8,128)S(1)} %fusion.6), channel_id=1, source_target_pairs={{0,1},{1,2},{2,3},{3,4},{4,5},{5,6},{6,7},{7,0},{8,9},{9,10},{10,1... | collective-permute-start | bytes 1572872 | tf_op jit(solution)/shard_map/ppermute | solution.py:231
  70.5 27.4 %copy-start.14 = (bf16[512,512]{1,0:T(8,128)(2,1)S(1)}, bf16[512,512]{1,0:T(8,128)(2,1)}, u32[]{:S(2)}) copy-start(bf16[512,512]{1,0:T(8,128)(2,1)} %get-tuple-element.47) | copy-start | bytes 1572868
  70.5 16.6 %collective-permute-start.10 = (f32[256,512]{1,0:T(8,128)S(1)}, f32[256,512]{1,0:T(8,128)S(1)}, u32[]{:S(2)}, u32[]{:S(2)}) collective-permute-start(f32[256,512]{1,0:T(8,128)S(1)} %fusion), channel_id=1, source_target_pairs={{0,7},{1,0},{2,1},{3,2},{4,3},{5,4},{6,5},{7,6},{8,15},{9,8},{10,9... | collective-permute-start | bytes 1572872 | tf_op jit(solution)/shard_map/ppermute | solution.py:231
  74.9 23.0 %collective-permute-start.7 = (f32[256,512]{1,0:T(8,128)S(1)}, f32[256,512]{1,0:T(8,128)S(1)}, u32[]{:S(2)}, u32[]{:S(2)}) collective-permute-start(f32[256,512]{1,0:T(8,128)S(1)} %fusion.2), channel_id=1, source_target_pairs={{0,1},{1,2},{2,3},{3,4},{4,5},{5,6},{6,7},{7,0},{8,9},{9,10},{10,1... | collective-permute-start | bytes 1572872 | tf_op jit(solution)/shard_map/ppermute | solution.py:231
  75.0 23.4 %collective-permute-start.4 = (f32[256,512]{1,0:T(8,128)S(1)}, f32[256,512]{1,0:T(8,128)S(1)}, u32[]{:S(2)}, u32[]{:S(2)}) collective-permute-start(f32[256,512]{1,0:T(8,128)S(1)} %fusion.4), channel_id=1, source_target_pairs={{0,7},{1,0},{2,1},{3,2},{4,3},{5,4},{6,5},{7,6},{8,15},{9,8},{10,9... | collective-permute-start | bytes 1572872 | tf_op jit(solution)/shard_map/ppermute | solution.py:231
  86.7 11.7 %copy-start.13 = (bf16[512,512]{1,0:T(8,128)(2,1)S(1)}, bf16[512,512]{1,0:T(8,128)(2,1)}, u32[]{:S(2)}) copy-start(bf16[512,512]{1,0:T(8,128)(2,1)} %get-tuple-element.54) | copy-start | bytes 1572868
  87.1 22.1 %collective-permute-start.1 = (f32[256,512]{1,0:T(8,128)S(1)}, f32[256,512]{1,0:T(8,128)S(1)}, u32[]{:S(2)}, u32[]{:S(2)}) collective-permute-start(f32[256,512]{1,0:T(8,128)S(1)} %add.131), channel_id=1, source_target_pairs={{0,1},{1,2},{2,3},{3,4},{4,5},{5,6},{6,7},{7,0},{8,9},{9,10},{10,1... | collective-permute-start | bytes 1572872 | tf_op jit(solution)/shard_map/ppermute | solution.py:231
  87.6 22.1 %collective-permute-start.11 = (f32[256,512]{1,0:T(8,128)S(1)}, f32[256,512]{1,0:T(8,128)S(1)}, u32[]{:S(2)}, u32[]{:S(2)}) collective-permute-start(f32[256,512]{1,0:T(8,128)S(1)} %add.140), channel_id=1, source_target_pairs={{0,7},{1,0},{2,1},{3,2},{4,3},{5,4},{6,5},{7,6},{8,15},{9,8},{10,9... | collective-permute-start | bytes 1572872 | tf_op jit(solution)/shard_map/ppermute | solution.py:231
  98.3 22.1 %copy-start.11 = (bf16[512,512]{1,0:T(8,128)(2,1)S(1)}, bf16[512,512]{1,0:T(8,128)(2,1)}, u32[]{:S(2)}) copy-start(bf16[512,512]{1,0:T(8,128)(2,1)} %get-tuple-element.50) | copy-start | bytes 1572868
  98.3 22.1 %collective-permute-start.8 = (f32[256,512]{1,0:T(8,128)S(1)}, f32[256,512]{1,0:T(8,128)S(1)}, u32[]{:S(2)}, u32[]{:S(2)}) collective-permute-start(f32[256,512]{1,0:T(8,128)S(1)} %add.138), channel_id=1, source_target_pairs={{0,1},{1,2},{2,3},{3,4},{4,5},{5,6},{6,7},{7,0},{8,9},{9,10},{10,1... | collective-permute-start | bytes 1572872 | tf_op jit(solution)/shard_map/ppermute | solution.py:231
  98.8 22.1 %copy-start.12 = (bf16[512,512]{1,0:T(8,128)(2,1)S(1)}, bf16[512,512]{1,0:T(8,128)(2,1)}, u32[]{:S(2)}) copy-start(bf16[512,512]{1,0:T(8,128)(2,1)} %get-tuple-element.57) | copy-start | bytes 1572868
  98.8 22.1 %collective-permute-start.5 = (f32[256,512]{1,0:T(8,128)S(1)}, f32[256,512]{1,0:T(8,128)S(1)}, u32[]{:S(2)}, u32[]{:S(2)}) collective-permute-start(f32[256,512]{1,0:T(8,128)S(1)} %add.134), channel_id=1, source_target_pairs={{0,7},{1,0},{2,1},{3,2},{4,3},{5,4},{6,5},{7,6},{8,15},{9,8},{10,9... | collective-permute-start | bytes 1572872 | tf_op jit(solution)/shard_map/ppermute | solution.py:231
  109.5 22.1 %collective-permute-start.2 = (f32[256,512]{1,0:T(8,128)S(1)}, f32[256,512]{1,0:T(8,128)S(1)}, u32[]{:S(2)}, u32[]{:S(2)}) collective-permute-start(f32[256,512]{1,0:T(8,128)S(1)} %add.132), channel_id=1, source_target_pairs={{0,1},{1,2},{2,3},{3,4},{4,5},{5,6},{6,7},{7,0},{8,9},{9,10},{10,1... | collective-permute-start | bytes 1572872 | tf_op jit(solution)/shard_map/ppermute | solution.py:231
  110.0 21.6 %collective-permute-start.12 = (f32[256,512]{1,0:T(8,128)S(1)}, f32[256,512]{1,0:T(8,128)S(1)}, u32[]{:S(2)}, u32[]{:S(2)}) collective-permute-start(f32[256,512]{1,0:T(8,128)S(1)} %add.141), channel_id=1, source_target_pairs={{0,7},{1,0},{2,1},{3,2},{4,3},{5,4},{6,5},{7,6},{8,15},{9,8},{10,9... | collective-permute-start | bytes 1572872 | tf_op jit(solution)/shard_map/ppermute | solution.py:231
  120.8 32.1 %copy-start.17 = (bf16[512,512]{1,0:T(8,128)(2,1)S(1)}, bf16[512,512]{1,0:T(8,128)(2,1)}, u32[]{:S(2)}) copy-start(bf16[512,512]{1,0:T(8,128)(2,1)} %get-tuple-element.61) | copy-start | bytes 1572868
  120.8 22.1 %collective-permute-start.9 = (f32[256,512]{1,0:T(8,128)S(1)}, f32[256,512]{1,0:T(8,128)S(1)}, u32[]{:S(2)}, u32[]{:S(2)}) collective-permute-start(f32[256,512]{1,0:T(8,128)S(1)} %add.139), channel_id=1, source_target_pairs={{0,1},{1,2},{2,3},{3,4},{4,5},{5,6},{6,7},{7,0},{8,9},{9,10},{10,1... | collective-permute-start | bytes 1572872 | tf_op jit(solution)/shard_map/ppermute | solution.py:231
  121.3 31.6 %collective-permute-start.6 = (f32[256,512]{1,0:T(8,128)S(1)}, f32[256,512]{1,0:T(8,128)S(1)}, u32[]{:S(2)}, u32[]{:S(2)}) collective-permute-start(f32[256,512]{1,0:T(8,128)S(1)} %add.135), channel_id=1, source_target_pairs={{0,7},{1,0},{2,1},{3,2},{4,3},{5,4},{6,5},{7,6},{8,15},{9,8},{10,9... | collective-permute-start | bytes 1572872 | tf_op jit(solution)/shard_map/ppermute | solution.py:231
  132.0 20.8 %collective-permute-start.13 = (f32[256,512]{1,0:T(8,128)S(1)}, f32[256,512]{1,0:T(8,128)S(1)}, u32[]{:S(2)}, u32[]{:S(2)}) collective-permute-start(f32[256,512]{1,0:T(8,128)S(1)} %add.142), channel_id=1, source_target_pairs={{0,7},{1,0},{2,1},{3,2},{4,3},{5,4},{6,5},{7,6},{8,15},{9,8},{10,9... | collective-permute-start | bytes 1572872 | tf_op jit(solution)/shard_map/ppermute | solution.py:231
  135.5 17.3 %collective-permute-start.3 = (f32[256,512]{1,0:T(8,128)S(1)}, f32[256,512]{1,0:T(8,128)S(1)}, u32[]{:S(2)}, u32[]{:S(2)}) collective-permute-start(f32[256,512]{1,0:T(8,128)S(1)} %add.133), channel_id=1, source_target_pairs={{0,1},{1,2},{2,3},{3,4},{4,5},{5,6},{6,7},{7,0},{8,9},{9,10},{10,1... | collective-permute-start | bytes 1572872 | tf_op jit(solution)/shard_map/ppermute | solution.py:231

commit v10 on v9

--- a/solution.py
+++ b/solution.py
@@ -25,7 +25,7 @@
 
 def exchange_order(n_parts):
     gray = (0, 1, 3, 2)
-    order = [(y * SIDE + gray[x]) * CORES + c for y in range(SIDE) for x in range(SIDE) for c in range(CORES)]
+    order = [(y * SIDE + gray[x]) * CORES + c for c in range(CORES) for y in range(SIDE) for x in range(SIDE)]
     return order if len(order) == n_parts else list(range(n_parts))
 
 

time: 155 us -> 154 us (level)
  transfers between devices with their start and end apart: 15 -> 15, of which waited for: 8 -> 9; matrix products, arithmetic and copies ran while one was open for 4% -> 4% of each run, Pallas kernels for 1% -> 1%
where the time goes in v10:
time: 154 us; the launch traced here: 153 us
  waiting for transfers between devices  68.4 us (44%)
  blocking collectives  36.1 us (23%)
  starting transfers between devices  28.1 us (18%)
  Pallas kernels  11.4 us (7%)
  matrix products  4.75 us (3%)
  local copies, waits for them, and re-layouts  3.13 us (2%)
    ppermute x14, waiting for transfers between devices, ring_sum(): got = lax.ppermute(total, 'chan', hops)  56.2 us
    all_to_all x1, blocking collectives, exchange(): lax.all_to_all(value, 'seq', split_axis=0, concat_axis=0, tiled=True, axi...  36.1 us
    ppermute x14, starting transfers between devices, ring_sum(): got = lax.ppermute(total, 'chan', hops)  22.9 us
    all_to_all x1, waiting for transfers between devices, exchange(): lax.all_to_all(value, 'seq', split_axis=0, concat_axis=0, tiled=True, axi...  12.2 us
    pallas_call x1, Pallas kernels, convolve(): pl.pallas_call(lambda *refs: conv_kernel(n_parts, width, group, *refs), o...  6.91 us
    all_to_all x1, starting transfers between devices, exchange(): lax.all_to_all(value, 'seq', split_axis=0, concat_axis=0, tiled=True, axi...  5.13 us
    dot_general x16, matrix products, dot(): return jnp.dot(left, right, preferred_element_type=F32)  4.75 us
  transfers between devices with their start and end apart: 15, of which 9 were waited for; matrix products, arithmetic and copies ran while one was open for 4% of the time, Pallas kernels for 1%

profile of v10, /device:TPU:1, one launch (start us, length us, event | category | flops | bytes accessed | tf_op | source)
XLA Modules:
  0.0 153.2 jit_solution(16509419407945029824)
XLA Ops:
  0.0 2.1 %pack.1 = f32[32,2,4,16,128]{4,3,2,1,0:T(8,128)S(1)} custom-call(bf16[512,512]{1,0:T(8,128)(2,1)} %key_ref.3, bf16[512,512]{1,0:T(8,128)(2,1)} %value_ref.3, f32[512,512]{1,0:T(8,128)} %taps_ref.1), custom_call_target="tpu_custom_call" | custom-call | tf_op jit(solution)/shard_map/pack/pallas_call | solution.py:113
  2.2 36.1 %all_to_all.10 = f32[32,2,4,16,128]{4,3,2,1,0:T(8,128)S(1)} all-to-all(f32[32,2,4,16,128]{4,3,2,1,0:T(8,128)S(1)} %pack.1), channel_id=1, replica_groups={{0,16,48,32,64,80,112,96,128,144,176,160,192,208,240,224,8,24,56,40,72,..., dimensions={0} | all-to-all | bytes 4194304 | tf_op jit(solution)/shard_map/all_to_all | solution.py:34
  38.3 6.9 %convolve.1 = f32[2048,128]{1,0:T(8,128)} custom-call(f32[4096,128]{1,0:T(8,128)S(1)} %bitcast.32, bf16[256,384]{1,0:T(8,128)(2,1)S(1)} %copy-done.7, f32[128,128]{1,0:T(8,128)S(1)} %copy-done.9, f32[128,128]{1,0:T(8,128)S(1)} %copy-done.8, bf16[768,256]{1,0:T(8,128)(2,1)S(1)} %copy-done.5, bf16[768,256]{1,0:T(8,128)(2,1)S(1)} %copy-done.4, ...), custom_call_target="tpu_custom_call" | custom-call | flops 3623878656 | bytes 3145728 | tf_op jit(solution)/shard_map/convolve/pallas_call | solution.py:175
  45.2 5.1 %all-to-all-start.1 = ((f32[32,4,16,128]{3,2,1,0:T(8,128)}), f32[32,4,16,128]{3,2,1,0:T(8,128)S(1)}, u32[]{:S(2)}, u32[]{:S(2)}) async-start(f32[32,4,16,128]{3,2,1,0:T(8,128)} %bitcast.1), calls=%async_computation.1 | async-start | bytes 2097152 | tf_op jit(solution)/shard_map/all_to_all | solution.py:34
  50.5 1.2 columns.1
  51.7 1.1 copy-done.10
  52.8 1.9 %constant_dynamic-slice_fusion = (bf16[512,512]{1,0:T(8,128)(2,1)}, bf16[512,512]{1,0:T(8,128)(2,1)}, bf16[512,512]{1,0:T(8,128)(2,1)}, bf16[512,512]{1,0:T(8,12...) fusion(bf16[512,4096]{1,0:T(8,128)(2,1)S(1)} %copy-done.10, ...), kind=kLoop, calls=%fused_computation.2 | loop fusion | bytes 7340060 | tf_op jit(solution)/shard_map/dynamic_slice | solution.py:269
  54.7 12.2 %all-to-all-done.1.conv_ref = f32[32,4,16,128]{3,2,1,0:T(8,128)S(1)} async-done(((f32[32,4,16,128]{3,2,1,0:T(8,128)}), f32[32,4,16,128]{3,2,1,0:T(8,128)S(1)}, u32[]{:S(2)}, u32[]{:S(2)}) %all-to-all-start.1) | async-done | bytes 1048608 | tf_op jit(solution)/shard_map/all_to_all | solution.py:34
  66.9 0.3 gate.1
  67.3 0.3 fusion
  67.6 0.3 fusion.6
  67.9 1.7 %collective-permute-start = (f32[256,512]{1,0:T(8,128)S(1)}, f32[256,512]{1,0:T(8,128)S(1)}, u32[]{:S(2)}, u32[]{:S(2)}) collective-permute-start(f32[256,512]{1,0:T(8,128)S(1)} %fusion.6), channel_id=1, source_target_pairs={{0,1},{1,2},{2,3},{3,4},{4,5},{5,6},{6,7},{7,0},{8,9},{9,10},{10,1... | collective-permute-start | bytes 1572872 | tf_op jit(solution)/shard_map/ppermute | solution.py:231
  69.6 0.3 fusion.4
  69.9 4.0 %collective-permute-start.10 = (f32[256,512]{1,0:T(8,128)S(1)}, f32[256,512]{1,0:T(8,128)S(1)}, u32[]{:S(2)}, u32[]{:S(2)}) collective-permute-start(f32[256,512]{1,0:T(8,128)S(1)} %fusion), channel_id=1, source_target_pairs={{0,7},{1,0},{2,1},{3,2},{4,3},{5,4},{6,5},{7,6},{8,15},{9,8},{10,9... | collective-permute-start | bytes 1572872 | tf_op jit(solution)/shard_map/ppermute | solution.py:231
  73.9 0.3 fusion.2
  74.2 0.1 collective-permute-start.7
  74.4 2.9 %collective-permute-start.4 = (f32[256,512]{1,0:T(8,128)S(1)}, f32[256,512]{1,0:T(8,128)S(1)}, u32[]{:S(2)}, u32[]{:S(2)}) collective-permute-start(f32[256,512]{1,0:T(8,128)S(1)} %fusion.4), channel_id=1, source_target_pairs={{0,7},{1,0},{2,1},{3,2},{4,3},{5,4},{6,5},{7,6},{8,15},{9,8},{10,9... | collective-permute-start | bytes 1572872 | tf_op jit(solution)/shard_map/ppermute | solution.py:231
  77.3 7.0 %collective-permute-done = f32[256,512]{1,0:T(8,128)S(1)} collective-permute-done((f32[256,512]{1,0:T(8,128)S(1)}, f32[256,512]{1,0:T(8,128)S(1)}, u32[]{:S(2)}, u32[]{:S(2)}) %collective-permute-start) | collective-permute-done | bytes 524320 | tf_op jit(solution)/shard_map/ppermute | solution.py:231
  84.3 0.3 fusion.9
  84.8 0.3 fusion.16
  85.1 0.1 add.140
  85.2 2.7 %collective-permute-start.11 = (f32[256,512]{1,0:T(8,128)S(1)}, f32[256,512]{1,0:T(8,128)S(1)}, u32[]{:S(2)}, u32[]{:S(2)}) collective-permute-start(f32[256,512]{1,0:T(8,128)S(1)} %add.140), channel_id=1, source_target_pairs={{0,7},{1,0},{2,1},{3,2},{4,3},{5,4},{6,5},{7,6},{8,15},{9,8},{10,9... | collective-permute-start | bytes 1572872 | tf_op jit(solution)/shard_map/ppermute | solution.py:231
  87.9 7.6 %collective-permute-done.7 = f32[256,512]{1,0:T(8,128)S(1)} collective-permute-done((f32[256,512]{1,0:T(8,128)S(1)}, f32[256,512]{1,0:T(8,128)S(1)}, u32[]{:S(2)}, u32[]{:S(2)}) %collective-permute-start.7) | collective-permute-done | bytes 524320 | tf_op jit(solution)/shard_map/ppermute | solution.py:231
  95.6 0.3 fusion.14
  96.0 0.1 collective-permute-start.8
  96.1 0.3 fusion.12
  96.5 2.7 %collective-permute-start.5 = (f32[256,512]{1,0:T(8,128)S(1)}, f32[256,512]{1,0:T(8,128)S(1)}, u32[]{:S(2)}, u32[]{:S(2)}) collective-permute-start(f32[256,512]{1,0:T(8,128)S(1)} %add.134), channel_id=1, source_target_pairs={{0,7},{1,0},{2,1},{3,2},{4,3},{5,4},{6,5},{7,6},{8,15},{9,8},{10,9... | collective-permute-start | bytes 1572872 | tf_op jit(solution)/shard_map/ppermute | solution.py:231
  99.2 7.6 %collective-permute-done.1 = f32[256,512]{1,0:T(8,128)S(1)} collective-permute-done((f32[256,512]{1,0:T(8,128)S(1)}, f32[256,512]{1,0:T(8,128)S(1)}, u32[]{:S(2)}, u32[]{:S(2)}) %collective-permute-start.1) | collective-permute-done | bytes 524320 | tf_op jit(solution)/shard_map/ppermute | solution.py:231
  106.8 0.3 fusion.10
  107.3 0.3 fusion.17
  107.7 2.7 %collective-permute-start.12 = (f32[256,512]{1,0:T(8,128)S(1)}, f32[256,512]{1,0:T(8,128)S(1)}, u32[]{:S(2)}, u32[]{:S(2)}) collective-permute-start(f32[256,512]{1,0:T(8,128)S(1)} %add.141), channel_id=1, source_target_pairs={{0,7},{1,0},{2,1},{3,2},{4,3},{5,4},{6,5},{7,6},{8,15},{9,8},{10,9... | collective-permute-start | bytes 1572872 | tf_op jit(solution)/shard_map/ppermute | solution.py:231
  110.4 7.6 %collective-permute-done.8 = f32[256,512]{1,0:T(8,128)S(1)} collective-permute-done((f32[256,512]{1,0:T(8,128)S(1)}, f32[256,512]{1,0:T(8,128)S(1)}, u32[]{:S(2)}, u32[]{:S(2)}) %collective-permute-start.8) | collective-permute-done | bytes 524320 | tf_op jit(solution)/shard_map/ppermute | solution.py:231
  118.0 0.3 fusion.15
  118.3 0.1 add.139
  118.6 0.3 fusion.13
  118.9 0.1 add.135
  119.0 2.7 %collective-permute-start.6 = (f32[256,512]{1,0:T(8,128)S(1)}, f32[256,512]{1,0:T(8,128)S(1)}, u32[]{:S(2)}, u32[]{:S(2)}) collective-permute-start(f32[256,512]{1,0:T(8,128)S(1)} %add.135), channel_id=1, source_target_pairs={{0,7},{1,0},{2,1},{3,2},{4,3},{5,4},{6,5},{7,6},{8,15},{9,8},{10,9... | collective-permute-start | bytes 1572872 | tf_op jit(solution)/shard_map/ppermute | solution.py:231
  121.7 7.6 %collective-permute-done.2 = f32[256,512]{1,0:T(8,128)S(1)} collective-permute-done((f32[256,512]{1,0:T(8,128)S(1)}, f32[256,512]{1,0:T(8,128)S(1)}, u32[]{:S(2)}, u32[]{:S(2)}) %collective-permute-start.2) | collective-permute-done | bytes 524320 | tf_op jit(solution)/shard_map/ppermute | solution.py:231
  129.3 0.3 fusion.18
  129.7 2.9 %collective-permute-start.13 = (f32[256,512]{1,0:T(8,128)S(1)}, f32[256,512]{1,0:T(8,128)S(1)}, u32[]{:S(2)}, u32[]{:S(2)}) collective-permute-start(f32[256,512]{1,0:T(8,128)S(1)} %add.142), channel_id=1, source_target_pairs={{0,7},{1,0},{2,1},{3,2},{4,3},{5,4},{6,5},{7,6},{8,15},{9,8},{10,9... | collective-permute-start | bytes 1572872 | tf_op jit(solution)/shard_map/ppermute | solution.py:231
  132.5 0.3 fusion.11
  132.9 0.1 collective-permute-start.3
  133.0 7.5 %collective-permute-done.9 = f32[256,512]{1,0:T(8,128)S(1)} collective-permute-done((f32[256,512]{1,0:T(8,128)S(1)}, f32[256,512]{1,0:T(8,128)S(1)}, u32[]{:S(2)}, u32[]{:S(2)}) %collective-permute-start.9) | collective-permute-done | bytes 524320 | tf_op jit(solution)/shard_map/ppermute | solution.py:231
  140.5 10.6 %collective-permute-done.13 = f32[256,512]{1,0:T(8,128)S(1)} collective-permute-done((f32[256,512]{1,0:T(8,128)S(1)}, f32[256,512]{1,0:T(8,128)S(1)}, u32[]{:S(2)}, u32[]{:S(2)}) %collective-permute-start.13) | collective-permute-done | bytes 524320 | tf_op jit(solution)/shard_map/ppermute | solution.py:231
  151.1 0.6 collective-permute-done.3
  151.7 0.3 add_convert_fusion.lower_ref
  152.1 0.3 add_convert_fusion.1.upper_ref
  152.4 0.8 join.1
  (52 shorter events, 1.0 us)
Async XLA Ops:
  0.0 38.3 %copy-start.4 = (bf16[768,256]{1,0:T(8,128)(2,1)S(1)}, bf16[768,256]{1,0:T(8,128)(2,1)}, u32[]{:S(2)}) copy-start(bf16[768,256]{1,0:T(8,128)(2,1)} %constant.79.clone.refs_5_) | copy-start | bytes 1179652
  0.0 38.3 %copy-start.5 = (bf16[768,256]{1,0:T(8,128)(2,1)S(1)}, bf16[768,256]{1,0:T(8,128)(2,1)}, u32[]{:S(2)}) copy-start(bf16[768,256]{1,0:T(8,128)(2,1)} %constant.78.clone.refs_4_) | copy-start | bytes 1179652
  0.0 38.3 %copy-start.6 = (bf16[128,768]{1,0:T(8,128)(2,1)S(1)}, bf16[128,768]{1,0:T(8,128)(2,1)}, u32[]{:S(2)}) copy-start(bf16[128,768]{1,0:T(8,128)(2,1)} %constant.80.clone.refs_6_) | copy-start | bytes 589828
  0.0 38.3 %copy-start.7 = (bf16[256,384]{1,0:T(8,128)(2,1)S(1)}, bf16[256,384]{1,0:T(8,128)(2,1)}, u32[]{:S(2)}) copy-start(bf16[256,384]{1,0:T(8,128)(2,1)} %constant.77.clone.refs_1_) | copy-start | bytes 589828
  0.0 38.3 %copy-start.8 = (f32[128,128]{1,0:T(8,128)S(1)}, f32[128,128]{1,0:T(8,128)}, u32[]{:S(2)}) copy-start(f32[128,128]{1,0:T(8,128)} %constant.76.clone.refs_3_) | copy-start | bytes 196612
  0.0 38.3 %copy-start.9 = (f32[128,128]{1,0:T(8,128)S(1)}, f32[128,128]{1,0:T(8,128)}, u32[]{:S(2)}) copy-start(f32[128,128]{1,0:T(8,128)} %constant.75.clone.refs_2_) | copy-start | bytes 196612
  45.2 21.7 %all-to-all-start.1 = ((f32[32,4,16,128]{3,2,1,0:T(8,128)}), f32[32,4,16,128]{3,2,1,0:T(8,128)S(1)}, u32[]{:S(2)}, u32[]{:S(2)}) async-start(f32[32,4,16,128]{3,2,1,0:T(8,128)} %bitcast.1), calls=%async_computation.1 | async-start | bytes 2097152 | tf_op jit(solution)/shard_map/all_to_all | solution.py:34
  50.5 2.4 %copy-start.10 = (bf16[512,4096]{1,0:T(8,128)(2,1)S(1)}, bf16[512,4096]{1,0:T(8,128)(2,1)}, u32[]{:S(2)}) copy-start(bf16[512,4096]{1,0:T(8,128)(2,1)} %weight_ref.1) | copy-start | bytes 12582916
  52.8 14.1 %copy-start = (bf16[512,512]{1,0:T(8,128)(2,1)S(1)}, bf16[512,512]{1,0:T(8,128)(2,1)}, u32[]{:S(2)}) copy-start(bf16[512,512]{1,0:T(8,128)(2,1)} %key_ref.3) | copy-start | bytes 1572868
  52.8 14.1 %copy-start.1 = (bf16[512,512]{1,0:T(8,128)(2,1)S(1)}, bf16[512,512]{1,0:T(8,128)(2,1)}, u32[]{:S(2)}) copy-start(bf16[512,512]{1,0:T(8,128)(2,1)} %value_ref.3) | copy-start | bytes 1572868
  52.8 14.1 %copy-start.2 = (bf16[512,512]{1,0:T(8,128)(2,1)S(1)}, bf16[512,512]{1,0:T(8,128)(2,1)}, u32[]{:S(2)}) copy-start(bf16[512,512]{1,0:T(8,128)(2,1)} %query_ref.1) | copy-start | bytes 1572868
  52.8 14.1 %copy-start.3 = (f32[512]{0:T(512)S(1)}, f32[512]{0:T(512)}, u32[]{:S(2)}) copy-start(f32[512]{0:T(512)} %param.16) | copy-start | bytes 6148
  66.9 2.7 %copy-start.15 = (bf16[512,512]{1,0:T(8,128)(2,1)S(1)}, bf16[512,512]{1,0:T(8,128)(2,1)}, u32[]{:S(2)}) copy-start(bf16[512,512]{1,0:T(8,128)(2,1)} %get-tuple-element.51) | copy-start | bytes 1572868
  66.9 7.1 %copy-start.16 = (bf16[512,512]{1,0:T(8,128)(2,1)S(1)}, bf16[512,512]{1,0:T(8,128)(2,1)}, u32[]{:S(2)}) copy-start(bf16[512,512]{1,0:T(8,128)(2,1)} %get-tuple-element.44) | copy-start | bytes 1572868
  67.9 16.5 %collective-permute-start = (f32[256,512]{1,0:T(8,128)S(1)}, f32[256,512]{1,0:T(8,128)S(1)}, u32[]{:S(2)}, u32[]{:S(2)}) collective-permute-start(f32[256,512]{1,0:T(8,128)S(1)} %fusion.6), channel_id=1, source_target_pairs={{0,1},{1,2},{2,3},{3,4},{4,5},{5,6},{6,7},{7,0},{8,9},{9,10},{10,1... | collective-permute-start | bytes 1572872 | tf_op jit(solution)/shard_map/ppermute | solution.py:231
  69.9 25.7 %copy-start.14 = (bf16[512,512]{1,0:T(8,128)(2,1)S(1)}, bf16[512,512]{1,0:T(8,128)(2,1)}, u32[]{:S(2)}) copy-start(bf16[512,512]{1,0:T(8,128)(2,1)} %get-tuple-element.47) | copy-start | bytes 1572868
  69.9 14.9 %collective-permute-start.10 = (f32[256,512]{1,0:T(8,128)S(1)}, f32[256,512]{1,0:T(8,128)S(1)}, u32[]{:S(2)}, u32[]{:S(2)}) collective-permute-start(f32[256,512]{1,0:T(8,128)S(1)} %fusion), channel_id=1, source_target_pairs={{0,7},{1,0},{2,1},{3,2},{4,3},{5,4},{6,5},{7,6},{8,15},{9,8},{10,9... | collective-permute-start | bytes 1572872 | tf_op jit(solution)/shard_map/ppermute | solution.py:231
  74.2 21.3 %collective-permute-start.7 = (f32[256,512]{1,0:T(8,128)S(1)}, f32[256,512]{1,0:T(8,128)S(1)}, u32[]{:S(2)}, u32[]{:S(2)}) collective-permute-start(f32[256,512]{1,0:T(8,128)S(1)} %fusion.2), channel_id=1, source_target_pairs={{0,1},{1,2},{2,3},{3,4},{4,5},{5,6},{6,7},{7,0},{8,9},{9,10},{10,1... | collective-permute-start | bytes 1572872 | tf_op jit(solution)/shard_map/ppermute | solution.py:231
  74.4 21.7 %collective-permute-start.4 = (f32[256,512]{1,0:T(8,128)S(1)}, f32[256,512]{1,0:T(8,128)S(1)}, u32[]{:S(2)}, u32[]{:S(2)}) collective-permute-start(f32[256,512]{1,0:T(8,128)S(1)} %fusion.4), channel_id=1, source_target_pairs={{0,7},{1,0},{2,1},{3,2},{4,3},{5,4},{6,5},{7,6},{8,15},{9,8},{10,9... | collective-permute-start | bytes 1572872 | tf_op jit(solution)/shard_map/ppermute | solution.py:231
  84.3 11.7 %copy-start.13 = (bf16[512,512]{1,0:T(8,128)(2,1)S(1)}, bf16[512,512]{1,0:T(8,128)(2,1)}, u32[]{:S(2)}) copy-start(bf16[512,512]{1,0:T(8,128)(2,1)} %get-tuple-element.54) | copy-start | bytes 1572868
  84.7 22.1 %collective-permute-start.1 = (f32[256,512]{1,0:T(8,128)S(1)}, f32[256,512]{1,0:T(8,128)S(1)}, u32[]{:S(2)}, u32[]{:S(2)}) collective-permute-start(f32[256,512]{1,0:T(8,128)S(1)} %add.131), channel_id=1, source_target_pairs={{0,1},{1,2},{2,3},{3,4},{4,5},{5,6},{6,7},{7,0},{8,9},{9,10},{10,1... | collective-permute-start | bytes 1572872 | tf_op jit(solution)/shard_map/ppermute | solution.py:231
  85.2 22.1 %collective-permute-start.11 = (f32[256,512]{1,0:T(8,128)S(1)}, f32[256,512]{1,0:T(8,128)S(1)}, u32[]{:S(2)}, u32[]{:S(2)}) collective-permute-start(f32[256,512]{1,0:T(8,128)S(1)} %add.140), channel_id=1, source_target_pairs={{0,7},{1,0},{2,1},{3,2},{4,3},{5,4},{6,5},{7,6},{8,15},{9,8},{10,9... | collective-permute-start | bytes 1572872 | tf_op jit(solution)/shard_map/ppermute | solution.py:231
  96.0 22.1 %copy-start.11 = (bf16[512,512]{1,0:T(8,128)(2,1)S(1)}, bf16[512,512]{1,0:T(8,128)(2,1)}, u32[]{:S(2)}) copy-start(bf16[512,512]{1,0:T(8,128)(2,1)} %get-tuple-element.50) | copy-start | bytes 1572868
  96.0 22.1 %collective-permute-start.8 = (f32[256,512]{1,0:T(8,128)S(1)}, f32[256,512]{1,0:T(8,128)S(1)}, u32[]{:S(2)}, u32[]{:S(2)}) collective-permute-start(f32[256,512]{1,0:T(8,128)S(1)} %add.138), channel_id=1, source_target_pairs={{0,1},{1,2},{2,3},{3,4},{4,5},{5,6},{6,7},{7,0},{8,9},{9,10},{10,1... | collective-permute-start | bytes 1572872 | tf_op jit(solution)/shard_map/ppermute | solution.py:231
  96.5 22.1 %copy-start.12 = (bf16[512,512]{1,0:T(8,128)(2,1)S(1)}, bf16[512,512]{1,0:T(8,128)(2,1)}, u32[]{:S(2)}) copy-start(bf16[512,512]{1,0:T(8,128)(2,1)} %get-tuple-element.57) | copy-start | bytes 1572868
  96.5 22.1 %collective-permute-start.5 = (f32[256,512]{1,0:T(8,128)S(1)}, f32[256,512]{1,0:T(8,128)S(1)}, u32[]{:S(2)}, u32[]{:S(2)}) collective-permute-start(f32[256,512]{1,0:T(8,128)S(1)} %add.134), channel_id=1, source_target_pairs={{0,7},{1,0},{2,1},{3,2},{4,3},{5,4},{6,5},{7,6},{8,15},{9,8},{10,9... | collective-permute-start | bytes 1572872 | tf_op jit(solution)/shard_map/ppermute | solution.py:231
  107.2 22.1 %collective-permute-start.2 = (f32[256,512]{1,0:T(8,128)S(1)}, f32[256,512]{1,0:T(8,128)S(1)}, u32[]{:S(2)}, u32[]{:S(2)}) collective-permute-start(f32[256,512]{1,0:T(8,128)S(1)} %add.132), channel_id=1, source_target_pairs={{0,1},{1,2},{2,3},{3,4},{4,5},{5,6},{6,7},{7,0},{8,9},{9,10},{10,1... | collective-permute-start | bytes 1572872 | tf_op jit(solution)/shard_map/ppermute | solution.py:231
  107.7 21.6 %collective-permute-start.12 = (f32[256,512]{1,0:T(8,128)S(1)}, f32[256,512]{1,0:T(8,128)S(1)}, u32[]{:S(2)}, u32[]{:S(2)}) collective-permute-start(f32[256,512]{1,0:T(8,128)S(1)} %add.141), channel_id=1, source_target_pairs={{0,7},{1,0},{2,1},{3,2},{4,3},{5,4},{6,5},{7,6},{8,15},{9,8},{10,9... | collective-permute-start | bytes 1572872 | tf_op jit(solution)/shard_map/ppermute | solution.py:231
  118.4 33.3 %copy-start.17 = (bf16[512,512]{1,0:T(8,128)(2,1)S(1)}, bf16[512,512]{1,0:T(8,128)(2,1)}, u32[]{:S(2)}) copy-start(bf16[512,512]{1,0:T(8,128)(2,1)} %get-tuple-element.61) | copy-start | bytes 1572868
  118.4 22.1 %collective-permute-start.9 = (f32[256,512]{1,0:T(8,128)S(1)}, f32[256,512]{1,0:T(8,128)S(1)}, u32[]{:S(2)}, u32[]{:S(2)}) collective-permute-start(f32[256,512]{1,0:T(8,128)S(1)} %add.139), channel_id=1, source_target_pairs={{0,1},{1,2},{2,3},{3,4},{4,5},{5,6},{6,7},{7,0},{8,9},{9,10},{10,1... | collective-permute-start | bytes 1572872 | tf_op jit(solution)/shard_map/ppermute | solution.py:231
  119.0 32.2 %collective-permute-start.6 = (f32[256,512]{1,0:T(8,128)S(1)}, f32[256,512]{1,0:T(8,128)S(1)}, u32[]{:S(2)}, u32[]{:S(2)}) collective-permute-start(f32[256,512]{1,0:T(8,128)S(1)} %add.135), channel_id=1, source_target_pairs={{0,7},{1,0},{2,1},{3,2},{4,3},{5,4},{6,5},{7,6},{8,15},{9,8},{10,9... | collective-permute-start | bytes 1572872 | tf_op jit(solution)/shard_map/ppermute | solution.py:231
  129.7 21.5 %collective-permute-start.13 = (f32[256,512]{1,0:T(8,128)S(1)}, f32[256,512]{1,0:T(8,128)S(1)}, u32[]{:S(2)}, u32[]{:S(2)}) collective-permute-start(f32[256,512]{1,0:T(8,128)S(1)} %add.142), channel_id=1, source_target_pairs={{0,7},{1,0},{2,1},{3,2},{4,3},{5,4},{6,5},{7,6},{8,15},{9,8},{10,9... | collective-permute-start | bytes 1572872 | tf_op jit(solution)/shard_map/ppermute | solution.py:231
  132.9 18.8 %collective-permute-start.3 = (f32[256,512]{1,0:T(8,128)S(1)}, f32[256,512]{1,0:T(8,128)S(1)}, u32[]{:S(2)}, u32[]{:S(2)}) collective-permute-start(f32[256,512]{1,0:T(8,128)S(1)} %add.133), channel_id=1, source_target_pairs={{0,1},{1,2},{2,3},{3,4},{4,5},{5,6},{6,7},{7,0},{8,9},{9,10},{10,1... | collective-permute-start | bytes 1572872 | tf_op jit(solution)/shard_map/ppermute | solution.py:231
